TPU v7x, 512 devices: a whole 4x4x16 slice. The times are simulated.
512 devices in a mesh: seq: 32 (over x, z_lo, core), chan: 16 (over z_hi, y).
Axes of the slice: x: 4, y: 4, z: 16 (z_hi: 4, z_lo: 4; z = z_hi * 4 + z_lo), core: 2. Of those that a mesh axis runs over, the one named last changes fastest.
Arguments:
- grad_out: bfloat16 [4096, 4096], P('seq', 'chan'), may hold values from -6 to 6
- query_gate: bfloat16 [4096, 4096], P('seq', 'chan'), may hold values from -6 to 6
- key_gate: bfloat16 [4096, 4096], P('seq', 'chan'), may hold values from -6 to 6
- value_input: bfloat16 [4096, 4096], P('seq', 'chan'), may hold values from -6 to 6
- filter_taps: float32 [4096, 128], P('chan'), may hold values from -2 to 2
- skip_gain: float32 [4096], P('chan'), may hold values from -1 to 1
- out_weight: bfloat16 [4096, 4096], P('chan'), may hold values from -0.09375 to 0.09375
Outputs:
- grad_query: bfloat16 [4096, 4096], P('seq', 'chan')
- grad_key: bfloat16 [4096, 4096], P('seq', 'chan')
- grad_value: bfloat16 [4096, 4096], P('seq', 'chan')
- grad_filter: float32 [4096, 128], P('chan')
- grad_skip: float32 [4096], P('chan')
- grad_weight: float32 [4096, 4096], P('chan', 'seq')
All inputs are finite; a program needn't handle non-finite values.
Results may differ from a plain program's by a relative error of at most 0.0029.
Values may be sent and summed in bfloat16 or wider, within the bound.
No kernel may reach another device: no remote copies, remote signals or barrier semaphores. Data moves between devices by JAX's collectives and lax.ppermute only.
A program may use at most 128 MiB of HBM per device.

v0:
```python
import math

import jax
import jax.numpy as jnp
from jax import lax
from jax.sharding import PartitionSpec as P

TAPS = 128


def passed_along(value, axis, by):
    size = lax.axis_size(axis)
    pairs = [(i, i + by) for i in range(size) if 0 <= i + by < size]
    return lax.ppermute(value, axis, pairs)


def causal_sum(padded, tap_values, length):
    running = jnp.zeros((length, padded.shape[1]), jnp.float32)
    for tap_index in range(TAPS):
        offset = TAPS - 1 - tap_index
        running = running + tap_values[:, tap_index] * padded[offset : offset + length]
    return running


def ahead_sum(padded, tap_values, length):
    running = jnp.zeros((length, padded.shape[1]), jnp.float32)
    for tap_index in range(TAPS):
        running = running + tap_values[:, tap_index] * padded[tap_index : tap_index + length]
    return running


def tap_products(grad_sum, padded, length):
    columns = []
    for tap_index in range(TAPS):
        offset = TAPS - 1 - tap_index
        columns.append(jnp.sum(grad_sum * padded[offset : offset + length], axis=0))
    return jnp.stack(columns, axis=1)


def body(grad_out, query_gate, key_gate, value_input, filter_taps, skip_gain, out_weight):
    local_rows = query_gate.shape[0]
    norm_factor = 1.0 / math.sqrt(local_rows * lax.axis_size("seq"))
    query_part = query_gate.astype(jnp.float32)
    key_part = key_gate.astype(jnp.float32)
    value_part = value_input.astype(jnp.float32)
    mixed_in = key_part * value_part
    previous = passed_along(mixed_in[local_rows - (TAPS - 1) :], "seq", 1)
    padded = jnp.concatenate([previous, mixed_in], axis=0)
    summed = causal_sum(padded, filter_taps, local_rows) + skip_gain * mixed_in
    mixer_out = (query_part * summed).astype(jnp.bfloat16)
    gathered = lax.all_gather(grad_out, "chan", axis=1, tiled=True)
    grad_mixed = lax.dot_general(
        gathered, out_weight, (((1,), (1,)), ((), ())), preferred_element_type=jnp.float32
    )
    weight_term = lax.dot_general(
        mixer_out, gathered, (((0,), (0,)), ((), ())), preferred_element_type=jnp.float32
    )
    grad_weight = lax.psum_scatter(
        weight_term * norm_factor, "seq", scatter_dimension=1, tiled=True
    )
    grad_query = (grad_mixed * summed).astype(jnp.bfloat16)
    grad_sum = grad_mixed * query_part
    incoming = passed_along(grad_sum[: TAPS - 1], "seq", -1)
    padded_grad = jnp.concatenate([grad_sum, incoming], axis=0)
    grad_mix = ahead_sum(padded_grad, filter_taps, local_rows) + skip_gain * grad_sum
    grad_key = (grad_mix * value_part).astype(jnp.bfloat16)
    grad_value = (grad_mix * key_part).astype(jnp.bfloat16)
    filter_term = tap_products(grad_sum, padded, local_rows) * norm_factor
    skip_term = jnp.sum(grad_sum * mixed_in, axis=0) * norm_factor
    grad_filter, grad_skip = lax.psum((filter_term, skip_term), "seq")
    return (grad_query, grad_key, grad_value, grad_filter, grad_skip, grad_weight)


def solution(mesh):
    return jax.shard_map(
        body,
        mesh=mesh,
        in_specs=(
            P("seq", "chan"),
            P("seq", "chan"),
            P("seq", "chan"),
            P("seq", "chan"),
            P("chan", None),
            P("chan"),
            P("chan", None),
        ),
        out_specs=(
            P("seq", "chan"),
            P("seq", "chan"),
            P("seq", "chan"),
            P("chan", None),
            P("chan"),
            P("chan", "seq"),
        ),
        check_vma=False,
    )
```

profile of v0, /device:TPU:1, one launch (start us, length us, event | category | flops | bytes accessed | tf_op | source)
XLA Modules:
  0.0 559.9 jit_solution(5761657235168609593)
XLA Ops:
  7.2 0.0 copy-start
  7.2 0.0 copy-start.1
  7.2 0.0 all-gather.2.cloned.1.call-start
  7.2 0.7 all-gather.2.cloned.1.call-update
  7.9 0.0 all-reduce.2.cloned.1.call-start
  8.0 0.9 convert_multiply_fusion.3
  8.9 4.9 collective-permute-start
  13.8 4.8 slice_reduce_fusion.123
  18.6 0.0 copy-done.1
  18.6 2.0 slice_reduce_fusion.124
  20.6 2.0 slice_reduce_fusion.125
  22.6 2.0 slice_reduce_fusion.120
  24.6 2.0 slice_reduce_fusion.121
  26.5 2.0 slice_reduce_fusion.122
  28.5 1.6 slice_reduce_fusion.119
  30.2 0.0 collective-permute-done
  30.2 1.0 fusion.434
  31.2 1.0 fusion.416
  32.2 1.1 fusion.461
  33.3 1.1 fusion.488
  34.3 1.1 fusion.398
  35.4 1.1 fusion.443
  36.5 1.1 fusion.386
  37.6 1.0 fusion.497
  38.6 1.1 fusion.470
  39.7 1.0 fusion.425
  40.7 1.1 fusion.407
  41.8 1.0 fusion.452
  42.8 1.1 fusion.479
  43.9 56.6 %all-gather.2.cloned.1.call-done = bf16[128,4096]{1,0:T(8,128)(2,1)} async-done(((bf16[128,256]{1,0:T(8,128)(2,1)}), bf16[128,4096]{1,0:T(8,128)(2,1)}) %all-gather.2.cloned.1.call-update) | async-done | bytes 1048592 | tf_op jit(solution)/shard_map/all_gather | solution.py:51
  100.5 0.0 copy-done.5
  100.8 3.4 multiply_reduce_fusion
  104.3 2.9 collective-permute-start.1
  107.1 0.8 multiply_reduce_fusion.54
  107.9 0.8 multiply_reduce_fusion.117
  108.7 0.8 multiply_reduce_fusion.72
  109.5 0.8 multiply_reduce_fusion.36
  110.2 0.8 multiply_reduce_fusion.108
  111.0 0.8 multiply_reduce_fusion.81
  111.8 0.8 multiply_reduce_fusion.99
  112.5 0.8 multiply_reduce_fusion.90
  113.3 0.8 multiply_reduce_fusion.18
  114.1 0.8 multiply_reduce_fusion.27
  114.9 0.8 multiply_reduce_fusion.63
  115.6 0.8 multiply_reduce_fusion.1
  116.4 0.8 multiply_reduce_fusion.45
  117.2 0.0 collective-permute-done.1
  117.2 0.0 copy-done.7
  117.5 6.1 %fusion = (bf16[128,256]{1,0:T(8,128)(2,1)}, f32[128,256]{1,0:T(8,128)S(1)}) fusion(bf16[128,256]{1,0:T(8,128)(2,1)S(1)} %copy-done.3, f32[128,256]{1,0:T(8,128)S(1)} %get-tuple-element.268, f32[256]{0:T(256)} %param.12, f32[127,256]{1,0:T(8,128)S(1)} %collective-permute-done.1, f32[256]{0:T(256)} %get-tuple-element.266, f32[256]{0:T(256)} %get-tuple-element.267, ...), kind=kLoop, calls=%fused_computation.510 | loop fusion | flops 12681216 | bytes 655360 | tf_op jit(solution)/shard_map/convert_element_type | solution.py:67
  123.6 2.2 multiply_reduce_fusion.126
  125.8 11.6 %stack.515 = f32[256,128]{0,1:T(8,128)S(1)} concatenate(f32[256,1]{0,1:T(1,128)} %bitcast.133, f32[256,1]{0,1:T(1,128)} %bitcast.251, f32[256,1]{0,1:T(1,128)} %bitcast.151, f32[256,1]{0,1:T(1,128)} %bitcast.150, f32[256,1]{0,1:T(1,128)} %bitcast.149, f32[256,1]{0,1:T(1,128)} %bitcast.148, f32[256,1]{0,1:T(1,128)} %bitcast.147, f32[256,1]{0,1:T(1,128)} %bitcast.146, ...), dimensions={1} | concatenate | bytes 262144 | tf_op jit(solution)/shard_map/stack | solution.py:37
  137.4 0.6 broadcast_multiply_fusion
  138.1 0.0 all-reduce.2.cloned.1.call-update
  138.1 0.0 reduce-scatter.2.cloned.1.call-start
  138.2 9.2 %multiply_convert_fusion = (bf16[128,256]{1,0:T(8,128)(2,1)}, f32[128,256]{1,0:T(8,128)S(1)}) fusion(f32[128,256]{1,0:T(8,128)} %get-tuple-element.399, f32[128,256]{1,0:T(8,128)S(1)} %convert_multiply_fusion.3, f32[256]{0:T(256)} %param.12, f32[128,256]{1,0:T(8,128)S(1)} %get-tuple-element.396, f32[256]{0:T(256)} %get-tuple-element.266, ...), kind=kLoop, calls=%fused_computation.1150 | loop fusion | flops 8388608 | bytes 17234944 | tf_op jit(solution)/shard_map/convert_element_type | solution.py:61
  147.3 0.0 copy-done.2
  147.3 0.0 copy-start.44
  147.3 2.7 convolution_multiply_fusion
  150.0 0.0 reduce-scatter.2.cloned.1.call-update
  150.0 0.0 copy-done.44
  150.0 68.3 %psum.15 = f32[256]{0:T(256)} all-reduce(f32[256]{0:T(256)S(1)} %broadcast_multiply_fusion.1), channel_id=1, replica_groups=mesh['seq'=32,'chan'=16] {'seq'}, use_global_device_ids=true, to_apply=%region_129.0 | all-reduce | flops 256 | bytes 2048 | tf_op jit(solution)/shard_map/psum | solution.py:70
  218.3 178.1 %all-reduce.2.cloned.1.call-done = f32[256,128]{0,1:T(8,128)} async-done(((f32[256,128]{0,1:T(8,128)}), f32[256,128]{0,1:T(8,128)}) %all-reduce.2.cloned.1.call-update) | async-done | bytes 131088 | tf_op jit(solution)/shard_map/psum | solution.py:70
  396.4 1.7 copy.13
  398.1 155.3 %reduce-scatter.2.cloned.1.call-done = f32[256,128]{1,0:T(8,128)} async-done(((f32[256,4096]{1,0:T(8,128)}), f32[256,128]{1,0:T(8,128)}) %reduce-scatter.2.cloned.1.call-update) | async-done | bytes 131088 | tf_op jit(solution)/shard_map/reduce_scatter | solution.py:58
  (85 shorter events, 0.2 us)
Async XLA Ops:
  7.2 93.3 %copy-start = (bf16[256,4096]{1,0:T(8,128)(2,1)S(1)}, bf16[256,4096]{1,0:T(8,128)(2,1)}, u32[]{:S(2)}) copy-start(bf16[256,4096]{1,0:T(8,128)(2,1)} %param.13) | copy-start | bytes 6291460
  7.2 11.4 %copy-start.1 = (f32[256,128]{1,0:T(8,128)S(1)}, f32[256,128]{1,0:T(8,128)}, u32[]{:S(2)}) copy-start(f32[256,128]{1,0:T(8,128)} %param.11) | copy-start | bytes 393220
  7.2 93.3 %all-gather.2.cloned.1.call-start = ((), (), s32[]{:S(2)}) async-start(), calls=%async_computation.1 | async-start | bytes 1114112 | tf_op jit(solution)/shard_map/all_gather | solution.py:51
  7.9 388.5 %all-reduce.2.cloned.1.call-start = ((), (), s32[]{:S(2)}) async-start(), calls=%async_computation.2 | async-start | bytes 262144 | tf_op jit(solution)/shard_map/psum | solution.py:70
  8.9 21.3 %collective-permute-start = (f32[127,256]{1,0:T(8,128)S(1)}, f32[127,256]{1,0:T(8,128)S(1)}, u32[]{:S(2)}, u32[]{:S(2)}) collective-permute-start(f32[127,256]{1,0:T(8,128)S(1)} %slice.1791), channel_id=1, source_target_pairs={{0,16},{16,32},{32,48},{48,64},{64,80},{80,96},{96,112},{112,128},... | collective-permute-start | bytes 390152 | tf_op jit(solution)/shard_map/ppermute | solution.py:14
  37.6 62.9 %copy-start.5 = (bf16[128,256]{1,0:T(8,128)(2,1)S(1)}, bf16[128,256]{1,0:T(8,128)(2,1)}, u32[]{:S(2)}) copy-start(bf16[128,256]{1,0:T(8,128)(2,1)} %param.8) | copy-start | bytes 196612
  43.9 73.3 %copy-start.3 = (bf16[128,256]{1,0:T(8,128)(2,1)S(1)}, bf16[128,256]{1,0:T(8,128)(2,1)}, u32[]{:S(2)}) copy-start(bf16[128,256]{1,0:T(8,128)(2,1)} %param.9) | copy-start | bytes 196612
  100.5 16.7 %copy-start.6 = (f32[256]{0:T(256)S(1)}, f32[256]{0:T(256)}, u32[]{:S(2)}) copy-start(f32[256]{0:T(256)} %get-tuple-element.182) | copy-start | bytes 3076
  100.5 16.7 %copy-start.7 = (f32[256]{0:T(256)S(1)}, f32[256]{0:T(256)}, u32[]{:S(2)}) copy-start(f32[256]{0:T(256)} %get-tuple-element.183) | copy-start | bytes 3076
  100.5 16.7 %copy-start.8 = (f32[256]{0:T(256)S(1)}, f32[256]{0:T(256)}, u32[]{:S(2)}) copy-start(f32[256]{0:T(256)} %get-tuple-element.184) | copy-start | bytes 3076
  100.5 16.7 %copy-start.9 = (f32[256]{0:T(256)S(1)}, f32[256]{0:T(256)}, u32[]{:S(2)}) copy-start(f32[256]{0:T(256)} %get-tuple-element.185) | copy-start | bytes 3076
  100.5 16.7 %copy-start.10 = (f32[256]{0:T(256)S(1)}, f32[256]{0:T(256)}, u32[]{:S(2)}) copy-start(f32[256]{0:T(256)} %get-tuple-element.186) | copy-start | bytes 3076
  100.5 16.7 %copy-start.11 = (f32[256]{0:T(256)S(1)}, f32[256]{0:T(256)}, u32[]{:S(2)}) copy-start(f32[256]{0:T(256)} %get-tuple-element.187) | copy-start | bytes 3076
  100.5 16.7 %copy-start.12 = (f32[256]{0:T(256)S(1)}, f32[256]{0:T(256)}, u32[]{:S(2)}) copy-start(f32[256]{0:T(256)} %get-tuple-element.188) | copy-start | bytes 3076
  100.5 16.7 %copy-start.13 = (f32[256]{0:T(256)S(1)}, f32[256]{0:T(256)}, u32[]{:S(2)}) copy-start(f32[256]{0:T(256)} %get-tuple-element.189) | copy-start | bytes 3076
  100.5 16.7 %copy-start.14 = (f32[256]{0:T(256)S(1)}, f32[256]{0:T(256)}, u32[]{:S(2)}) copy-start(f32[256]{0:T(256)} %get-tuple-element.190) | copy-start | bytes 3076
  100.6 16.7 %copy-start.15 = (f32[256]{0:T(256)S(1)}, f32[256]{0:T(256)}, u32[]{:S(2)}) copy-start(f32[256]{0:T(256)} %get-tuple-element.191) | copy-start | bytes 3076
  100.6 16.7 %copy-start.16 = (f32[256]{0:T(256)S(1)}, f32[256]{0:T(256)}, u32[]{:S(2)}) copy-start(f32[256]{0:T(256)} %get-tuple-element.192) | copy-start | bytes 3076
  100.6 16.7 %copy-start.17 = (f32[256]{0:T(256)S(1)}, f32[256]{0:T(256)}, u32[]{:S(2)}) copy-start(f32[256]{0:T(256)} %get-tuple-element.193) | copy-start | bytes 3076
  100.6 16.7 %copy-start.18 = (f32[256]{0:T(256)S(1)}, f32[256]{0:T(256)}, u32[]{:S(2)}) copy-start(f32[256]{0:T(256)} %get-tuple-element.194) | copy-start | bytes 3076
  100.6 16.7 %copy-start.19 = (f32[256]{0:T(256)S(1)}, f32[256]{0:T(256)}, u32[]{:S(2)}) copy-start(f32[256]{0:T(256)} %get-tuple-element.195) | copy-start | bytes 3076
  100.6 16.7 %copy-start.20 = (f32[256]{0:T(256)S(1)}, f32[256]{0:T(256)}, u32[]{:S(2)}) copy-start(f32[256]{0:T(256)} %get-tuple-element.196) | copy-start | bytes 3076
  100.6 16.7 %copy-start.21 = (f32[256]{0:T(256)S(1)}, f32[256]{0:T(256)}, u32[]{:S(2)}) copy-start(f32[256]{0:T(256)} %get-tuple-element.159) | copy-start | bytes 3076
  100.6 16.7 %copy-start.22 = (f32[256]{0:T(256)S(1)}, f32[256]{0:T(256)}, u32[]{:S(2)}) copy-start(f32[256]{0:T(256)} %get-tuple-element.160) | copy-start | bytes 3076
  100.6 16.7 %copy-start.23 = (f32[256]{0:T(256)S(1)}, f32[256]{0:T(256)}, u32[]{:S(2)}) copy-start(f32[256]{0:T(256)} %get-tuple-element.161) | copy-start | bytes 3076
  100.6 16.7 %copy-start.24 = (f32[256]{0:T(256)S(1)}, f32[256]{0:T(256)}, u32[]{:S(2)}) copy-start(f32[256]{0:T(256)} %get-tuple-element.162) | copy-start | bytes 3076
  100.7 16.7 %copy-start.25 = (f32[256]{0:T(256)S(1)}, f32[256]{0:T(256)}, u32[]{:S(2)}) copy-start(f32[256]{0:T(256)} %get-tuple-element.163) | copy-start | bytes 3076
  100.7 16.7 %copy-start.26 = (f32[256]{0:T(256)S(1)}, f32[256]{0:T(256)}, u32[]{:S(2)}) copy-start(f32[256]{0:T(256)} %get-tuple-element.164) | copy-start | bytes 3076
  100.7 16.7 %copy-start.27 = (f32[256]{0:T(256)S(1)}, f32[256]{0:T(256)}, u32[]{:S(2)}) copy-start(f32[256]{0:T(256)} %get-tuple-element.165) | copy-start | bytes 3076
  100.7 16.7 %copy-start.28 = (f32[256]{0:T(256)S(1)}, f32[256]{0:T(256)}, u32[]{:S(2)}) copy-start(f32[256]{0:T(256)} %get-tuple-element.166) | copy-start | bytes 3076
  100.7 16.7 %copy-start.29 = (f32[256]{0:T(256)S(1)}, f32[256]{0:T(256)}, u32[]{:S(2)}) copy-start(f32[256]{0:T(256)} %get-tuple-element.167) | copy-start | bytes 3076
  100.7 16.7 %copy-start.30 = (f32[256]{0:T(256)S(1)}, f32[256]{0:T(256)}, u32[]{:S(2)}) copy-start(f32[256]{0:T(256)} %get-tuple-element.168) | copy-start | bytes 3076
  100.7 16.7 %copy-start.31 = (f32[256]{0:T(256)S(1)}, f32[256]{0:T(256)}, u32[]{:S(2)}) copy-start(f32[256]{0:T(256)} %get-tuple-element.169) | copy-start | bytes 3076
  100.7 16.7 %copy-start.32 = (f32[256]{0:T(256)S(1)}, f32[256]{0:T(256)}, u32[]{:S(2)}) copy-start(f32[256]{0:T(256)} %get-tuple-element.170) | copy-start | bytes 3076
  100.7 16.7 %copy-start.33 = (f32[256]{0:T(256)S(1)}, f32[256]{0:T(256)}, u32[]{:S(2)}) copy-start(f32[256]{0:T(256)} %get-tuple-element.171) | copy-start | bytes 3076
  100.7 16.7 %copy-start.34 = (f32[256]{0:T(256)S(1)}, f32[256]{0:T(256)}, u32[]{:S(2)}) copy-start(f32[256]{0:T(256)} %get-tuple-element.172) | copy-start | bytes 3076
  100.8 16.7 %copy-start.35 = (f32[256]{0:T(256)S(1)}, f32[256]{0:T(256)}, u32[]{:S(2)}) copy-start(f32[256]{0:T(256)} %get-tuple-element.173) | copy-start | bytes 3076
  100.8 16.7 %copy-start.36 = (f32[256]{0:T(256)S(1)}, f32[256]{0:T(256)}, u32[]{:S(2)}) copy-start(f32[256]{0:T(256)} %get-tuple-element.174) | copy-start | bytes 3076
  100.8 16.7 %copy-start.37 = (f32[256]{0:T(256)S(1)}, f32[256]{0:T(256)}, u32[]{:S(2)}) copy-start(f32[256]{0:T(256)} %get-tuple-element.175) | copy-start | bytes 3076
  100.8 16.7 %copy-start.38 = (f32[256]{0:T(256)S(1)}, f32[256]{0:T(256)}, u32[]{:S(2)}) copy-start(f32[256]{0:T(256)} %get-tuple-element.176) | copy-start | bytes 3076
  100.8 16.7 %copy-start.39 = (f32[256]{0:T(256)S(1)}, f32[256]{0:T(256)}, u32[]{:S(2)}) copy-start(f32[256]{0:T(256)} %get-tuple-element.177) | copy-start | bytes 3076
  100.8 16.7 %copy-start.40 = (f32[256]{0:T(256)S(1)}, f32[256]{0:T(256)}, u32[]{:S(2)}) copy-start(f32[256]{0:T(256)} %get-tuple-element.140) | copy-start | bytes 3076
  100.8 16.7 %copy-start.41 = (f32[256]{0:T(256)S(1)}, f32[256]{0:T(256)}, u32[]{:S(2)}) copy-start(f32[256]{0:T(256)} %get-tuple-element.141) | copy-start | bytes 3076
  104.3 19.4 %copy-start.4 = (bf16[128,256]{1,0:T(8,128)(2,1)S(1)}, bf16[128,256]{1,0:T(8,128)(2,1)}, u32[]{:S(2)}) copy-start(bf16[128,256]{1,0:T(8,128)(2,1)} %param.10) | copy-start | bytes 196612
  104.3 13.3 %copy-start.42 = (f32[256]{0:T(256)S(1)}, f32[256]{0:T(256)}, u32[]{:S(2)}) copy-start(f32[256]{0:T(256)} %get-tuple-element.142) | copy-start | bytes 3076
  104.3 13.3 %copy-start.43 = (f32[256]{0:T(256)S(1)}, f32[256]{0:T(256)}, u32[]{:S(2)}) copy-start(f32[256]{0:T(256)} %get-tuple-element.143) | copy-start | bytes 3076
  104.3 12.9 %collective-permute-start.1 = (f32[127,256]{1,0:T(8,128)S(1)}, f32[127,256]{1,0:T(8,128)S(1)}, u32[]{:S(2)}, u32[]{:S(2)}) collective-permute-start(f32[127,256]{1,0:T(8,128)S(1)} %bitcast.132), channel_id=1, source_target_pairs={{16,0},{32,16},{48,32},{64,48},{80,64},{96,80},{112,96},{128,112},... | collective-permute-start | bytes 390152 | tf_op jit(solution)/shard_map/ppermute | solution.py:14
  138.1 415.3 %reduce-scatter.2.cloned.1.call-start = ((), (), s32[]{:S(2)}) async-start(), calls=%async_computation.3 | async-start | bytes 4325376 | tf_op jit(solution)/shard_map/reduce_scatter | solution.py:58
  138.1 9.2 %copy-start.2 = (bf16[128,4096]{1,0:T(8,128)(2,1)S(1)}, bf16[128,4096]{1,0:T(8,128)(2,1)}, u32[]{:S(2)}) copy-start(bf16[128,4096]{1,0:T(8,128)(2,1)} %all-gather.2.cloned.1.call-done) | copy-start | bytes 3145732
  147.3 2.7 copy-start.44
Sparse Core Ops, SparseCore 0:
  11.0 89.4 all-gather.1
  138.2 258.1 all-reduce.1
  400.1 153.2 reduce-scatter.1
where the time goes:
time: 565 us; the launch traced here: 560 us
  waiting for transfers between devices  391 us (69%)
  blocking collectives  68.3 us (12%)
  other arithmetic  42.7 us (8%)
  local copies, waits for them, and re-layouts  29.8 us (5%)
  between operations  14.4 us (3%)
  starting transfers between devices  7.93 us (1%)
  matrix products  6.08 us (1%)
    psum x1, waiting for transfers between devices, body(): grad_filter, grad_skip = lax.psum((filter_term, skip_term), 'seq')  178 us
    reduce_scatter x1, waiting for transfers between devices, body(): lax.psum_scatter(weight_term * norm_factor, 'seq', scatter_dimension=1, t...  155 us
    psum x1, blocking collectives, body(): grad_filter, grad_skip = lax.psum((filter_term, skip_term), 'seq')  68.3 us
    all_gather x1, waiting for transfers between devices, body(): gathered = lax.all_gather(grad_out, 'chan', axis=1, tiled=True)  56.6 us
    slice x7, local copies, waits for them, and re-layouts, causal_sum(): tap_values[:, tap_index] * padded[offset:offset + length]  16.3 us
    concatenate x14, other arithmetic, body(): padded = jnp.concatenate([previous, mixed_in], axis=0)  13.7 us
    reduce_sum x14, other arithmetic, tap_products(): columns.append(jnp.sum(grad_sum * padded[offset:offset + length], axis=0))  12.2 us
    another operation x1, local copies, waits for them, and re-layouts, tap_products(): return jnp.stack(columns, axis=1)  11.6 us
  transfers between devices with their start and end apart: 5, of which 3 were waited for; matrix products, arithmetic and copies ran while one was open for 10% of the time, Pallas kernels for 0%

commit v1 on v0

v1 whole, which is shorter than its diff:
```python
import math

import jax
import jax.numpy as jnp
from jax import lax
from jax.experimental import pallas as pl
from jax.experimental.pallas import tpu as pltpu
from jax.sharding import PartitionSpec as P

TAPS = 128
LANES = 128
SUB = 8
XS, ZL, CORES = 4, 4, 2
ZH, YS = 4, 4
F32 = jnp.float32
BF16 = jnp.bfloat16


def seq_index(x, zl, core):
    return (x * ZL + zl) * CORES + core


def chan_index(zh, y):
    return zh * YS + y


ZH_GROUPS = [[chan_index(zh, y) for zh in range(ZH)] for y in range(YS)]
Y_GROUPS = [[chan_index(zh, y) for y in range(YS)] for zh in range(ZH)]
XC_GROUPS = [
    [seq_index(x, zl, core) for x in range(XS) for core in range(CORES)] for zl in range(ZL)
]
ZL_GROUPS = [
    [seq_index(x, zl, core) for zl in range(ZL)] for x in range(XS) for core in range(CORES)
]


def exchange(value, axis, groups):
    return lax.all_to_all(value, axis, 0, 0, tiled=True, axis_index_groups=groups)


def spread(value, axis, groups, size):
    return exchange(jnp.broadcast_to(value[None], (size, *value.shape)), axis, groups)


def passed_along(value, axis, by):
    size = lax.axis_size(axis)
    pairs = [(i, i + by) for i in range(size) if 0 <= i + by < size]
    return lax.ppermute(value, axis, pairs)


def causal_kernel(prev_ref, mixed_ref, taps_ref, gain_ref, query_ref, summed_ref, out_ref, pad):
    rows, width = mixed_ref.shape
    pad[:rows] = prev_ref[...]
    pad[rows:] = mixed_ref[...]
    for lane in range(0, width, LANES):
        cols = pl.ds(lane, LANES)
        tap_rows = taps_ref[cols, :].T
        total = gain_ref[:, cols] * mixed_ref[:, cols]
        for r in range(SUB):
            shifted = pad[pl.ds(SUB - r, 2 * rows - SUB), cols]
            for q in range(TAPS // SUB):
                start = rows - SUB - SUB * q
                j = SUB * q + r
                total = total + tap_rows[j : j + 1] * shifted[start : start + rows]
        summed_ref[:, cols] = total
        out_ref[:, cols] = (query_ref[:, cols].astype(F32) * total).astype(BF16)


def project_kernel(gathered_ref, weight_ref, query_ref, summed_ref, grad_query_ref, grad_sum_ref):
    width = gathered_ref.shape[-1]
    total = None
    for y in range(YS):
        for zh in range(ZH):
            block = weight_ref[:, pl.ds(chan_index(zh, y) * width, width)]
            term = lax.dot_general(
                gathered_ref[y, zh], block, (((1,), (1,)), ((), ())), preferred_element_type=F32
            )
            total = term if total is None else total + term
    grad_query_ref[...] = (total * summed_ref[...]).astype(BF16)
    grad_sum_ref[...] = total * query_ref[...].astype(F32)


def taps_kernel(norm_factor, prev_ref, mixed_ref, grad_sum_ref, out_ref, pad, rows_ref):
    rows, width = mixed_ref.shape
    pad[:rows] = prev_ref[...]
    pad[rows:] = mixed_ref[...]
    for lane in range(0, width, LANES):
        cols = pl.ds(lane, LANES)
        grad_sum = grad_sum_ref[:, cols]
        for r in range(SUB):
            shifted = pad[pl.ds(SUB - r, 2 * rows - SUB), cols]
            for q in range(TAPS // SUB):
                start = rows - SUB - SUB * q
                j = SUB * q + r
                rows_ref[j : j + 1, :] = jnp.sum(
                    grad_sum * shifted[start : start + rows], axis=0, keepdims=True
                )
        out_ref[cols, :] = rows_ref[...].T * norm_factor


def ahead_kernel(
    grad_sum_ref, incoming_ref, taps_ref, gain_ref, key_ref, value_ref, grad_key_ref, grad_value_ref, pad
):
    rows, width = grad_sum_ref.shape
    pad[:rows] = grad_sum_ref[...]
    pad[rows:] = incoming_ref[...]
    for lane in range(0, width, LANES):
        cols = pl.ds(lane, LANES)
        tap_rows = taps_ref[cols, :].T
        total = gain_ref[:, cols] * grad_sum_ref[:, cols]
        for r in range(SUB):
            shifted = pad[pl.ds(r, 2 * rows - SUB), cols]
            for q in range(TAPS // SUB):
                start = SUB * q
                j = SUB * q + r
                total = total + tap_rows[j : j + 1] * shifted[start : start + rows]
        grad_key_ref[:, cols] = (total * value_ref[:, cols].astype(F32)).astype(BF16)
        grad_value_ref[:, cols] = (total * key_ref[:, cols].astype(F32)).astype(BF16)


def weight_kernel(mixer_ref, pieces_ref, out_ref):
    for part in range(ZL):
        total = None
        for source in range(XS * CORES):
            term = lax.dot_general(
                mixer_ref[source],
                pieces_ref[source, part],
                (((0,), (0,)), ((), ())),
                preferred_element_type=F32,
            )
            total = term if total is None else total + term
        out_ref[part] = total.astype(BF16)


def call(kernel, name, shapes, scratch, flops, moved):
    return pl.pallas_call(
        kernel,
        out_shape=shapes,
        scratch_shapes=scratch,
        name=name,
        compiler_params=pltpu.CompilerParams(vmem_limit_bytes=32 * 1024 * 1024),
        cost_estimate=pl.CostEstimate(flops=flops, bytes_accessed=moved, transcendentals=0),
    )


def body(grad_out, query_gate, key_gate, value_input, filter_taps, skip_gain, out_weight):
    rows, width = query_gate.shape
    norm_factor = 1.0 / math.sqrt(rows * lax.axis_size("seq"))
    gain = skip_gain.reshape(1, width)
    block_f32 = jax.ShapeDtypeStruct((rows, width), F32)
    block_bf16 = jax.ShapeDtypeStruct((rows, width), BF16)
    padded = pltpu.VMEM((2 * rows, width), F32)
    size = rows * width

    mixed_in = key_gate.astype(F32) * value_input.astype(F32)
    previous = passed_along(mixed_in, "seq", 1)
    over_zh = spread(grad_out, "chan", ZH_GROUPS, ZH)
    gathered = spread(over_zh, "chan", Y_GROUPS, YS)
    gathered = gathered.reshape(YS, ZH, rows, width)

    summed, mixer_out = call(
        causal_kernel, "causal", (block_f32, block_bf16), [padded], 2 * size * TAPS, 20 * size
    )(previous, mixed_in, filter_taps, gain, query_gate)
    mixers = spread(mixer_out, "seq", XC_GROUPS, XS * CORES)

    grad_query, grad_sum = call(
        project_kernel, "project", (block_bf16, block_f32), [], 2 * size * 4096, 3 * 1024 * 1024
    )(gathered, out_weight, query_gate, summed)
    incoming = passed_along(grad_sum, "seq", -1)

    pieces = gathered.reshape(YS, ZH, rows, CORES, LANES).transpose(1, 3, 0, 2, 4)
    pieces = exchange(pieces.reshape(ZH * CORES, YS, rows, LANES), "seq", XC_GROUPS)

    filter_term = call(
        lambda *refs: taps_kernel(norm_factor, *refs),
        "taps",
        jax.ShapeDtypeStruct((width, TAPS), F32),
        [padded, pltpu.VMEM((TAPS, LANES), F32)],
        2 * size * TAPS,
        16 * size,
    )(previous, mixed_in, grad_sum)
    seq_size = lax.axis_size("seq")
    share = exchange(filter_term.reshape(seq_size, width // seq_size, TAPS), "seq", None)
    grad_filter = spread(jnp.sum(share, axis=0), "seq", None, seq_size).reshape(width, TAPS)
    grad_skip = grad_filter[:, 0]

    grad_key, grad_value = call(
        ahead_kernel, "ahead", (block_bf16, block_bf16), [padded], 2 * size * TAPS, 20 * size
    )(grad_sum, incoming, filter_taps, gain, key_gate, value_input)

    partial = call(
        weight_kernel,
        "weight",
        jax.ShapeDtypeStruct((ZL, width, LANES), BF16),
        [],
        2 * XS * CORES * rows * width * ZL * LANES,
        2 * 1024 * 1024,
    )(mixers, pieces)
    terms = exchange(partial, "seq", ZL_GROUPS)
    grad_weight = jnp.sum(terms.astype(F32), axis=0) * norm_factor
    return (grad_query, grad_key, grad_value, grad_filter, grad_skip, grad_weight)


def solution(mesh):
    return jax.shard_map(
        body,
        mesh=mesh,
        in_specs=(
            P("seq", "chan"),
            P("seq", "chan"),
            P("seq", "chan"),
            P("seq", "chan"),
            P("chan", None),
            P("chan"),
            P("chan", None),
        ),
        out_specs=(
            P("seq", "chan"),
            P("seq", "chan"),
            P("seq", "chan"),
            P("chan", None),
            P("chan"),
            P("chan", "seq"),
        ),
        check_vma=False,
    )
```

time: 565 us -> 137 us (0.24)
  waiting for transfers between devices: 391 us -> 41.8 us
  other arithmetic: 42.7 us -> 0.75 us
  blocking collectives: 68.3 us -> 29.7 us
  starting transfers between devices: 7.93 us -> 45.3 us
  local copies, waits for them, and re-layouts: 29.8 us -> 7.94 us
  between operations: 14.4 us -> 0.76 us
  Pallas kernels: 0 us -> 10.2 us
  matrix products: 6.08 us -> 0 us
    psum x1 -> x0, waiting for transfers between devices: 178 us -> none  [body(): grad_filter, grad_skip = lax.psum((filter_term, skip_term), 'seq')]
    reduce_scatter x1 -> x0, waiting for transfers between devices: 155 us -> none  [body(): lax.psum_scatter(weight_term * norm_factor, 'seq', scatter_dimension=1, t...]
    psum x1 -> x0, blocking collectives: 68.3 us -> none  [body(): grad_filter, grad_skip = lax.psum((filter_term, skip_term), 'seq')]
    all_gather x1 -> x0, waiting for transfers between devices: 56.6 us -> none  [body(): gathered = lax.all_gather(grad_out, 'chan', axis=1, tiled=True)]
    all_to_all x0 -> x6, waiting for transfers between devices: none -> 33.9 us  [exchange(): lax.all_to_all(value, axis, 0, 0, tiled=True, axis_index_groups=groups)]
    all_to_all x0 -> x6, starting transfers between devices: none -> 32.1 us  [exchange(): lax.all_to_all(value, axis, 0, 0, tiled=True, axis_index_groups=groups)]
    all_to_all x0 -> x1, blocking collectives: none -> 29.7 us  [exchange(): lax.all_to_all(value, axis, 0, 0, tiled=True, axis_index_groups=groups)]
    slice x8 -> x1, local copies, waits for them, and re-layouts: 16.3 us -> 0.68 us  [body(): grad_skip = grad_filter[:, 0]]
  transfers between devices with their start and end apart: 5 -> 8, of which waited for: 3 -> 6; matrix products, arithmetic and copies ran while one was open for 10% -> 2% of each run, Pallas kernels for 0% -> 7%
where the time goes in v1:
time: 137 us; the launch traced here: 136 us
  starting transfers between devices  45.3 us (33%)
  waiting for transfers between devices  41.8 us (31%)
  blocking collectives  29.7 us (22%)
  Pallas kernels  10.2 us (7%)
  local copies, waits for them, and re-layouts  7.94 us (6%)
    all_to_all x6, waiting for transfers between devices, exchange(): lax.all_to_all(value, axis, 0, 0, tiled=True, axis_index_groups=groups)  33.9 us
    all_to_all x6, starting transfers between devices, exchange(): lax.all_to_all(value, axis, 0, 0, tiled=True, axis_index_groups=groups)  32.1 us
    all_to_all x1, blocking collectives, exchange(): lax.all_to_all(value, axis, 0, 0, tiled=True, axis_index_groups=groups)  29.7 us
    ppermute x2, starting transfers between devices, passed_along(): return lax.ppermute(value, axis, pairs)  13.2 us
    ppermute x2, waiting for transfers between devices, passed_along(): return lax.ppermute(value, axis, pairs)  7.9 us
    broadcast_in_dim x4, local copies, waits for them, and re-layouts, spread(): jnp.broadcast_to(value[None], (size, *value.shape))  3.47 us
    pallas_call x1, Pallas kernels, body(): call(ahead_kernel, 'ahead', (block_bf16, block_bf16), [padded], 2 * size...  2.87 us
  transfers between devices with their start and end apart: 8, of which 6 were waited for; matrix products, arithmetic and copies ran while one was open for 2% of the time, Pallas kernels for 7%

profile of v1, /device:TPU:1, one launch (start us, length us, event | category | flops | bytes accessed | tf_op | source)
XLA Modules:
  0.0 136.4 jit_solution(12973597725415972850)
XLA Ops:
  0.6 0.0 copy-start.3
  0.6 0.0 copy-start.4
  0.7 0.9 broadcast_in_dim.8
  1.5 0.0 copy-start.1
  1.6 0.0 copy-start.2
  1.6 0.0 copy-start.5
  1.6 29.7 %all_to_all.35 = bf16[4,128,256]{2,1,0:T(8,128)(2,1)S(1)} all-to-all(bf16[4,128,256]{2,1,0:T(8,128)(2,1)S(1)} %broadcast_in_dim.8), channel_id=1, replica_groups={{0,4,8,12},{1,5,9,13},{2,6,10,14},{3,7,11,15},{16,20,24,28},{17,21,25,2..., dimensions={0} | all-to-all | bytes 524288 | tf_op jit(solution)/shard_map/all_to_all | solution.py:38
  31.3 1.1 broadcast_in_dim.9
  32.4 4.2 %all-to-all-start.1 = ((bf16[4,4,128,256]{3,2,1,0:T(8,128)(2,1)}), bf16[4,4,128,256]{3,2,1,0:T(8,128)(2,1)S(1)}, u32[]{:S(2)}, u32[]{:S(2)}) async-start(bf16[4,4,128,256]{3,2,1,0:T(8,128)(2,1)} %broadcast_in_dim.9), calls=%async_computation.1 | async-start | bytes 2097152 | tf_op jit(solution)/shard_map/all_to_all | solution.py:38
  36.6 0.0 copy-done.3
  36.6 0.0 copy-done.4
  36.6 10.9 %collective-permute-start = (f32[128,256]{1,0:T(8,128)S(1)}, f32[128,256]{1,0:T(8,128)S(1)}, u32[]{:S(2)}, u32[]{:S(2)}) collective-permute-start(f32[128,256]{1,0:T(8,128)S(1)} %convert_multiply_fusion.mixed_ref.refs_1_), channel_id=1, source_target_pairs={{0,16},{16,32},{32,48},{48,64},{64,80},{80,96},{96,112},{112,128},... | collective-permute-start | bytes 393224 | tf_op jit(solution)/shard_map/ppermute | solution.py:48
  47.5 1.9 %collective-permute-done.prev_ref.refs_0_ = f32[128,256]{1,0:T(8,128)S(1)} collective-permute-done((f32[128,256]{1,0:T(8,128)S(1)}, f32[128,256]{1,0:T(8,128)S(1)}, u32[]{:S(2)}, u32[]{:S(2)}) %collective-permute-start) | collective-permute-done | bytes 131104 | tf_op jit(solution)/shard_map/ppermute | solution.py:48
  49.4 0.0 copy-done.1
  49.4 0.0 copy-done.2
  49.4 0.0 copy-done.5
  49.4 2.2 %causal.1 = (f32[128,256]{1,0:T(8,128)S(1)}, bf16[128,256]{1,0:T(8,128)(2,1)S(1)}) custom-call(f32[128,256]{1,0:T(8,128)S(1)} %collective-permute-done.prev_ref.refs_0_, f32[128,256]{1,0:T(8,128)S(1)} %convert_multiply_fusion.mixed_ref.refs_1_, f32[256,128]{1,0:T(8,128)S(1)} %copy-done.1, f32[1,256]{1,0:T(1,128)S(1)} %bitcast.8, bf16[128,256]{1,0:T(8,128)(2,1)S(1)} %copy-done.2), custom_call_target="tpu_custom_call" | custom-call | flops 8388608 | bytes 655360 | tf_op jit(solution)/shard_map/causal/pallas_call | solution.py:161
  51.7 0.0 all-to-all-done.1.gathered_ref
  51.7 0.8 broadcast_in_dim.11
  52.5 6.3 %all-to-all-start.4 = ((bf16[8,128,256]{2,1,0:T(8,128)(2,1)}), bf16[8,128,256]{2,1,0:T(8,128)(2,1)S(1)}, u32[]{:S(2)}, u32[]{:S(2)}) async-start(bf16[8,128,256]{2,1,0:T(8,128)(2,1)} %broadcast_in_dim.11), calls=%async_computation.4 | async-start | bytes 1048576 | tf_op jit(solution)/shard_map/all_to_all | solution.py:38
  58.7 0.0 copy-start
  58.8 1.6 %copy-done = bf16[256,4096]{1,0:T(8,128)(2,1)S(1)} copy-done((bf16[256,4096]{1,0:T(8,128)(2,1)S(1)}, bf16[256,4096]{1,0:T(8,128)(2,1)}, u32[]{:S(2)}) %copy-start) | copy-done | bytes 2097176
  60.3 1.4 %project.1 = (bf16[128,256]{1,0:T(8,128)(2,1)}, f32[128,256]{1,0:T(8,128)S(1)}) custom-call(bf16[4,4,128,256]{3,2,1,0:T(8,128)(2,1)S(1)} %all-to-all-done.1.gathered_ref, bf16[256,4096]{1,0:T(8,128)(2,1)S(1)} %copy-done, bf16[128,256]{1,0:T(8,128)(2,1)S(1)} %copy-done.2, f32[128,256]{1,0:T(8,128)S(1)} %get-tuple-element.12.summed_ref), custom_call_target="tpu_custom_call" | custom-call | flops 268435456 | bytes 3145728 | tf_op jit(solution)/shard_map/project/pallas_call | solution.py:166
  61.8 2.2 %taps.1 = f32[256,128]{1,0:T(8,128)} custom-call(f32[128,256]{1,0:T(8,128)S(1)} %collective-permute-done.prev_ref.refs_0_, f32[128,256]{1,0:T(8,128)S(1)} %convert_multiply_fusion.mixed_ref.refs_1_, f32[128,256]{1,0:T(8,128)S(1)} %get-tuple-element.14.grad_sum_ref.refs_2_), custom_call_target="tpu_custom_call" | custom-call | flops 8388608 | bytes 524288 | tf_op jit(solution)/shard_map/taps/pallas_call | solution.py:174
  64.0 4.3 %all-to-all-done.4.mixer_ref = bf16[8,128,256]{2,1,0:T(8,128)(2,1)S(1)} async-done(((bf16[8,128,256]{2,1,0:T(8,128)(2,1)}), bf16[8,128,256]{2,1,0:T(8,128)(2,1)S(1)}, u32[]{:S(2)}, u32[]{:S(2)}) %all-to-all-start.4) | async-done | bytes 524320 | tf_op jit(solution)/shard_map/all_to_all | solution.py:38
  68.2 10.0 %all-to-all-start.2 = ((f32[32,8,128]{2,1,0:T(8,128)}), f32[32,8,128]{2,1,0:T(8,128)S(1)}, u32[]{:S(2)}, u32[]{:S(2)}) async-start(f32[32,8,128]{2,1,0:T(8,128)} %bitcast.1), calls=%async_computation.2 | async-start | bytes 262144 | tf_op jit(solution)/shard_map/all_to_all | solution.py:38
  78.2 0.3 reshape.34
  78.5 1.2 copy.14
  79.8 7.2 %all-to-all-done.2 = f32[32,8,128]{2,1,0:T(8,128)S(1)} async-done(((f32[32,8,128]{2,1,0:T(8,128)}), f32[32,8,128]{2,1,0:T(8,128)S(1)}, u32[]{:S(2)}, u32[]{:S(2)}) %all-to-all-start.2) | async-done | bytes 131104 | tf_op jit(solution)/shard_map/all_to_all | solution.py:38
  86.9 3.9 %all-to-all-start.5 = ((bf16[8,4,128,128]{3,2,1,0:T(8,128)(2,1)}), bf16[8,4,128,128]{3,2,1,0:T(8,128)(2,1)S(1)}, u32[]{:S(2)}, u32[]{:S(2)}) async-start(bf16[8,4,128,128]{3,2,1,0:T(8,128)(2,1)} %bitcast.4), calls=%async_computation.5 | async-start | bytes 2097152 | tf_op jit(solution)/shard_map/all_to_all | solution.py:38
  90.8 15.1 %all-to-all-done.5.pieces_ref = bf16[8,4,128,128]{3,2,1,0:T(8,128)(2,1)S(1)} async-done(((bf16[8,4,128,128]{3,2,1,0:T(8,128)(2,1)}), bf16[8,4,128,128]{3,2,1,0:T(8,128)(2,1)S(1)}, u32[]{:S(2)}, u32[]{:S(2)}) %all-to-all-start.5) | async-done | bytes 1048608 | tf_op jit(solution)/shard_map/all_to_all | solution.py:38
  105.9 0.7 broadcast_in_dim.10
  106.6 4.4 %all-to-all-start.3 = ((f32[32,8,128]{2,1,0:T(8,128)}), f32[32,8,128]{2,1,0:T(8,128)S(1)}, u32[]{:S(2)}, u32[]{:S(2)}) async-start(f32[32,8,128]{2,1,0:T(8,128)} %broadcast_in_dim.10), calls=%async_computation.3 | async-start | bytes 262144 | tf_op jit(solution)/shard_map/all_to_all | solution.py:38
  111.0 1.4 %weight.1 = bf16[4,256,128]{2,1,0:T(8,128)(2,1)} custom-call(bf16[8,128,256]{2,1,0:T(8,128)(2,1)S(1)} %all-to-all-done.4.mixer_ref, bf16[8,4,128,128]{3,2,1,0:T(8,128)(2,1)S(1)} %all-to-all-done.5.pieces_ref), custom_call_target="tpu_custom_call" | custom-call | flops 268435456 | bytes 2097152 | tf_op jit(solution)/shard_map/weight/pallas_call | solution.py:191
  112.4 7.4 %all-to-all-done.3 = f32[32,8,128]{2,1,0:T(8,128)S(1)} async-done(((f32[32,8,128]{2,1,0:T(8,128)}), f32[32,8,128]{2,1,0:T(8,128)S(1)}, u32[]{:S(2)}, u32[]{:S(2)}) %all-to-all-start.3) | async-done | bytes 131104 | tf_op jit(solution)/shard_map/all_to_all | solution.py:38
  119.8 3.4 %all-to-all-start.6 = ((bf16[4,256,128]{2,1,0:T(8,128)(2,1)}), bf16[4,256,128]{2,1,0:T(8,128)(2,1)S(1)}, u32[]{:S(2)}, u32[]{:S(2)}) async-start(bf16[4,256,128]{2,1,0:T(8,128)(2,1)} %weight.1), calls=%async_computation.6 | async-start | bytes 524288 | tf_op jit(solution)/shard_map/all_to_all | solution.py:38
  123.2 2.3 %collective-permute-start.1 = (f32[128,256]{1,0:T(8,128)S(1)}, f32[128,256]{1,0:T(8,128)S(1)}, u32[]{:S(2)}, u32[]{:S(2)}) collective-permute-start(f32[128,256]{1,0:T(8,128)S(1)} %get-tuple-element.14.grad_sum_ref.refs_2_), channel_id=1, source_target_pairs={{16,0},{32,16},{48,32},{64,48},{80,64},{96,80},{112,96},{128,112},... | collective-permute-start | bytes 393224 | tf_op jit(solution)/shard_map/ppermute | solution.py:48
  125.5 6.0 %collective-permute-done.1.incoming_ref = f32[128,256]{1,0:T(8,128)S(1)} collective-permute-done((f32[128,256]{1,0:T(8,128)S(1)}, f32[128,256]{1,0:T(8,128)S(1)}, u32[]{:S(2)}, u32[]{:S(2)}) %collective-permute-start.1) | collective-permute-done | bytes 131104 | tf_op jit(solution)/shard_map/ppermute | solution.py:48
  131.5 2.9 %ahead.1 = (bf16[128,256]{1,0:T(8,128)(2,1)}, bf16[128,256]{1,0:T(8,128)(2,1)}) custom-call(f32[128,256]{1,0:T(8,128)S(1)} %get-tuple-element.14.grad_sum_ref.refs_2_, f32[128,256]{1,0:T(8,128)S(1)} %collective-permute-done.1.incoming_ref, f32[256,128]{1,0:T(8,128)S(1)} %copy-done.1, f32[1,256]{1,0:T(1,128)S(1)} %bitcast.9, bf16[128,256]{1,0:T(8,128)(2,1)S(1)} %copy-done.4, ...), custom_call_target="tpu_custom_call" | custom-call | flops 8388608 | bytes 655360 | tf_op jit(solution)/shard_map/ahead/pallas_call | solution.py:187
  134.4 0.7 slice_reduce_fusion
  135.0 0.0 all-to-all-done.6
  135.1 0.7 broadcast_multiply_fusion
  135.7 0.7 copy.16
  (3 shorter events, 0.1 us)
Async XLA Ops:
  0.6 35.9 %copy-start.3 = (bf16[128,256]{1,0:T(8,128)(2,1)S(1)}, bf16[128,256]{1,0:T(8,128)(2,1)}, u32[]{:S(2)}) copy-start(bf16[128,256]{1,0:T(8,128)(2,1)} %value_ref.1) | copy-start | bytes 196612
  0.6 35.9 %copy-start.4 = (bf16[128,256]{1,0:T(8,128)(2,1)S(1)}, bf16[128,256]{1,0:T(8,128)(2,1)}, u32[]{:S(2)}) copy-start(bf16[128,256]{1,0:T(8,128)(2,1)} %key_ref.1) | copy-start | bytes 196612
  1.5 47.9 %copy-start.1 = (f32[256,128]{1,0:T(8,128)S(1)}, f32[256,128]{1,0:T(8,128)}, u32[]{:S(2)}) copy-start(f32[256,128]{1,0:T(8,128)} %taps_ref.3) | copy-start | bytes 393220
  1.6 47.9 %copy-start.2 = (bf16[128,256]{1,0:T(8,128)(2,1)S(1)}, bf16[128,256]{1,0:T(8,128)(2,1)}, u32[]{:S(2)}) copy-start(bf16[128,256]{1,0:T(8,128)(2,1)} %query_ref.3) | copy-start | bytes 196612
  1.6 47.9 %copy-start.5 = (f32[256]{0:T(256)S(1)}, f32[256]{0:T(256)}, u32[]{:S(2)}) copy-start(f32[256]{0:T(256)} %param.12) | copy-start | bytes 3076
  32.4 19.3 %all-to-all-start.1 = ((bf16[4,4,128,256]{3,2,1,0:T(8,128)(2,1)}), bf16[4,4,128,256]{3,2,1,0:T(8,128)(2,1)S(1)}, u32[]{:S(2)}, u32[]{:S(2)}) async-start(bf16[4,4,128,256]{3,2,1,0:T(8,128)(2,1)} %broadcast_in_dim.9), calls=%async_computation.1 | async-start | bytes 2097152 | tf_op jit(solution)/shard_map/all_to_all | solution.py:38
  36.6 12.8 %collective-permute-start = (f32[128,256]{1,0:T(8,128)S(1)}, f32[128,256]{1,0:T(8,128)S(1)}, u32[]{:S(2)}, u32[]{:S(2)}) collective-permute-start(f32[128,256]{1,0:T(8,128)S(1)} %convert_multiply_fusion.mixed_ref.refs_1_), channel_id=1, source_target_pairs={{0,16},{16,32},{32,48},{48,64},{64,80},{80,96},{96,112},{112,128},... | collective-permute-start | bytes 393224 | tf_op jit(solution)/shard_map/ppermute | solution.py:48
  52.5 15.7 %all-to-all-start.4 = ((bf16[8,128,256]{2,1,0:T(8,128)(2,1)}), bf16[8,128,256]{2,1,0:T(8,128)(2,1)S(1)}, u32[]{:S(2)}, u32[]{:S(2)}) async-start(bf16[8,128,256]{2,1,0:T(8,128)(2,1)} %broadcast_in_dim.11), calls=%async_computation.4 | async-start | bytes 1048576 | tf_op jit(solution)/shard_map/all_to_all | solution.py:38
  58.7 1.6 %copy-start = (bf16[256,4096]{1,0:T(8,128)(2,1)S(1)}, bf16[256,4096]{1,0:T(8,128)(2,1)}, u32[]{:S(2)}) copy-start(bf16[256,4096]{1,0:T(8,128)(2,1)} %weight_ref.1) | copy-start | bytes 6291460
  68.2 18.7 %all-to-all-start.2 = ((f32[32,8,128]{2,1,0:T(8,128)}), f32[32,8,128]{2,1,0:T(8,128)S(1)}, u32[]{:S(2)}, u32[]{:S(2)}) async-start(f32[32,8,128]{2,1,0:T(8,128)} %bitcast.1), calls=%async_computation.2 | async-start | bytes 262144 | tf_op jit(solution)/shard_map/all_to_all | solution.py:38
  86.9 19.0 %all-to-all-start.5 = ((bf16[8,4,128,128]{3,2,1,0:T(8,128)(2,1)}), bf16[8,4,128,128]{3,2,1,0:T(8,128)(2,1)S(1)}, u32[]{:S(2)}, u32[]{:S(2)}) async-start(bf16[8,4,128,128]{3,2,1,0:T(8,128)(2,1)} %bitcast.4), calls=%async_computation.5 | async-start | bytes 2097152 | tf_op jit(solution)/shard_map/all_to_all | solution.py:38
  106.6 13.2 %all-to-all-start.3 = ((f32[32,8,128]{2,1,0:T(8,128)}), f32[32,8,128]{2,1,0:T(8,128)S(1)}, u32[]{:S(2)}, u32[]{:S(2)}) async-start(f32[32,8,128]{2,1,0:T(8,128)} %broadcast_in_dim.10), calls=%async_computation.3 | async-start | bytes 262144 | tf_op jit(solution)/shard_map/all_to_all | solution.py:38
  119.8 15.2 %all-to-all-start.6 = ((bf16[4,256,128]{2,1,0:T(8,128)(2,1)}), bf16[4,256,128]{2,1,0:T(8,128)(2,1)S(1)}, u32[]{:S(2)}, u32[]{:S(2)}) async-start(bf16[4,256,128]{2,1,0:T(8,128)(2,1)} %weight.1), calls=%async_computation.6 | async-start | bytes 524288 | tf_op jit(solution)/shard_map/all_to_all | solution.py:38
  123.2 8.3 %collective-permute-start.1 = (f32[128,256]{1,0:T(8,128)S(1)}, f32[128,256]{1,0:T(8,128)S(1)}, u32[]{:S(2)}, u32[]{:S(2)}) collective-permute-start(f32[128,256]{1,0:T(8,128)S(1)} %get-tuple-element.14.grad_sum_ref.refs_2_), channel_id=1, source_target_pairs={{16,0},{32,16},{48,32},{64,48},{80,64},{96,80},{112,96},{128,112},... | collective-permute-start | bytes 393224 | tf_op jit(solution)/shard_map/ppermute | solution.py:48

commit v2 on v1

v2 whole, which is shorter than its diff:
```python
import math

import jax
import jax.numpy as jnp
from jax import lax
from jax.experimental import pallas as pl
from jax.experimental.pallas import tpu as pltpu
from jax.sharding import PartitionSpec as P

TAPS = 128
LANES = 128
SUB = 8
XS, ZL, CORES = 4, 4, 2
ZH, YS = 4, 4
F32 = jnp.float32
BF16 = jnp.bfloat16


def seq_index(x, zl, core):
    return (x * ZL + zl) * CORES + core


def chan_index(zh, y):
    return zh * YS + y


ZH_GROUPS = [[chan_index(zh, y) for zh in range(ZH)] for y in range(YS)]
Y_GROUPS = [[chan_index(zh, y) for y in range(YS)] for zh in range(ZH)]
XC_GROUPS = [
    [seq_index(x, zl, core) for x in range(XS) for core in range(CORES)] for zl in range(ZL)
]
ZL_GROUPS = [
    [seq_index(x, zl, core) for zl in range(ZL)] for x in range(XS) for core in range(CORES)
]
X_GROUPS = [
    [seq_index(x, zl, core) for x in range(XS)] for zl in range(ZL) for core in range(CORES)
]


def exchange(value, axis, groups):
    return lax.all_to_all(value, axis, 0, 0, tiled=True, axis_index_groups=groups)


def spread(value, axis, groups, size):
    return exchange(jnp.broadcast_to(value[None], (size, *value.shape)), axis, groups)


def collect(value, groups):
    return lax.all_gather(value, "seq", axis=0, axis_index_groups=groups)


def other_core(value):
    size = lax.axis_size("seq")
    return lax.ppermute(value, "seq", [(i, i ^ 1) for i in range(size)])


def passed_along(value, axis, by):
    size = lax.axis_size(axis)
    pairs = [(i, i + by) for i in range(size) if 0 <= i + by < size]
    return lax.ppermute(value, axis, pairs)


def fetch(sources, held, sem, first=0):
    copies = [
        pltpu.make_async_copy(source, target, sem.at[first + at])
        for at, (source, target) in enumerate(zip(sources, held))
    ]
    for copy in copies:
        copy.start()
    return copies


def finish(copies):
    for copy in copies:
        copy.wait()


def causal_kernel(
    prev_ref,
    mixed_ref,
    taps_ref,
    gain_ref,
    query_ref,
    summed_ref,
    out_ref,
    pad,
    query,
    summed,
    out,
    sem,
):
    copies = fetch((query_ref,), (query,), sem)
    rows, width = mixed_ref.shape
    pad[:rows] = prev_ref[...]
    pad[rows:] = mixed_ref[...]
    for lane in range(0, width, LANES):
        cols = pl.ds(lane, LANES)
        tap_rows = taps_ref[cols, :].T
        total = gain_ref[:, cols] * mixed_ref[:, cols]
        for r in range(SUB):
            shifted = pad[pl.ds(SUB - r, 2 * rows - SUB), cols]
            for q in range(TAPS // SUB):
                start = rows - SUB - SUB * q
                j = SUB * q + r
                total = total + tap_rows[j : j + 1] * shifted[start : start + rows]
        summed[:, cols] = total
        if lane == 0:
            finish(copies)
        out[lane // LANES] = (query[:, cols].astype(F32) * total).T.astype(BF16)
    finish(fetch((summed, out), (summed_ref, out_ref), sem, 1))


def main_kernel(
    norm_factor,
    gathered_ref,
    mixer_ref,
    weight_ref,
    query_ref,
    summed_ref,
    prev_ref,
    mixed_ref,
    grad_query_ref,
    grad_sum_ref,
    filter_ref,
    packed_ref,
    held,
    mixers,
    query,
    summed,
    pad,
    tap_rows,
    weight_sem,
    pack_sem,
    sem,
):
    rows, width = mixed_ref.shape
    blocks = fetch((mixer_ref, query_ref, summed_ref), (mixers, query, summed), sem)
    loads = []
    for zh in range(ZH):
        cols = pl.ds(zh * YS * width, YS * width)
        loads.append(pltpu.make_async_copy(weight_ref.at[:, cols], held.at[zh], weight_sem.at[zh]))
        loads[-1].start()
    packs = []
    for zh in range(ZH):
        for core in range(CORES):
            target = zh * CORES + core
            for y in range(YS):
                source = gathered_ref.at[y, zh, :, pl.ds(core * LANES, LANES)]
                packs.append(
                    pltpu.make_async_copy(source, packed_ref.at[target, y], pack_sem.at[target, y])
                )
            place = packed_ref.at[target, pl.ds(YS, mixers.shape[0])]
            packs.append(pltpu.make_async_copy(mixers, place, pack_sem.at[target, YS]))
    finish(blocks)
    for copy in packs:
        copy.start()

    total = None
    for zh in range(ZH):
        loads[zh].wait()
        for y in range(YS):
            term = lax.dot_general(
                gathered_ref[y, zh],
                held[zh, :, pl.ds(y * width, width)],
                (((1,), (1,)), ((), ())),
                preferred_element_type=F32,
            )
            total = term if total is None else total + term
    grad_query_ref[...] = (total * summed[...]).astype(BF16)
    grad_sum_ref[...] = total * query[...].astype(F32)

    pad[:rows] = prev_ref[...]
    pad[rows:] = mixed_ref[...]
    for lane in range(0, width, LANES):
        cols = pl.ds(lane, LANES)
        grad_sum = grad_sum_ref[:, cols]
        for r in range(SUB):
            shifted = pad[pl.ds(SUB - r, 2 * rows - SUB), cols]
            for q in range(TAPS // SUB):
                start = rows - SUB - SUB * q
                j = SUB * q + r
                tap_rows[j : j + 1, :] = jnp.sum(
                    grad_sum * shifted[start : start + rows], axis=0, keepdims=True
                )
        filter_ref[cols, :] = tap_rows[...].T * norm_factor
    finish(packs)


def ahead_kernel(
    grad_sum_ref,
    incoming_ref,
    taps_ref,
    gain_ref,
    key_ref,
    value_ref,
    grad_key_ref,
    grad_value_ref,
    pad,
    key,
    value,
    sem,
):
    copies = fetch((key_ref, value_ref), (key, value), sem)
    rows, width = grad_sum_ref.shape
    pad[:rows] = grad_sum_ref[...]
    pad[rows:] = incoming_ref[...]
    for lane in range(0, width, LANES):
        cols = pl.ds(lane, LANES)
        tap_rows = taps_ref[cols, :].T
        total = gain_ref[:, cols] * grad_sum_ref[:, cols]
        for r in range(SUB):
            shifted = pad[pl.ds(r, 2 * rows - SUB), cols]
            for q in range(TAPS // SUB):
                start = SUB * q
                j = SUB * q + r
                total = total + tap_rows[j : j + 1] * shifted[start : start + rows]
        if lane == 0:
            finish(copies)
        grad_key_ref[:, cols] = (total * value[:, cols].astype(F32)).astype(BF16)
        grad_value_ref[:, cols] = (total * key[:, cols].astype(F32)).astype(BF16)


def weight_kernel(pieces_ref, out_ref):
    def side_by_side(blocks):
        return jnp.concatenate(blocks, axis=1)

    halves = pieces_ref.shape[1] - ZL
    for pair in range(0, ZL, 2):
        total = None
        for x in range(XS):
            sources = range(CORES * x, CORES * (x + 1))
            mixers = jnp.concatenate(
                [side_by_side([pieces_ref[at, ZL + half] for at in sources]) for half in range(halves)],
                axis=0,
            )
            tokens = jnp.concatenate(
                [side_by_side([pieces_ref[at, pair + k] for k in range(2)]) for at in sources], axis=0
            )
            term = jnp.dot(mixers, tokens, preferred_element_type=F32)
            total = term if total is None else total + term
        for k in range(2):
            out_ref[pair + k] = total[:, k * LANES : (k + 1) * LANES].astype(BF16)


def call(kernel, name, shapes, scratch, flops, moved, vmem=32, **specs):
    return pl.pallas_call(
        kernel,
        out_shape=shapes,
        scratch_shapes=scratch,
        name=name,
        compiler_params=pltpu.CompilerParams(vmem_limit_bytes=vmem * 1024 * 1024),
        cost_estimate=pl.CostEstimate(flops=flops, bytes_accessed=moved, transcendentals=0),
        **specs,
    )


def body(grad_out, query_gate, key_gate, value_input, filter_taps, skip_gain, out_weight):
    rows, width = query_gate.shape
    norm_factor = 1.0 / math.sqrt(rows * lax.axis_size("seq"))
    gain = skip_gain.reshape(1, width)
    block_f32 = jax.ShapeDtypeStruct((rows, width), F32)
    block_bf16 = jax.ShapeDtypeStruct((rows, width), BF16)
    padded = pltpu.VMEM((2 * rows, width), F32)
    held_f32, held_bf16 = pltpu.VMEM((rows, width), F32), pltpu.VMEM((rows, width), BF16)
    in_vmem = pl.BlockSpec(memory_space=pltpu.VMEM)
    in_hbm = pl.BlockSpec(memory_space=pltpu.HBM)
    stay = lambda value: pltpu.with_memory_space_constraint(value, pltpu.HBM)
    query, key, value = stay(query_gate), stay(key_gate), stay(value_input)
    weight = stay(out_weight)
    halves = width // LANES
    held_mixers = pltpu.VMEM((halves, LANES, rows), BF16)
    size = rows * width

    mixed_in = key_gate.astype(F32) * value_input.astype(F32)
    previous = passed_along(mixed_in, "seq", 1)
    over_zh = lax.all_gather(grad_out, "chan", axis=0, axis_index_groups=ZH_GROUPS)
    gathered = spread(over_zh, "chan", Y_GROUPS, YS)
    gathered = gathered.reshape(YS, ZH, rows, width)
    summed, mixer_out = call(
        causal_kernel,
        "causal",
        (pltpu.HBM((rows, width), F32), pltpu.HBM((halves, LANES, rows), BF16)),
        [
            padded,
            held_bf16,
            held_f32,
            held_mixers,
            pltpu.SemaphoreType.DMA((3,)),
        ],
        2 * size * TAPS,
        20 * size,
        in_specs=[in_vmem, in_vmem, in_vmem, in_vmem, in_hbm],
        out_specs=[in_hbm, in_hbm],
    )(previous, mixed_in, filter_taps, gain, query)

    targets, blocks = ZH * CORES, YS + halves
    grad_query, grad_sum, filter_term, packed = call(
        lambda *refs: main_kernel(norm_factor, *refs),
        "main",
        (
            block_bf16,
            block_f32,
            jax.ShapeDtypeStruct((width, TAPS), F32),
            pltpu.HBM((targets, blocks, rows, LANES), BF16),
        ),
        [
            pltpu.VMEM((ZH, width, YS * width), BF16),
            held_mixers,
            held_bf16,
            held_f32,
            padded,
            pltpu.VMEM((TAPS, LANES), F32),
            pltpu.SemaphoreType.DMA((ZH,)),
            pltpu.SemaphoreType.DMA((targets, YS + 1)),
            pltpu.SemaphoreType.DMA((3,)),
        ],
        2 * size * (4096 + TAPS),
        8 * 1024 * 1024,
        in_specs=[in_vmem, in_hbm, in_hbm, in_hbm, in_hbm, in_vmem, in_vmem],
        out_specs=[in_vmem, in_vmem, in_vmem, in_hbm],
    )(gathered, stay(mixer_out), weight, query, stay(summed), previous, mixed_in)
    pieces = exchange(packed, "seq", XC_GROUPS)
    incoming = passed_along(grad_sum, "seq", -1)
    from_core = other_core(filter_term)
    grad_key, grad_value = call(
        ahead_kernel,
        "ahead",
        (block_bf16, block_bf16),
        [
            padded,
            held_bf16,
            held_bf16,
            pltpu.SemaphoreType.DMA((2,)),
        ],
        2 * size * TAPS,
        20 * size,
        in_specs=[in_vmem, in_vmem, in_vmem, in_vmem, in_hbm, in_hbm],
    )(grad_sum, incoming, filter_taps, gain, key, value)
    from_core, grad_key, grad_value = lax.optimization_barrier((from_core, grad_key, grad_value))
    filter_term = (filter_term + from_core).astype(BF16)
    filter_term = jnp.sum(collect(filter_term, ZL_GROUPS).astype(F32), axis=0)

    pieces, filter_term = lax.optimization_barrier((pieces, filter_term))
    partial = call(
        weight_kernel,
        "weight",
        jax.ShapeDtypeStruct((ZL, width, LANES), BF16),
        [],
        2 * XS * CORES * rows * width * ZL * LANES,
        2 * 1024 * 1024,
    )(pieces)
    partial, filter_term = lax.optimization_barrier((partial, filter_term))
    terms = exchange(partial, "seq", ZL_GROUPS)
    grad_filter = jnp.sum(collect(filter_term, X_GROUPS), axis=0)
    grad_skip = grad_filter[:, 0]
    grad_weight = jnp.sum(terms.astype(F32), axis=0) * norm_factor
    return (grad_query, grad_key, grad_value, grad_filter, grad_skip, grad_weight)


def solution(mesh):
    return jax.shard_map(
        body,
        mesh=mesh,
        in_specs=(
            P("seq", "chan"),
            P("seq", "chan"),
            P("seq", "chan"),
            P("seq", "chan"),
            P("chan", None),
            P("chan"),
            P("chan", None),
        ),
        out_specs=(
            P("seq", "chan"),
            P("seq", "chan"),
            P("seq", "chan"),
            P("chan", None),
            P("chan"),
            P("chan", "seq"),
        ),
        check_vma=False,
    )
```

time: 137 us -> 100 us (0.73)
  the two profiles are of different devices: /device:TPU:1 before, /device:TPU:32 now
where the time goes in v2:
time: 100 us; the launch traced here: 99.8 us
  blocking collectives  54.7 us (55%)
  starting transfers between devices  20.7 us (21%)
  Pallas kernels  13.1 us (13%)
  waiting for transfers between devices  8.02 us (8%)
  local copies, waits for them, and re-layouts  1.78 us (2%)
    all_gather x2, blocking collectives, collect(): return lax.all_gather(value, 'seq', axis=0, axis_index_groups=groups)  28.5 us
    all_gather x1, blocking collectives, body(): lax.all_gather(grad_out, 'chan', axis=0, axis_index_groups=ZH_GROUPS)  26.2 us
    all_to_all x3, starting transfers between devices, exchange(): lax.all_to_all(value, axis, 0, 0, tiled=True, axis_index_groups=groups)  13.8 us
    pallas_call x1, Pallas kernels, body(): call(lambda *refs: main_kernel(norm_factor, *refs), 'main', (block_bf16,...  5.59 us
    ppermute x2, waiting for transfers between devices, passed_along(): return lax.ppermute(value, axis, pairs)  4.93 us
    ppermute x2, starting transfers between devices, passed_along(): return lax.ppermute(value, axis, pairs)  4.91 us
    pallas_call x1, Pallas kernels, body(): call(causal_kernel, 'causal', (pltpu.HBM((rows, width), F32), pltpu.HBM((...  3.39 us
    all_to_all x3, waiting for transfers between devices, exchange(): lax.all_to_all(value, axis, 0, 0, tiled=True, axis_index_groups=groups)  3.09 us
  transfers between devices with their start and end apart: 6, of which 4 were waited for; matrix products, arithmetic and copies ran while one was open for 1% of the time, Pallas kernels for 6%

profile of v2, /device:TPU:32, one launch (start us, length us, event | category | flops | bytes accessed | tf_op | source)
XLA Modules:
  0.0 99.8 jit_solution(1308491699652369080)
XLA Ops:
  0.6 26.2 %all-gather = bf16[512,256]{1,0:T(8,128)(2,1)S(1)} all-gather(bf16[128,256]{1,0:T(8,128)(2,1)} %param.7), channel_id=2, replica_groups={{0,4,8,12},{1,5,9,13},{2,6,10,14},{3,7,11,15},{16,20,24,28},{17,21,25,2..., dimensions={0}, use_global_device_ids=true | all-gather | bytes 327680 | tf_op jit(solution)/shard_map/all_gather | solution.py:276
  26.8 0.0 copy-start.3
  26.8 0.0 copy-start.4
  26.8 0.0 copy-start
  26.8 0.0 copy-start.1
  26.8 1.1 %broadcast_in_dim.2 = bf16[4,4,128,256]{3,2,1,0:T(8,128)(2,1)} broadcast(bf16[4,128,256]{2,1,0:T(8,128)(2,1)S(1)} %bitcast.8), dimensions={1,2,3} | broadcast | bytes 1310720 | tf_op jit(solution)/shard_map/broadcast_in_dim | solution.py:45
  27.9 4.5 %all-to-all-start = ((bf16[4,4,128,256]{3,2,1,0:T(8,128)(2,1)}), bf16[4,4,128,256]{3,2,1,0:T(8,128)(2,1)S(1)}, u32[]{:S(2)}, u32[]{:S(2)}) async-start(bf16[4,4,128,256]{3,2,1,0:T(8,128)(2,1)} %broadcast_in_dim.2), calls=%async_computation | async-start | bytes 2097152 | tf_op jit(solution)/shard_map/all_to_all | solution.py:41
  32.4 0.0 copy-done.3
  32.4 0.0 copy-done.4
  32.4 1.9 %collective-permute-start = (f32[128,256]{1,0:T(8,128)S(1)}, f32[128,256]{1,0:T(8,128)S(1)}, u32[]{:S(2)}, u32[]{:S(2)}) collective-permute-start(f32[128,256]{1,0:T(8,128)S(1)} %convert_multiply_fusion.mixed_ref.refs_6_), channel_id=1, source_target_pairs={{0,16},{16,32},{32,48},{48,64},{64,80},{80,96},{96,112},{112,128},... | collective-permute-start | bytes 393224 | tf_op jit(solution)/shard_map/ppermute | solution.py:60
  34.3 4.4 %collective-permute-done.prev_ref.refs_5_ = f32[128,256]{1,0:T(8,128)S(1)} collective-permute-done((f32[128,256]{1,0:T(8,128)S(1)}, f32[128,256]{1,0:T(8,128)S(1)}, u32[]{:S(2)}, u32[]{:S(2)}) %collective-permute-start) | collective-permute-done | bytes 131104 | tf_op jit(solution)/shard_map/ppermute | solution.py:60
  38.7 0.0 copy-done
  38.7 0.0 copy-done.1
  38.7 3.4 %causal.1 = (f32[128,256]{1,0:T(8,128)}, bf16[2,128,128]{2,1,0:T(8,128)(2,1)}) custom-call(f32[128,256]{1,0:T(8,128)S(1)} %collective-permute-done.prev_ref.refs_5_, f32[128,256]{1,0:T(8,128)S(1)} %convert_multiply_fusion.mixed_ref.refs_6_, f32[256,128]{1,0:T(8,128)S(1)} %copy-done, f32[1,256]{1,0:T(1,128)S(1)} %bitcast.5, bf16[128,256]{1,0:T(8,128)(2,1)} %refs_3_.1), custom_call_target="tpu_custom_call" | custom-call | flops 8388608 | bytes 655360 | tf_op jit(solution)/shard_map/causal/pallas_call | solution.py:279
  42.1 2.9 %all-to-all-done.refs_0_ = bf16[4,4,128,256]{3,2,1,0:T(8,128)(2,1)S(1)} async-done(((bf16[4,4,128,256]{3,2,1,0:T(8,128)(2,1)}), bf16[4,4,128,256]{3,2,1,0:T(8,128)(2,1)S(1)}, u32[]{:S(2)}, u32[]{:S(2)}) %all-to-all-start) | async-done | bytes 1048608 | tf_op jit(solution)/shard_map/all_to_all | solution.py:41
  45.1 5.6 %main.1 = (bf16[128,256]{1,0:T(8,128)(2,1)}, f32[128,256]{1,0:T(8,128)S(1)}, f32[256,128]{1,0:T(8,128)S(1)}, bf16[8,6,128,128]{3,2,1,0:T(8,128)(2,1)}) custom-call(bf16[4,4,128,256]{3,2,1,0:T(8,128)(2,1)S(1)} %all-to-all-done.refs_0_, bf16[2,128,128]{2,1,0:T(8,128)(2,1)} %get-tuple-element.21.refs_1_, bf16[256,4096]{1,0:T(8,128)(2,1)} %refs_2_.1, ...), custom_call_target="tpu_custom_call" | custom-call | flops 276824064 | bytes 8388608 | tf_op jit(solution)/shard_map/main/pallas_call | solution.py:297
  50.7 4.3 %all-to-all-start.1 = ((bf16[8,6,128,128]{3,2,1,0:T(8,128)(2,1)}), bf16[8,6,128,128]{3,2,1,0:T(8,128)(2,1)S(1)}, u32[]{:S(2)}, u32[]{:S(2)}) async-start(bf16[8,6,128,128]{3,2,1,0:T(8,128)(2,1)} %get-tuple-element.30), calls=%async_computation.1 | async-start | bytes 3145728 | tf_op jit(solution)/shard_map/all_to_all | solution.py:41
  55.0 3.0 %collective-permute-start.2 = (f32[128,256]{1,0:T(8,128)S(1)}, f32[128,256]{1,0:T(8,128)S(1)}, u32[]{:S(2)}, u32[]{:S(2)}) collective-permute-start(f32[128,256]{1,0:T(8,128)S(1)} %get-tuple-element.25.grad_sum_ref), channel_id=1, source_target_pairs={{16,0},{32,16},{48,32},{64,48},{80,64},{96,80},{112,96},{128,112},... | collective-permute-start | bytes 393224 | tf_op jit(solution)/shard_map/ppermute | solution.py:60
  58.0 1.9 %collective-permute-start.1 = (f32[256,128]{1,0:T(8,128)S(1)}, f32[256,128]{1,0:T(8,128)S(1)}, u32[]{:S(2)}, u32[]{:S(2)}) collective-permute-start(f32[256,128]{1,0:T(8,128)S(1)} %get-tuple-element.24), channel_id=1, source_target_pairs={{0,16},{16,0},{32,48},{48,32},{64,80},{80,64},{96,112},{112,96},{1... | collective-permute-start | bytes 393224 | tf_op jit(solution)/shard_map/ppermute | solution.py:54
  59.9 0.6 collective-permute-done.2.incoming_ref
  60.5 3.0 %ahead.1 = (bf16[128,256]{1,0:T(8,128)(2,1)}, bf16[128,256]{1,0:T(8,128)(2,1)}) custom-call(f32[128,256]{1,0:T(8,128)S(1)} %get-tuple-element.25.grad_sum_ref, f32[128,256]{1,0:T(8,128)S(1)} %collective-permute-done.2.incoming_ref, f32[256,128]{1,0:T(8,128)S(1)} %copy-done, f32[1,256]{1,0:T(1,128)S(1)} %bitcast.6, bf16[128,256]{1,0:T(8,128)(2,1)} %key_ref.1, ...), custom_call_target="tpu_custom_call" | custom-call | flops 8388608 | bytes 655360 | tf_op jit(solution)/shard_map/ahead/pallas_call | solution.py:325
  63.4 0.0 collective-permute-done.1
  63.5 12.9 %all-gather.1 = bf16[1024,128]{1,0:T(8,128)(2,1)S(1)} all-gather(bf16[256,128]{1,0:T(8,128)(2,1)S(1)} %add_convert_fusion), channel_id=3, replica_groups={{0,32,64,96},{16,48,80,112},{128,160,192,224},{144,176,208,240},{256,28..., dimensions={0}, use_global_device_ids=true | all-gather | bytes 327680 | tf_op jit(solution)/shard_map/all_gather | solution.py:49
  76.4 0.1 all-to-all-done.1.pieces_ref
  76.6 1.1 %weight.1 = bf16[4,256,128]{2,1,0:T(8,128)(2,1)} custom-call(bf16[8,6,128,128]{3,2,1,0:T(8,128)(2,1)S(1)} %all-to-all-done.1.pieces_ref), custom_call_target="tpu_custom_call" | custom-call | flops 268435456 | bytes 2097152 | tf_op jit(solution)/shard_map/weight/pallas_call | solution.py:344
  77.7 5.1 %all-to-all-start.2 = ((bf16[4,256,128]{2,1,0:T(8,128)(2,1)}), bf16[4,256,128]{2,1,0:T(8,128)(2,1)S(1)}, u32[]{:S(2)}, u32[]{:S(2)}) async-start(bf16[4,256,128]{2,1,0:T(8,128)(2,1)} %weight.1), calls=%async_computation.2 | async-start | bytes 524288 | tf_op jit(solution)/shard_map/all_to_all | solution.py:41
  82.7 15.6 %all-gather.2 = f32[1024,128]{1,0:T(8,128)S(1)} all-gather(f32[256,128]{1,0:T(8,128)S(1)} %convert_reduce_fusion), channel_id=4, replica_groups={{0,128,256,384},{16,144,272,400},{32,160,288,416},{48,176,304,432},{64,..., dimensions={0}, use_global_device_ids=true | all-gather | bytes 655360 | tf_op jit(solution)/shard_map/all_gather | solution.py:49
  98.4 0.0 copy-start.2
  98.4 0.7 slice_reduce_fusion
  99.1 0.0 all-to-all-done.2
  99.1 0.7 broadcast_multiply_fusion
  99.8 0.0 copy-done.2
  (5 shorter events, 0.1 us)
Async XLA Ops:
  26.8 5.6 %copy-start.3 = (bf16[128,256]{1,0:T(8,128)(2,1)S(1)}, bf16[128,256]{1,0:T(8,128)(2,1)}, u32[]{:S(2)}) copy-start(bf16[128,256]{1,0:T(8,128)(2,1)} %value_ref.1) | copy-start | bytes 196612
  26.8 5.6 %copy-start.4 = (bf16[128,256]{1,0:T(8,128)(2,1)S(1)}, bf16[128,256]{1,0:T(8,128)(2,1)}, u32[]{:S(2)}) copy-start(bf16[128,256]{1,0:T(8,128)(2,1)} %key_ref.1) | copy-start | bytes 196612
  26.8 11.9 %copy-start = (f32[256,128]{1,0:T(8,128)S(1)}, f32[256,128]{1,0:T(8,128)}, u32[]{:S(2)}) copy-start(f32[256,128]{1,0:T(8,128)} %taps_ref.3) | copy-start | bytes 393220
  26.8 11.9 %copy-start.1 = (f32[256]{0:T(256)S(1)}, f32[256]{0:T(256)}, u32[]{:S(2)}) copy-start(f32[256]{0:T(256)} %param.12) | copy-start | bytes 3076
  27.9 17.1 %all-to-all-start = ((bf16[4,4,128,256]{3,2,1,0:T(8,128)(2,1)}), bf16[4,4,128,256]{3,2,1,0:T(8,128)(2,1)S(1)}, u32[]{:S(2)}, u32[]{:S(2)}) async-start(bf16[4,4,128,256]{3,2,1,0:T(8,128)(2,1)} %broadcast_in_dim.2), calls=%async_computation | async-start | bytes 2097152 | tf_op jit(solution)/shard_map/all_to_all | solution.py:41
  32.4 6.3 %collective-permute-start = (f32[128,256]{1,0:T(8,128)S(1)}, f32[128,256]{1,0:T(8,128)S(1)}, u32[]{:S(2)}, u32[]{:S(2)}) collective-permute-start(f32[128,256]{1,0:T(8,128)S(1)} %convert_multiply_fusion.mixed_ref.refs_6_), channel_id=1, source_target_pairs={{0,16},{16,32},{32,48},{48,64},{64,80},{80,96},{96,112},{112,128},... | collective-permute-start | bytes 393224 | tf_op jit(solution)/shard_map/ppermute | solution.py:60
  50.7 25.9 %all-to-all-start.1 = ((bf16[8,6,128,128]{3,2,1,0:T(8,128)(2,1)}), bf16[8,6,128,128]{3,2,1,0:T(8,128)(2,1)S(1)}, u32[]{:S(2)}, u32[]{:S(2)}) async-start(bf16[8,6,128,128]{3,2,1,0:T(8,128)(2,1)} %get-tuple-element.30), calls=%async_computation.1 | async-start | bytes 3145728 | tf_op jit(solution)/shard_map/all_to_all | solution.py:41
  55.0 5.5 %collective-permute-start.2 = (f32[128,256]{1,0:T(8,128)S(1)}, f32[128,256]{1,0:T(8,128)S(1)}, u32[]{:S(2)}, u32[]{:S(2)}) collective-permute-start(f32[128,256]{1,0:T(8,128)S(1)} %get-tuple-element.25.grad_sum_ref), channel_id=1, source_target_pairs={{16,0},{32,16},{48,32},{64,48},{80,64},{96,80},{112,96},{128,112},... | collective-permute-start | bytes 393224 | tf_op jit(solution)/shard_map/ppermute | solution.py:60
  58.0 5.5 %collective-permute-start.1 = (f32[256,128]{1,0:T(8,128)S(1)}, f32[256,128]{1,0:T(8,128)S(1)}, u32[]{:S(2)}, u32[]{:S(2)}) collective-permute-start(f32[256,128]{1,0:T(8,128)S(1)} %get-tuple-element.24), channel_id=1, source_target_pairs={{0,16},{16,0},{32,48},{48,32},{64,80},{80,64},{96,112},{112,96},{1... | collective-permute-start | bytes 393224 | tf_op jit(solution)/shard_map/ppermute | solution.py:54
  77.7 21.4 %all-to-all-start.2 = ((bf16[4,256,128]{2,1,0:T(8,128)(2,1)}), bf16[4,256,128]{2,1,0:T(8,128)(2,1)S(1)}, u32[]{:S(2)}, u32[]{:S(2)}) async-start(bf16[4,256,128]{2,1,0:T(8,128)(2,1)} %weight.1), calls=%async_computation.2 | async-start | bytes 524288 | tf_op jit(solution)/shard_map/all_to_all | solution.py:41
  98.4 1.4 %copy-start.2 = (f32[256,128]{1,0:T(8,128)}, f32[256,128]{1,0:T(8,128)S(1)}, u32[]{:S(2)}) copy-start(f32[256,128]{1,0:T(8,128)S(1)} %reduce_sum.28) | copy-start | bytes 393220

commit v3 on v2

--- a/solution.py
+++ b/solution.py
@@ -35,6 +35,9 @@
 X_GROUPS = [
     [seq_index(x, zl, core) for x in range(XS)] for zl in range(ZL) for core in range(CORES)
 ]
+CORE_GROUPS = [
+    [seq_index(x, zl, core) for core in range(CORES)] for x in range(XS) for zl in range(ZL)
+]
 
 
 def exchange(value, axis, groups):
@@ -49,9 +52,14 @@
     return lax.all_gather(value, "seq", axis=0, axis_index_groups=groups)
 
 
-def other_core(value):
-    size = lax.axis_size("seq")
-    return lax.ppermute(value, "seq", [(i, i ^ 1) for i in range(size)])
+def other_z(value, flip):
+    pairs = [
+        (seq_index(x, zl, core), seq_index(x, zl ^ flip, core))
+        for x in range(XS)
+        for zl in range(ZL)
+        for core in range(CORES)
+    ]
+    return lax.ppermute(value, "seq", pairs)
 
 
 def passed_along(value, axis, by):
@@ -75,6 +83,14 @@
         copy.wait()
 
 
+def weighted(shifted, tap_rows, starts, rows):
+    part = None
+    for tap, start in starts:
+        term = tap_rows[tap : tap + 1, :] * shifted[start : start + rows]
+        part = term if part is None else part + term
+    return part
+
+
 def causal_kernel(
     prev_ref,
     mixed_ref,
@@ -82,11 +98,12 @@
     gain_ref,
     query_ref,
     summed_ref,
-    out_ref,
+    packed_ref,
     pad,
+    tap_rows,
     query,
     summed,
-    out,
+    mixers,
     sem,
 ):
     copies = fetch((query_ref,), (query,), sem)
@@ -95,25 +112,39 @@
     pad[rows:] = mixed_ref[...]
     for lane in range(0, width, LANES):
         cols = pl.ds(lane, LANES)
-        tap_rows = taps_ref[cols, :].T
+        tap_rows[...] = taps_ref[cols, :].T
         total = gain_ref[:, cols] * mixed_ref[:, cols]
         for r in range(SUB):
             shifted = pad[pl.ds(SUB - r, 2 * rows - SUB), cols]
-            for q in range(TAPS // SUB):
-                start = rows - SUB - SUB * q
-                j = SUB * q + r
-                total = total + tap_rows[j : j + 1] * shifted[start : start + rows]
+            starts = [(SUB * q + r, rows - SUB - SUB * q) for q in range(TAPS // SUB)]
+            total = total + weighted(shifted, tap_rows, starts, rows)
         summed[:, cols] = total
         if lane == 0:
             finish(copies)
-        out[lane // LANES] = (query[:, cols].astype(F32) * total).T.astype(BF16)
-    finish(fetch((summed, out), (summed_ref, out_ref), sem, 1))
+        mixers[lane // LANES] = (query[:, cols].astype(F32) * total).T.astype(BF16)
+    targets, halves = packed_ref.shape[0], mixers.shape[0]
+    places = [packed_ref.at[target, pl.ds(YS, halves)] for target in range(targets)]
+    finish(fetch([summed] + [mixers] * targets, [summed_ref] + places, sem, 1))
+
+
+def pack_kernel(gathered_ref, begun_ref, packed_ref, sem):
+    del begun_ref
+    packs = []
+    for zh in range(ZH):
+        for core in range(CORES):
+            target = zh * CORES + core
+            for y in range(YS):
+                source = gathered_ref.at[y, zh, :, pl.ds(core * LANES, LANES)]
+                packs.append(
+                    pltpu.make_async_copy(source, packed_ref.at[target, y], sem.at[target, y])
+                )
+                packs[-1].start()
+    finish(packs)
 
 
 def main_kernel(
     norm_factor,
     gathered_ref,
-    mixer_ref,
     weight_ref,
     query_ref,
     summed_ref,
@@ -122,38 +153,23 @@
     grad_query_ref,
     grad_sum_ref,
     filter_ref,
-    packed_ref,
     held,
-    mixers,
     query,
     summed,
     pad,
     tap_rows,
     weight_sem,
-    pack_sem,
     sem,
 ):
     rows, width = mixed_ref.shape
-    blocks = fetch((mixer_ref, query_ref, summed_ref), (mixers, query, summed), sem)
     loads = []
     for zh in range(ZH):
         cols = pl.ds(zh * YS * width, YS * width)
         loads.append(pltpu.make_async_copy(weight_ref.at[:, cols], held.at[zh], weight_sem.at[zh]))
         loads[-1].start()
-    packs = []
-    for zh in range(ZH):
-        for core in range(CORES):
-            target = zh * CORES + core
-            for y in range(YS):
-                source = gathered_ref.at[y, zh, :, pl.ds(core * LANES, LANES)]
-                packs.append(
-                    pltpu.make_async_copy(source, packed_ref.at[target, y], pack_sem.at[target, y])
-                )
-            place = packed_ref.at[target, pl.ds(YS, mixers.shape[0])]
-            packs.append(pltpu.make_async_copy(mixers, place, pack_sem.at[target, YS]))
-    finish(blocks)
-    for copy in packs:
-        copy.start()
+    blocks = fetch((query_ref, summed_ref), (query, summed), sem)
+    pad[:rows] = prev_ref[...]
+    pad[rows:] = mixed_ref[...]
 
     total = None
     for zh in range(ZH):
@@ -166,11 +182,10 @@
                 preferred_element_type=F32,
             )
             total = term if total is None else total + term
+    finish(blocks)
     grad_query_ref[...] = (total * summed[...]).astype(BF16)
     grad_sum_ref[...] = total * query[...].astype(F32)
 
-    pad[:rows] = prev_ref[...]
-    pad[rows:] = mixed_ref[...]
     for lane in range(0, width, LANES):
         cols = pl.ds(lane, LANES)
         grad_sum = grad_sum_ref[:, cols]
@@ -183,7 +198,6 @@
                     grad_sum * shifted[start : start + rows], axis=0, keepdims=True
                 )
         filter_ref[cols, :] = tap_rows[...].T * norm_factor
-    finish(packs)
 
 
 def ahead_kernel(
@@ -196,6 +210,7 @@
     grad_key_ref,
     grad_value_ref,
     pad,
+    tap_rows,
     key,
     value,
     sem,
@@ -206,14 +221,12 @@
     pad[rows:] = incoming_ref[...]
     for lane in range(0, width, LANES):
         cols = pl.ds(lane, LANES)
-        tap_rows = taps_ref[cols, :].T
+        tap_rows[...] = taps_ref[cols, :].T
         total = gain_ref[:, cols] * grad_sum_ref[:, cols]
         for r in range(SUB):
             shifted = pad[pl.ds(r, 2 * rows - SUB), cols]
-            for q in range(TAPS // SUB):
-                start = SUB * q
-                j = SUB * q + r
-                total = total + tap_rows[j : j + 1] * shifted[start : start + rows]
+            starts = [(SUB * q + r, SUB * q) for q in range(TAPS // SUB)]
+            total = total + weighted(shifted, tap_rows, starts, rows)
         if lane == 0:
             finish(copies)
         grad_key_ref[:, cols] = (total * value[:, cols].astype(F32)).astype(BF16)
@@ -242,6 +255,19 @@
             out_ref[pair + k] = total[:, k * LANES : (k + 1) * LANES].astype(BF16)
 
 
+def finish_kernel(norm_factor, filters_ref, terms_ref, filter_ref, skip_ref, weight_ref):
+    for row in range(0, filter_ref.shape[0], LANES):
+        rows = pl.ds(row, LANES)
+        total = sum((filters_ref[at, rows] for at in range(1, XS)), filters_ref[0, rows])
+        filter_ref[rows, :] = total
+        skip_ref[:, rows] = total.T[:1]
+        total = sum(
+            (terms_ref[at, rows].astype(F32) for at in range(1, ZL)),
+            terms_ref[0, rows].astype(F32),
+        )
+        weight_ref[rows, :] = total * norm_factor
+
+
 def call(kernel, name, shapes, scratch, flops, moved, vmem=32, **specs):
     return pl.pallas_call(
         kernel,
@@ -262,6 +288,7 @@
     block_bf16 = jax.ShapeDtypeStruct((rows, width), BF16)
     padded = pltpu.VMEM((2 * rows, width), F32)
     held_f32, held_bf16 = pltpu.VMEM((rows, width), F32), pltpu.VMEM((rows, width), BF16)
+    held_rows = pltpu.VMEM((TAPS, LANES), F32)
     in_vmem = pl.BlockSpec(memory_space=pltpu.VMEM)
     in_hbm = pl.BlockSpec(memory_space=pltpu.HBM)
     stay = lambda value: pltpu.with_memory_space_constraint(value, pltpu.HBM)
@@ -276,58 +303,66 @@
     over_zh = lax.all_gather(grad_out, "chan", axis=0, axis_index_groups=ZH_GROUPS)
     gathered = spread(over_zh, "chan", Y_GROUPS, YS)
     gathered = gathered.reshape(YS, ZH, rows, width)
-    summed, mixer_out = call(
+    targets, blocks = ZH * CORES, YS + halves
+    packed_out = pltpu.HBM((targets, blocks, rows, LANES), BF16)
+    summed, packed = call(
         causal_kernel,
         "causal",
-        (pltpu.HBM((rows, width), F32), pltpu.HBM((halves, LANES, rows), BF16)),
+        (pltpu.HBM((rows, width), F32), packed_out),
         [
             padded,
+            held_rows,
             held_bf16,
             held_f32,
             held_mixers,
-            pltpu.SemaphoreType.DMA((3,)),
+            pltpu.SemaphoreType.DMA((2 + targets,)),
         ],
         2 * size * TAPS,
         20 * size,
         in_specs=[in_vmem, in_vmem, in_vmem, in_vmem, in_hbm],
         out_specs=[in_hbm, in_hbm],
     )(previous, mixed_in, filter_taps, gain, query)
-
-    targets, blocks = ZH * CORES, YS + halves
-    grad_query, grad_sum, filter_term, packed = call(
+    packed = call(
+        pack_kernel,
+        "pack",
+        packed_out,
+        [pltpu.SemaphoreType.DMA((targets, YS))],
+        0,
+        64 * size,
+        in_specs=[in_vmem, in_hbm],
+        out_specs=in_hbm,
+        input_output_aliases={1: 0},
+    )(gathered, stay(packed))
+    pieces = exchange(packed, "seq", XC_GROUPS)
+
+    grad_query, grad_sum, filter_term = call(
         lambda *refs: main_kernel(norm_factor, *refs),
         "main",
-        (
-            block_bf16,
-            block_f32,
-            jax.ShapeDtypeStruct((width, TAPS), F32),
-            pltpu.HBM((targets, blocks, rows, LANES), BF16),
-        ),
+        (block_bf16, block_f32, jax.ShapeDtypeStruct((width, TAPS), F32)),
         [
             pltpu.VMEM((ZH, width, YS * width), BF16),
-            held_mixers,
             held_bf16,
             held_f32,
             padded,
-            pltpu.VMEM((TAPS, LANES), F32),
+            held_rows,
             pltpu.SemaphoreType.DMA((ZH,)),
-            pltpu.SemaphoreType.DMA((targets, YS + 1)),
-            pltpu.SemaphoreType.DMA((3,)),
+            pltpu.SemaphoreType.DMA((2,)),
         ],
         2 * size * (4096 + TAPS),
-        8 * 1024 * 1024,
-        in_specs=[in_vmem, in_hbm, in_hbm, in_hbm, in_hbm, in_vmem, in_vmem],
-        out_specs=[in_vmem, in_vmem, in_vmem, in_hbm],
-    )(gathered, stay(mixer_out), weight, query, stay(summed), previous, mixed_in)
-    pieces = exchange(packed, "seq", XC_GROUPS)
+        4 * 1024 * 1024,
+        in_specs=[in_vmem, in_hbm, in_hbm, in_hbm, in_vmem, in_vmem],
+    )(gathered, weight, query, stay(summed), previous, mixed_in)
     incoming = passed_along(grad_sum, "seq", -1)
-    from_core = other_core(filter_term)
+    filter_term = jnp.sum(collect(filter_term, CORE_GROUPS), axis=0)
+    filter_term = (filter_term + other_z(filter_term, 1)).astype(BF16)
+    filter_term = filter_term.astype(F32) + other_z(filter_term, 2).astype(F32)
     grad_key, grad_value = call(
         ahead_kernel,
         "ahead",
         (block_bf16, block_bf16),
         [
             padded,
+            held_rows,
             held_bf16,
             held_bf16,
             pltpu.SemaphoreType.DMA((2,)),
@@ -336,11 +371,7 @@
         20 * size,
         in_specs=[in_vmem, in_vmem, in_vmem, in_vmem, in_hbm, in_hbm],
     )(grad_sum, incoming, filter_taps, gain, key, value)
-    from_core, grad_key, grad_value = lax.optimization_barrier((from_core, grad_key, grad_value))
-    filter_term = (filter_term + from_core).astype(BF16)
-    filter_term = jnp.sum(collect(filter_term, ZL_GROUPS).astype(F32), axis=0)
-
-    pieces, filter_term = lax.optimization_barrier((pieces, filter_term))
+    pieces, grad_key, grad_value = lax.optimization_barrier((pieces, grad_key, grad_value))
     partial = call(
         weight_kernel,
         "weight",
@@ -351,9 +382,19 @@
     )(pieces)
     partial, filter_term = lax.optimization_barrier((partial, filter_term))
     terms = exchange(partial, "seq", ZL_GROUPS)
-    grad_filter = jnp.sum(collect(filter_term, X_GROUPS), axis=0)
-    grad_skip = grad_filter[:, 0]
-    grad_weight = jnp.sum(terms.astype(F32), axis=0) * norm_factor
+    grad_filter, grad_skip, grad_weight = call(
+        lambda *refs: finish_kernel(norm_factor, *refs),
+        "finish",
+        (
+            jax.ShapeDtypeStruct((width, TAPS), F32),
+            jax.ShapeDtypeStruct((1, width), F32),
+            jax.ShapeDtypeStruct((width, LANES), F32),
+        ),
+        [],
+        8 * size,
+        32 * size,
+    )(collect(filter_term, X_GROUPS), terms)
+    grad_skip = grad_skip.reshape(width)
     return (grad_query, grad_key, grad_value, grad_filter, grad_skip, grad_weight)
 
 

time: 100 us -> 93.6 us (0.936)
  blocking collectives: 54.7 us -> 42.2 us
  starting transfers between devices: 20.7 us -> 24.6 us
  waiting for transfers between devices: 8.02 us -> 11.8 us
    all_gather x2, blocking collectives: 28.5 us -> 16 us  [collect(): return lax.all_gather(value, 'seq', axis=0, axis_index_groups=groups)]
    ppermute x1 -> x2, starting transfers between devices: 1.92 us -> 6.29 us  [other_z(): return lax.ppermute(value, 'seq', pairs)]
    ppermute x1 -> x2, waiting for transfers between devices: 0.01 us -> 3.61 us  [other_z(): return lax.ppermute(value, 'seq', pairs)]
    pallas_call x2 -> x4, Pallas kernels: 6.35 us -> 6.74 us  [the longest x1 2.5 us: body(): call(causal_kernel, 'causal', (pltpu.HBM((rows, width), F32), packed_out)...]
  transfers between devices with their start and end apart: 6 -> 7, of which waited for: 4 -> 4; matrix products, arithmetic and copies ran while one was open for 1% -> 0% of each run, Pallas kernels for 6% -> 10%
where the time goes in v3:
time: 93.6 us; the launch traced here: 93.1 us
  blocking collectives  42.2 us (45%)
  starting transfers between devices  24.6 us (26%)
  Pallas kernels  12.6 us (13%)
  waiting for transfers between devices  11.8 us (13%)
  local copies, waits for them, and re-layouts  1.11 us (1%)
    all_gather x1, blocking collectives, body(): lax.all_gather(grad_out, 'chan', axis=0, axis_index_groups=ZH_GROUPS)  26.2 us
    all_gather x2, blocking collectives, collect(): return lax.all_gather(value, 'seq', axis=0, axis_index_groups=groups)  16 us
    all_to_all x3, starting transfers between devices, exchange(): lax.all_to_all(value, axis, 0, 0, tiled=True, axis_index_groups=groups)  13.7 us
    ppermute x2, starting transfers between devices, other_z(): return lax.ppermute(value, 'seq', pairs)  6.29 us
    pallas_call x1, Pallas kernels, body(): call(lambda *refs: main_kernel(norm_factor, *refs), 'main', (block_bf16,...  4.74 us
    ppermute x2, starting transfers between devices, passed_along(): return lax.ppermute(value, axis, pairs)  4.54 us
    ppermute x2, waiting for transfers between devices, passed_along(): return lax.ppermute(value, axis, pairs)  4.36 us
    all_to_all x3, waiting for transfers between devices, exchange(): lax.all_to_all(value, axis, 0, 0, tiled=True, axis_index_groups=groups)  3.85 us
  transfers between devices with their start and end apart: 7, of which 4 were waited for; matrix products, arithmetic and copies ran while one was open for 0% of the time, Pallas kernels for 10%

profile of v3, /device:TPU:32, one launch (start us, length us, event | category | flops | bytes accessed | tf_op | source)
XLA Modules:
  0.0 93.1 jit_solution(17315790652513463293)
XLA Ops:
  0.6 26.2 %all-gather = bf16[512,256]{1,0:T(8,128)(2,1)S(1)} all-gather(bf16[128,256]{1,0:T(8,128)(2,1)} %param.7), channel_id=2, replica_groups={{0,4,8,12},{1,5,9,13},{2,6,10,14},{3,7,11,15},{16,20,24,28},{17,21,25,2..., dimensions={0}, use_global_device_ids=true | all-gather | bytes 327680 | tf_op jit(solution)/shard_map/all_gather | solution.py:303
  26.8 0.0 copy-start.2
  26.8 0.0 copy-start.3
  26.8 0.0 copy-start
  26.8 0.0 copy-start.1
  26.8 1.1 %broadcast_in_dim.2 = bf16[4,4,128,256]{3,2,1,0:T(8,128)(2,1)} broadcast(bf16[4,128,256]{2,1,0:T(8,128)(2,1)S(1)} %bitcast.8), dimensions={1,2,3} | broadcast | bytes 1310720 | tf_op jit(solution)/shard_map/broadcast_in_dim | solution.py:48
  27.9 4.5 %all-to-all-start = ((bf16[4,4,128,256]{3,2,1,0:T(8,128)(2,1)}), bf16[4,4,128,256]{3,2,1,0:T(8,128)(2,1)S(1)}, u32[]{:S(2)}, u32[]{:S(2)}) async-start(bf16[4,4,128,256]{3,2,1,0:T(8,128)(2,1)} %broadcast_in_dim.2), calls=%async_computation | async-start | bytes 2097152 | tf_op jit(solution)/shard_map/all_to_all | solution.py:44
  32.4 0.0 copy-done.2
  32.4 0.0 copy-done.3
  32.4 1.9 %collective-permute-start = (f32[128,256]{1,0:T(8,128)S(1)}, f32[128,256]{1,0:T(8,128)S(1)}, u32[]{:S(2)}, u32[]{:S(2)}) collective-permute-start(f32[128,256]{1,0:T(8,128)S(1)} %convert_multiply_fusion.mixed_ref.refs_5_), channel_id=1, source_target_pairs={{0,16},{16,32},{32,48},{48,64},{64,80},{80,96},{96,112},{112,128},... | collective-permute-start | bytes 393224 | tf_op jit(solution)/shard_map/ppermute | solution.py:68
  34.4 4.4 %collective-permute-done.prev_ref.refs_4_ = f32[128,256]{1,0:T(8,128)S(1)} collective-permute-done((f32[128,256]{1,0:T(8,128)S(1)}, f32[128,256]{1,0:T(8,128)S(1)}, u32[]{:S(2)}, u32[]{:S(2)}) %collective-permute-start) | collective-permute-done | bytes 131104 | tf_op jit(solution)/shard_map/ppermute | solution.py:68
  38.7 0.0 copy-done
  38.7 0.0 copy-done.1
  38.7 2.5 %causal.1 = (f32[128,256]{1,0:T(8,128)}, bf16[8,6,128,128]{3,2,1,0:T(8,128)(2,1)}) custom-call(f32[128,256]{1,0:T(8,128)S(1)} %collective-permute-done.prev_ref.refs_4_, f32[128,256]{1,0:T(8,128)S(1)} %convert_multiply_fusion.mixed_ref.refs_5_, f32[256,128]{1,0:T(8,128)S(1)} %copy-done, f32[1,256]{1,0:T(1,128)S(1)} %bitcast.6, bf16[128,256]{1,0:T(8,128)(2,1)} %refs_2_.1), custom_call_target="tpu_custom_call" | custom-call | flops 8388608 | bytes 655360 | tf_op jit(solution)/shard_map/causal/pallas_call | solution.py:308
  41.2 3.8 %all-to-all-done.refs_0_.gathered_ref = bf16[4,4,128,256]{3,2,1,0:T(8,128)(2,1)S(1)} async-done(((bf16[4,4,128,256]{3,2,1,0:T(8,128)(2,1)}), bf16[4,4,128,256]{3,2,1,0:T(8,128)(2,1)S(1)}, u32[]{:S(2)}, u32[]{:S(2)}) %all-to-all-start) | async-done | bytes 1048608 | tf_op jit(solution)/shard_map/all_to_all | solution.py:44
  45.1 1.3 %pack.1 = bf16[8,6,128,128]{3,2,1,0:T(8,128)(2,1)} custom-call(bf16[4,4,128,256]{3,2,1,0:T(8,128)(2,1)S(1)} %all-to-all-done.refs_0_.gathered_ref, bf16[8,6,128,128]{3,2,1,0:T(8,128)(2,1)} %get-tuple-element.23.begun_ref), custom_call_target="tpu_custom_call", output_to_operand_aliasing={{}: (1, {})} | custom-call | bytes 2097152 | tf_op jit(solution)/shard_map/pack/pallas_call | solution.py:325
  46.3 4.3 %all-to-all-start.1 = ((bf16[8,6,128,128]{3,2,1,0:T(8,128)(2,1)}), bf16[8,6,128,128]{3,2,1,0:T(8,128)(2,1)S(1)}, u32[]{:S(2)}, u32[]{:S(2)}) async-start(bf16[8,6,128,128]{3,2,1,0:T(8,128)(2,1)} %pack.1), calls=%async_computation.1 | async-start | bytes 3145728 | tf_op jit(solution)/shard_map/all_to_all | solution.py:44
  50.6 4.7 %main.1 = (bf16[128,256]{1,0:T(8,128)(2,1)}, f32[128,256]{1,0:T(8,128)S(1)}, f32[256,128]{1,0:T(8,128)S(1)}) custom-call(bf16[4,4,128,256]{3,2,1,0:T(8,128)(2,1)S(1)} %all-to-all-done.refs_0_.gathered_ref, bf16[256,4096]{1,0:T(8,128)(2,1)} %refs_1_.1, bf16[128,256]{1,0:T(8,128)(2,1)} %refs_2_.1, f32[128,256]{1,0:T(8,128)} %get-tuple-element.21.refs_3_, ...), custom_call_target="tpu_custom_call" | custom-call | flops 276824064 | bytes 4194304 | tf_op jit(solution)/shard_map/main/pallas_call | solution.py:338
  55.4 2.1 %all-gather.1 = f32[512,128]{1,0:T(8,128)S(1)} all-gather(f32[256,128]{1,0:T(8,128)S(1)} %get-tuple-element.30), channel_id=3, replica_groups={{0,16},{32,48},{64,80},{96,112},{128,144},{160,176},{192,208},{224,240}..., dimensions={0}, use_global_device_ids=true | all-gather | bytes 393216 | tf_op jit(solution)/shard_map/all_gather | solution.py:52
  57.6 2.9 %collective-permute-start.2 = (f32[256,128]{1,0:T(8,128)S(1)}, f32[256,128]{1,0:T(8,128)S(1)}, u32[]{:S(2)}, u32[]{:S(2)}) collective-permute-start(f32[256,128]{1,0:T(8,128)S(1)} %reduce_sum.9), channel_id=1, source_target_pairs={{0,32},{16,48},{32,0},{48,16},{64,96},{80,112},{96,64},{112,80},{1... | collective-permute-start | bytes 393224 | tf_op jit(solution)/shard_map/ppermute | solution.py:62
  60.5 2.6 %collective-permute-start.1 = (f32[128,256]{1,0:T(8,128)S(1)}, f32[128,256]{1,0:T(8,128)S(1)}, u32[]{:S(2)}, u32[]{:S(2)}) collective-permute-start(f32[128,256]{1,0:T(8,128)S(1)} %get-tuple-element.24.grad_sum_ref), channel_id=1, source_target_pairs={{16,0},{32,16},{48,32},{64,48},{80,64},{96,80},{112,96},{128,112},... | collective-permute-start | bytes 393224 | tf_op jit(solution)/shard_map/ppermute | solution.py:68
  63.1 2.1 %collective-permute-done.2 = f32[256,128]{1,0:T(8,128)S(1)} collective-permute-done((f32[256,128]{1,0:T(8,128)S(1)}, f32[256,128]{1,0:T(8,128)S(1)}, u32[]{:S(2)}, u32[]{:S(2)}) %collective-permute-start.2) | collective-permute-done | bytes 131104 | tf_op jit(solution)/shard_map/ppermute | solution.py:62
  65.2 3.4 %collective-permute-start.3 = (bf16[256,128]{1,0:T(8,128)(2,1)S(1)}, bf16[256,128]{1,0:T(8,128)(2,1)S(1)}, u32[]{:S(2)}, u32[]{:S(2)}) collective-permute-start(bf16[256,128]{1,0:T(8,128)(2,1)S(1)} %add_convert_fusion), channel_id=1, source_target_pairs={{0,64},{16,80},{32,96},{48,112},{64,0},{80,16},{96,32},{112,48},{1... | collective-permute-start | bytes 196616 | tf_op jit(solution)/shard_map/ppermute | solution.py:62
  68.6 0.0 collective-permute-done.1.incoming_ref
  68.6 2.3 %ahead.1 = (bf16[128,256]{1,0:T(8,128)(2,1)}, bf16[128,256]{1,0:T(8,128)(2,1)}) custom-call(f32[128,256]{1,0:T(8,128)S(1)} %get-tuple-element.24.grad_sum_ref, f32[128,256]{1,0:T(8,128)S(1)} %collective-permute-done.1.incoming_ref, f32[256,128]{1,0:T(8,128)S(1)} %copy-done, f32[1,256]{1,0:T(1,128)S(1)} %bitcast.7, bf16[128,256]{1,0:T(8,128)(2,1)} %key_ref.1, ...), custom_call_target="tpu_custom_call" | custom-call | flops 8388608 | bytes 655360 | tf_op jit(solution)/shard_map/ahead/pallas_call | solution.py:359
  70.9 1.5 %collective-permute-done.3 = bf16[256,128]{1,0:T(8,128)(2,1)S(1)} collective-permute-done((bf16[256,128]{1,0:T(8,128)(2,1)S(1)}, bf16[256,128]{1,0:T(8,128)(2,1)S(1)}, u32[]{:S(2)}, u32[]{:S(2)}) %collective-permute-start.3) | collective-permute-done | bytes 65568 | tf_op jit(solution)/shard_map/ppermute | solution.py:62
  72.4 0.0 all-to-all-done.1.pieces_ref
  72.4 1.1 %weight.1 = bf16[4,256,128]{2,1,0:T(8,128)(2,1)} custom-call(bf16[8,6,128,128]{3,2,1,0:T(8,128)(2,1)S(1)} %all-to-all-done.1.pieces_ref), custom_call_target="tpu_custom_call" | custom-call | flops 268435456 | bytes 2097152 | tf_op jit(solution)/shard_map/weight/pallas_call | solution.py:375
  73.6 5.0 %all-to-all-start.2 = ((bf16[4,256,128]{2,1,0:T(8,128)(2,1)}), bf16[4,256,128]{2,1,0:T(8,128)(2,1)S(1)}, u32[]{:S(2)}, u32[]{:S(2)}) async-start(bf16[4,256,128]{2,1,0:T(8,128)(2,1)} %weight.1), calls=%async_computation.2 | async-start | bytes 524288 | tf_op jit(solution)/shard_map/all_to_all | solution.py:44
  78.5 13.8 %all-gather.2 = f32[1024,128]{1,0:T(8,128)S(1)} all-gather(f32[256,128]{1,0:T(8,128)S(1)} %convert_add_fusion), channel_id=4, replica_groups={{0,128,256,384},{16,144,272,400},{32,160,288,416},{48,176,304,432},{64,..., dimensions={0}, use_global_device_ids=true | all-gather | bytes 655360 | tf_op jit(solution)/shard_map/all_gather | solution.py:52
  92.3 0.0 all-to-all-done.2.refs_1_
  92.3 0.7 finish.1
  (4 shorter events, 0.1 us)
Async XLA Ops:
  26.8 5.6 %copy-start.2 = (bf16[128,256]{1,0:T(8,128)(2,1)S(1)}, bf16[128,256]{1,0:T(8,128)(2,1)}, u32[]{:S(2)}) copy-start(bf16[128,256]{1,0:T(8,128)(2,1)} %value_ref.1) | copy-start | bytes 196612
  26.8 5.6 %copy-start.3 = (bf16[128,256]{1,0:T(8,128)(2,1)S(1)}, bf16[128,256]{1,0:T(8,128)(2,1)}, u32[]{:S(2)}) copy-start(bf16[128,256]{1,0:T(8,128)(2,1)} %key_ref.1) | copy-start | bytes 196612
  26.8 11.9 %copy-start = (f32[256,128]{1,0:T(8,128)S(1)}, f32[256,128]{1,0:T(8,128)}, u32[]{:S(2)}) copy-start(f32[256,128]{1,0:T(8,128)} %taps_ref.3) | copy-start | bytes 393220
  26.8 11.9 %copy-start.1 = (f32[256]{0:T(256)S(1)}, f32[256]{0:T(256)}, u32[]{:S(2)}) copy-start(f32[256]{0:T(256)} %param.12) | copy-start | bytes 3076
  27.9 17.1 %all-to-all-start = ((bf16[4,4,128,256]{3,2,1,0:T(8,128)(2,1)}), bf16[4,4,128,256]{3,2,1,0:T(8,128)(2,1)S(1)}, u32[]{:S(2)}, u32[]{:S(2)}) async-start(bf16[4,4,128,256]{3,2,1,0:T(8,128)(2,1)} %broadcast_in_dim.2), calls=%async_computation | async-start | bytes 2097152 | tf_op jit(solution)/shard_map/all_to_all | solution.py:44
  32.4 6.3 %collective-permute-start = (f32[128,256]{1,0:T(8,128)S(1)}, f32[128,256]{1,0:T(8,128)S(1)}, u32[]{:S(2)}, u32[]{:S(2)}) collective-permute-start(f32[128,256]{1,0:T(8,128)S(1)} %convert_multiply_fusion.mixed_ref.refs_5_), channel_id=1, source_target_pairs={{0,16},{16,32},{32,48},{48,64},{64,80},{80,96},{96,112},{112,128},... | collective-permute-start | bytes 393224 | tf_op jit(solution)/shard_map/ppermute | solution.py:68
  46.3 26.1 %all-to-all-start.1 = ((bf16[8,6,128,128]{3,2,1,0:T(8,128)(2,1)}), bf16[8,6,128,128]{3,2,1,0:T(8,128)(2,1)S(1)}, u32[]{:S(2)}, u32[]{:S(2)}) async-start(bf16[8,6,128,128]{3,2,1,0:T(8,128)(2,1)} %pack.1), calls=%async_computation.1 | async-start | bytes 3145728 | tf_op jit(solution)/shard_map/all_to_all | solution.py:44
  57.6 7.7 %collective-permute-start.2 = (f32[256,128]{1,0:T(8,128)S(1)}, f32[256,128]{1,0:T(8,128)S(1)}, u32[]{:S(2)}, u32[]{:S(2)}) collective-permute-start(f32[256,128]{1,0:T(8,128)S(1)} %reduce_sum.9), channel_id=1, source_target_pairs={{0,32},{16,48},{32,0},{48,16},{64,96},{80,112},{96,64},{112,80},{1... | collective-permute-start | bytes 393224 | tf_op jit(solution)/shard_map/ppermute | solution.py:62
  60.5 8.2 %collective-permute-start.1 = (f32[128,256]{1,0:T(8,128)S(1)}, f32[128,256]{1,0:T(8,128)S(1)}, u32[]{:S(2)}, u32[]{:S(2)}) collective-permute-start(f32[128,256]{1,0:T(8,128)S(1)} %get-tuple-element.24.grad_sum_ref), channel_id=1, source_target_pairs={{16,0},{32,16},{48,32},{64,48},{80,64},{96,80},{112,96},{128,112},... | collective-permute-start | bytes 393224 | tf_op jit(solution)/shard_map/ppermute | solution.py:68
  65.2 7.2 %collective-permute-start.3 = (bf16[256,128]{1,0:T(8,128)(2,1)S(1)}, bf16[256,128]{1,0:T(8,128)(2,1)S(1)}, u32[]{:S(2)}, u32[]{:S(2)}) collective-permute-start(bf16[256,128]{1,0:T(8,128)(2,1)S(1)} %add_convert_fusion), channel_id=1, source_target_pairs={{0,64},{16,80},{32,96},{48,112},{64,0},{80,16},{96,32},{112,48},{1... | collective-permute-start | bytes 196616 | tf_op jit(solution)/shard_map/ppermute | solution.py:62
  73.6 18.8 %all-to-all-start.2 = ((bf16[4,256,128]{2,1,0:T(8,128)(2,1)}), bf16[4,256,128]{2,1,0:T(8,128)(2,1)S(1)}, u32[]{:S(2)}, u32[]{:S(2)}) async-start(bf16[4,256,128]{2,1,0:T(8,128)(2,1)} %weight.1), calls=%async_computation.2 | async-start | bytes 524288 | tf_op jit(solution)/shard_map/all_to_all | solution.py:44

commit v4 on v3

--- a/solution.py
+++ b/solution.py
@@ -129,17 +129,10 @@
 
 def pack_kernel(gathered_ref, begun_ref, packed_ref, sem):
     del begun_ref
-    packs = []
-    for zh in range(ZH):
-        for core in range(CORES):
-            target = zh * CORES + core
-            for y in range(YS):
-                source = gathered_ref.at[y, zh, :, pl.ds(core * LANES, LANES)]
-                packs.append(
-                    pltpu.make_async_copy(source, packed_ref.at[target, y], sem.at[target, y])
-                )
-                packs[-1].start()
-    finish(packs)
+    targets = [(zh, core) for zh in range(ZH) for core in range(CORES)]
+    sources = [gathered_ref.at[:, zh, :, pl.ds(core * LANES, LANES)] for zh, core in targets]
+    places = [packed_ref.at[zh * CORES + core, pl.ds(0, YS)] for zh, core in targets]
+    finish(fetch(sources, places, sem))
 
 
 def main_kernel(
@@ -326,7 +319,7 @@
         pack_kernel,
         "pack",
         packed_out,
-        [pltpu.SemaphoreType.DMA((targets, YS))],
+        [pltpu.SemaphoreType.DMA((targets,))],
         0,
         64 * size,
         in_specs=[in_vmem, in_hbm],
@@ -355,7 +348,7 @@
     incoming = passed_along(grad_sum, "seq", -1)
     filter_term = jnp.sum(collect(filter_term, CORE_GROUPS), axis=0)
     filter_term = (filter_term + other_z(filter_term, 1)).astype(BF16)
-    filter_term = filter_term.astype(F32) + other_z(filter_term, 2).astype(F32)
+    from_z = other_z(filter_term, 2)
     grad_key, grad_value = call(
         ahead_kernel,
         "ahead",
@@ -381,6 +374,8 @@
         2 * 1024 * 1024,
     )(pieces)
     partial, filter_term = lax.optimization_barrier((partial, filter_term))
+    filter_term = filter_term.astype(F32) + from_z.astype(F32)
+    partial, filter_term = lax.optimization_barrier((partial, filter_term))
     terms = exchange(partial, "seq", ZL_GROUPS)
     grad_filter, grad_skip, grad_weight = call(
         lambda *refs: finish_kernel(norm_factor, *refs),

time: 93.6 us -> 92.1 us (0.984)
  the two profiles are of different devices: /device:TPU:32 before, /device:TPU:34 now
where the time goes in v4:
time: 92.1 us; the launch traced here: 91.5 us
  blocking collectives  41.1 us (45%)
  starting transfers between devices  25.4 us (28%)
  Pallas kernels  12.4 us (13%)
  waiting for transfers between devices  10.7 us (12%)
  local copies, waits for them, and re-layouts  1.11 us (1%)
    all_gather x1, blocking collectives, body(): lax.all_gather(grad_out, 'chan', axis=0, axis_index_groups=ZH_GROUPS)  26.2 us
    all_gather x2, blocking collectives, collect(): return lax.all_gather(value, 'seq', axis=0, axis_index_groups=groups)  14.9 us
    all_to_all x3, starting transfers between devices, exchange(): lax.all_to_all(value, axis, 0, 0, tiled=True, axis_index_groups=groups)  14.8 us
    ppermute x2, starting transfers between devices, other_z(): return lax.ppermute(value, 'seq', pairs)  6.27 us
    pallas_call x1, Pallas kernels, body(): call(lambda *refs: main_kernel(norm_factor, *refs), 'main', (block_bf16,...  4.74 us
    ppermute x2, waiting for transfers between devices, passed_along(): return lax.ppermute(value, axis, pairs)  4.36 us
    ppermute x2, starting transfers between devices, passed_along(): return lax.ppermute(value, axis, pairs)  4.34 us
    all_to_all x3, waiting for transfers between devices, exchange(): lax.all_to_all(value, axis, 0, 0, tiled=True, axis_index_groups=groups)  4.08 us
  transfers between devices with their start and end apart: 7, of which 5 were waited for; matrix products, arithmetic and copies ran while one was open for 0% of the time, Pallas kernels for 12%

profile of v4, /device:TPU:34, one launch (start us, length us, event | category | flops | bytes accessed | tf_op | source)
XLA Modules:
  0.0 91.5 jit_solution(10609269460381437903)
XLA Ops:
  0.6 26.2 %all-gather = bf16[512,256]{1,0:T(8,128)(2,1)S(1)} all-gather(bf16[128,256]{1,0:T(8,128)(2,1)} %param.7), channel_id=2, replica_groups={{0,4,8,12},{1,5,9,13},{2,6,10,14},{3,7,11,15},{16,20,24,28},{17,21,25,2..., dimensions={0}, use_global_device_ids=true | all-gather | bytes 327680 | tf_op jit(solution)/shard_map/all_gather | solution.py:296
  26.8 0.0 copy-start.2
  26.8 0.0 copy-start.3
  26.8 0.0 copy-start
  26.8 0.0 copy-start.1
  26.8 1.1 %broadcast_in_dim.2 = bf16[4,4,128,256]{3,2,1,0:T(8,128)(2,1)} broadcast(bf16[4,128,256]{2,1,0:T(8,128)(2,1)S(1)} %bitcast.8), dimensions={1,2,3} | broadcast | bytes 1310720 | tf_op jit(solution)/shard_map/broadcast_in_dim | solution.py:48
  27.9 4.5 %all-to-all-start = ((bf16[4,4,128,256]{3,2,1,0:T(8,128)(2,1)}), bf16[4,4,128,256]{3,2,1,0:T(8,128)(2,1)S(1)}, u32[]{:S(2)}, u32[]{:S(2)}) async-start(bf16[4,4,128,256]{3,2,1,0:T(8,128)(2,1)} %broadcast_in_dim.2), calls=%async_computation | async-start | bytes 2097152 | tf_op jit(solution)/shard_map/all_to_all | solution.py:44
  32.4 0.0 copy-done.2
  32.4 0.0 copy-done.3
  32.4 1.9 %collective-permute-start = (f32[128,256]{1,0:T(8,128)S(1)}, f32[128,256]{1,0:T(8,128)S(1)}, u32[]{:S(2)}, u32[]{:S(2)}) collective-permute-start(f32[128,256]{1,0:T(8,128)S(1)} %convert_multiply_fusion.mixed_ref.refs_5_), channel_id=1, source_target_pairs={{0,16},{16,32},{32,48},{48,64},{64,80},{80,96},{96,112},{112,128},... | collective-permute-start | bytes 393224 | tf_op jit(solution)/shard_map/ppermute | solution.py:68
  34.4 4.4 %collective-permute-done.prev_ref.refs_4_ = f32[128,256]{1,0:T(8,128)S(1)} collective-permute-done((f32[128,256]{1,0:T(8,128)S(1)}, f32[128,256]{1,0:T(8,128)S(1)}, u32[]{:S(2)}, u32[]{:S(2)}) %collective-permute-start) | collective-permute-done | bytes 131104 | tf_op jit(solution)/shard_map/ppermute | solution.py:68
  38.7 0.0 copy-done
  38.7 0.0 copy-done.1
  38.7 2.5 %causal.1 = (f32[128,256]{1,0:T(8,128)}, bf16[8,6,128,128]{3,2,1,0:T(8,128)(2,1)}) custom-call(f32[128,256]{1,0:T(8,128)S(1)} %collective-permute-done.prev_ref.refs_4_, f32[128,256]{1,0:T(8,128)S(1)} %convert_multiply_fusion.mixed_ref.refs_5_, f32[256,128]{1,0:T(8,128)S(1)} %copy-done, f32[1,256]{1,0:T(1,128)S(1)} %bitcast.6, bf16[128,256]{1,0:T(8,128)(2,1)} %refs_2_.1), custom_call_target="tpu_custom_call" | custom-call | flops 8388608 | bytes 655360 | tf_op jit(solution)/shard_map/causal/pallas_call | solution.py:301
  41.2 3.8 %all-to-all-done.refs_0_.gathered_ref = bf16[4,4,128,256]{3,2,1,0:T(8,128)(2,1)S(1)} async-done(((bf16[4,4,128,256]{3,2,1,0:T(8,128)(2,1)}), bf16[4,4,128,256]{3,2,1,0:T(8,128)(2,1)S(1)}, u32[]{:S(2)}, u32[]{:S(2)}) %all-to-all-start) | async-done | bytes 1048608 | tf_op jit(solution)/shard_map/all_to_all | solution.py:44
  45.1 1.0 %pack.1 = bf16[8,6,128,128]{3,2,1,0:T(8,128)(2,1)} custom-call(bf16[4,4,128,256]{3,2,1,0:T(8,128)(2,1)S(1)} %all-to-all-done.refs_0_.gathered_ref, bf16[8,6,128,128]{3,2,1,0:T(8,128)(2,1)} %get-tuple-element.25.begun_ref), custom_call_target="tpu_custom_call", output_to_operand_aliasing={{}: (1, {})} | custom-call | bytes 2097152 | tf_op jit(solution)/shard_map/pack/pallas_call | solution.py:318
  46.1 4.8 %all-to-all-start.1 = ((bf16[8,6,128,128]{3,2,1,0:T(8,128)(2,1)}), bf16[8,6,128,128]{3,2,1,0:T(8,128)(2,1)S(1)}, u32[]{:S(2)}, u32[]{:S(2)}) async-start(bf16[8,6,128,128]{3,2,1,0:T(8,128)(2,1)} %pack.1), calls=%async_computation.1 | async-start | bytes 3145728 | tf_op jit(solution)/shard_map/all_to_all | solution.py:44
  51.0 4.7 %main.1 = (bf16[128,256]{1,0:T(8,128)(2,1)}, f32[128,256]{1,0:T(8,128)S(1)}, f32[256,128]{1,0:T(8,128)S(1)}) custom-call(bf16[4,4,128,256]{3,2,1,0:T(8,128)(2,1)S(1)} %all-to-all-done.refs_0_.gathered_ref, bf16[256,4096]{1,0:T(8,128)(2,1)} %refs_1_.1, bf16[128,256]{1,0:T(8,128)(2,1)} %refs_2_.1, f32[128,256]{1,0:T(8,128)} %get-tuple-element.23.refs_3_, ...), custom_call_target="tpu_custom_call" | custom-call | flops 276824064 | bytes 4194304 | tf_op jit(solution)/shard_map/main/pallas_call | solution.py:331
  55.7 2.0 %all-gather.1 = f32[512,128]{1,0:T(8,128)S(1)} all-gather(f32[256,128]{1,0:T(8,128)S(1)} %get-tuple-element.32), channel_id=3, replica_groups={{0,16},{32,48},{64,80},{96,112},{128,144},{160,176},{192,208},{224,240}..., dimensions={0}, use_global_device_ids=true | all-gather | bytes 393216 | tf_op jit(solution)/shard_map/all_gather | solution.py:52
  57.7 2.9 %collective-permute-start.2 = (f32[256,128]{1,0:T(8,128)S(1)}, f32[256,128]{1,0:T(8,128)S(1)}, u32[]{:S(2)}, u32[]{:S(2)}) collective-permute-start(f32[256,128]{1,0:T(8,128)S(1)} %reduce_sum.9), channel_id=1, source_target_pairs={{0,32},{16,48},{32,0},{48,16},{64,96},{80,112},{96,64},{112,80},{1... | collective-permute-start | bytes 393224 | tf_op jit(solution)/shard_map/ppermute | solution.py:62
  60.6 2.4 %collective-permute-start.1 = (f32[128,256]{1,0:T(8,128)S(1)}, f32[128,256]{1,0:T(8,128)S(1)}, u32[]{:S(2)}, u32[]{:S(2)}) collective-permute-start(f32[128,256]{1,0:T(8,128)S(1)} %get-tuple-element.26.grad_sum_ref), channel_id=1, source_target_pairs={{16,0},{32,16},{48,32},{64,48},{80,64},{96,80},{112,96},{128,112},... | collective-permute-start | bytes 393224 | tf_op jit(solution)/shard_map/ppermute | solution.py:68
  63.1 2.1 %collective-permute-done.2 = f32[256,128]{1,0:T(8,128)S(1)} collective-permute-done((f32[256,128]{1,0:T(8,128)S(1)}, f32[256,128]{1,0:T(8,128)S(1)}, u32[]{:S(2)}, u32[]{:S(2)}) %collective-permute-start.2) | collective-permute-done | bytes 131104 | tf_op jit(solution)/shard_map/ppermute | solution.py:62
  65.2 3.4 %collective-permute-start.3 = (bf16[256,128]{1,0:T(8,128)(2,1)S(1)}, bf16[256,128]{1,0:T(8,128)(2,1)S(1)}, u32[]{:S(2)}, u32[]{:S(2)}) collective-permute-start(bf16[256,128]{1,0:T(8,128)(2,1)S(1)} %add_convert_fusion), channel_id=1, source_target_pairs={{0,64},{16,80},{32,96},{48,112},{64,0},{80,16},{96,32},{112,48},{1... | collective-permute-start | bytes 196616 | tf_op jit(solution)/shard_map/ppermute | solution.py:62
  68.6 0.0 collective-permute-done.1.incoming_ref
  68.6 2.3 %ahead.1 = (bf16[128,256]{1,0:T(8,128)(2,1)}, bf16[128,256]{1,0:T(8,128)(2,1)}) custom-call(f32[128,256]{1,0:T(8,128)S(1)} %get-tuple-element.26.grad_sum_ref, f32[128,256]{1,0:T(8,128)S(1)} %collective-permute-done.1.incoming_ref, f32[256,128]{1,0:T(8,128)S(1)} %copy-done, f32[1,256]{1,0:T(1,128)S(1)} %bitcast.7, bf16[128,256]{1,0:T(8,128)(2,1)} %key_ref.1, ...), custom_call_target="tpu_custom_call" | custom-call | flops 8388608 | bytes 655360 | tf_op jit(solution)/shard_map/ahead/pallas_call | solution.py:352
  70.9 0.2 all-to-all-done.1.pieces_ref
  71.1 1.1 %weight.1 = bf16[4,256,128]{2,1,0:T(8,128)(2,1)} custom-call(bf16[8,6,128,128]{3,2,1,0:T(8,128)(2,1)S(1)} %all-to-all-done.1.pieces_ref), custom_call_target="tpu_custom_call" | custom-call | flops 268435456 | bytes 2097152 | tf_op jit(solution)/shard_map/weight/pallas_call | solution.py:368
  72.2 0.1 collective-permute-done.3
  72.4 5.5 %all-to-all-start.2 = ((bf16[4,256,128]{2,1,0:T(8,128)(2,1)}), bf16[4,256,128]{2,1,0:T(8,128)(2,1)S(1)}, u32[]{:S(2)}, u32[]{:S(2)}) async-start(bf16[4,256,128]{2,1,0:T(8,128)(2,1)} %weight.1), calls=%async_computation.2 | async-start | bytes 524288 | tf_op jit(solution)/shard_map/all_to_all | solution.py:44
  77.9 12.9 %all-gather.2 = f32[1024,128]{1,0:T(8,128)S(1)} all-gather(f32[256,128]{1,0:T(8,128)S(1)} %convert_add_fusion), channel_id=4, replica_groups={{0,128,256,384},{16,144,272,400},{32,160,288,416},{48,176,304,432},{64,..., dimensions={0}, use_global_device_ids=true | all-gather | bytes 655360 | tf_op jit(solution)/shard_map/all_gather | solution.py:52
  90.8 0.0 all-to-all-done.2.refs_1_
  90.8 0.7 finish.1
  (4 shorter events, 0.1 us)
Async XLA Ops:
  26.8 5.6 %copy-start.2 = (bf16[128,256]{1,0:T(8,128)(2,1)S(1)}, bf16[128,256]{1,0:T(8,128)(2,1)}, u32[]{:S(2)}) copy-start(bf16[128,256]{1,0:T(8,128)(2,1)} %value_ref.1) | copy-start | bytes 196612
  26.8 5.6 %copy-start.3 = (bf16[128,256]{1,0:T(8,128)(2,1)S(1)}, bf16[128,256]{1,0:T(8,128)(2,1)}, u32[]{:S(2)}) copy-start(bf16[128,256]{1,0:T(8,128)(2,1)} %key_ref.1) | copy-start | bytes 196612
  26.8 11.9 %copy-start = (f32[256,128]{1,0:T(8,128)S(1)}, f32[256,128]{1,0:T(8,128)}, u32[]{:S(2)}) copy-start(f32[256,128]{1,0:T(8,128)} %taps_ref.3) | copy-start | bytes 393220
  26.8 11.9 %copy-start.1 = (f32[256]{0:T(256)S(1)}, f32[256]{0:T(256)}, u32[]{:S(2)}) copy-start(f32[256]{0:T(256)} %param.12) | copy-start | bytes 3076
  27.9 17.1 %all-to-all-start = ((bf16[4,4,128,256]{3,2,1,0:T(8,128)(2,1)}), bf16[4,4,128,256]{3,2,1,0:T(8,128)(2,1)S(1)}, u32[]{:S(2)}, u32[]{:S(2)}) async-start(bf16[4,4,128,256]{3,2,1,0:T(8,128)(2,1)} %broadcast_in_dim.2), calls=%async_computation | async-start | bytes 2097152 | tf_op jit(solution)/shard_map/all_to_all | solution.py:44
  32.4 6.3 %collective-permute-start = (f32[128,256]{1,0:T(8,128)S(1)}, f32[128,256]{1,0:T(8,128)S(1)}, u32[]{:S(2)}, u32[]{:S(2)}) collective-permute-start(f32[128,256]{1,0:T(8,128)S(1)} %convert_multiply_fusion.mixed_ref.refs_5_), channel_id=1, source_target_pairs={{0,16},{16,32},{32,48},{48,64},{64,80},{80,96},{96,112},{112,128},... | collective-permute-start | bytes 393224 | tf_op jit(solution)/shard_map/ppermute | solution.py:68
  46.1 25.0 %all-to-all-start.1 = ((bf16[8,6,128,128]{3,2,1,0:T(8,128)(2,1)}), bf16[8,6,128,128]{3,2,1,0:T(8,128)(2,1)S(1)}, u32[]{:S(2)}, u32[]{:S(2)}) async-start(bf16[8,6,128,128]{3,2,1,0:T(8,128)(2,1)} %pack.1), calls=%async_computation.1 | async-start | bytes 3145728 | tf_op jit(solution)/shard_map/all_to_all | solution.py:44
  57.7 7.4 %collective-permute-start.2 = (f32[256,128]{1,0:T(8,128)S(1)}, f32[256,128]{1,0:T(8,128)S(1)}, u32[]{:S(2)}, u32[]{:S(2)}) collective-permute-start(f32[256,128]{1,0:T(8,128)S(1)} %reduce_sum.9), channel_id=1, source_target_pairs={{0,32},{16,48},{32,0},{48,16},{64,96},{80,112},{96,64},{112,80},{1... | collective-permute-start | bytes 393224 | tf_op jit(solution)/shard_map/ppermute | solution.py:62
  60.6 8.0 %collective-permute-start.1 = (f32[128,256]{1,0:T(8,128)S(1)}, f32[128,256]{1,0:T(8,128)S(1)}, u32[]{:S(2)}, u32[]{:S(2)}) collective-permute-start(f32[128,256]{1,0:T(8,128)S(1)} %get-tuple-element.26.grad_sum_ref), channel_id=1, source_target_pairs={{16,0},{32,16},{48,32},{64,48},{80,64},{96,80},{112,96},{128,112},... | collective-permute-start | bytes 393224 | tf_op jit(solution)/shard_map/ppermute | solution.py:68
  65.2 7.2 %collective-permute-start.3 = (bf16[256,128]{1,0:T(8,128)(2,1)S(1)}, bf16[256,128]{1,0:T(8,128)(2,1)S(1)}, u32[]{:S(2)}, u32[]{:S(2)}) collective-permute-start(bf16[256,128]{1,0:T(8,128)(2,1)S(1)} %add_convert_fusion), channel_id=1, source_target_pairs={{0,64},{16,80},{32,96},{48,112},{64,0},{80,16},{96,32},{112,48},{1... | collective-permute-start | bytes 196616 | tf_op jit(solution)/shard_map/ppermute | solution.py:62
  72.4 18.4 %all-to-all-start.2 = ((bf16[4,256,128]{2,1,0:T(8,128)(2,1)}), bf16[4,256,128]{2,1,0:T(8,128)(2,1)S(1)}, u32[]{:S(2)}, u32[]{:S(2)}) async-start(bf16[4,256,128]{2,1,0:T(8,128)(2,1)} %weight.1), calls=%async_computation.2 | async-start | bytes 524288 | tf_op jit(solution)/shard_map/all_to_all | solution.py:44

commit v5 on v4

--- a/solution.py
+++ b/solution.py
@@ -32,8 +32,11 @@
 ZL_GROUPS = [
     [seq_index(x, zl, core) for zl in range(ZL)] for x in range(XS) for core in range(CORES)
 ]
-X_GROUPS = [
-    [seq_index(x, zl, core) for x in range(XS)] for zl in range(ZL) for core in range(CORES)
+X_PAIRS = [
+    [seq_index(x + half, zl, core) for half in (0, XS // 2)]
+    for x in range(XS // 2)
+    for zl in range(ZL)
+    for core in range(CORES)
 ]
 CORE_GROUPS = [
     [seq_index(x, zl, core) for core in range(CORES)] for x in range(XS) for zl in range(ZL)
@@ -52,9 +55,9 @@
     return lax.all_gather(value, "seq", axis=0, axis_index_groups=groups)
 
 
-def other_z(value, flip):
+def swapped(value, flip_x, flip_z):
     pairs = [
-        (seq_index(x, zl, core), seq_index(x, zl ^ flip, core))
+        (seq_index(x, zl, core), seq_index(x ^ flip_x, zl ^ flip_z, core))
         for x in range(XS)
         for zl in range(ZL)
         for core in range(CORES)
@@ -248,17 +251,12 @@
             out_ref[pair + k] = total[:, k * LANES : (k + 1) * LANES].astype(BF16)
 
 
-def finish_kernel(norm_factor, filters_ref, terms_ref, filter_ref, skip_ref, weight_ref):
+def filter_kernel(both_ref, filter_ref, skip_ref):
     for row in range(0, filter_ref.shape[0], LANES):
         rows = pl.ds(row, LANES)
-        total = sum((filters_ref[at, rows] for at in range(1, XS)), filters_ref[0, rows])
+        total = both_ref[0, rows] + both_ref[1, rows]
         filter_ref[rows, :] = total
         skip_ref[:, rows] = total.T[:1]
-        total = sum(
-            (terms_ref[at, rows].astype(F32) for at in range(1, ZL)),
-            terms_ref[0, rows].astype(F32),
-        )
-        weight_ref[rows, :] = total * norm_factor
 
 
 def call(kernel, name, shapes, scratch, flops, moved, vmem=32, **specs):
@@ -347,8 +345,8 @@
     )(gathered, weight, query, stay(summed), previous, mixed_in)
     incoming = passed_along(grad_sum, "seq", -1)
     filter_term = jnp.sum(collect(filter_term, CORE_GROUPS), axis=0)
-    filter_term = (filter_term + other_z(filter_term, 1)).astype(BF16)
-    from_z = other_z(filter_term, 2)
+    filter_term = (filter_term + swapped(filter_term, 0, 1)).astype(BF16)
+    from_z = swapped(filter_term, 0, 2)
     grad_key, grad_value = call(
         ahead_kernel,
         "ahead",
@@ -376,20 +374,19 @@
     partial, filter_term = lax.optimization_barrier((partial, filter_term))
     filter_term = filter_term.astype(F32) + from_z.astype(F32)
     partial, filter_term = lax.optimization_barrier((partial, filter_term))
+    from_x = swapped(filter_term, 1, 0)
     terms = exchange(partial, "seq", ZL_GROUPS)
-    grad_filter, grad_skip, grad_weight = call(
-        lambda *refs: finish_kernel(norm_factor, *refs),
-        "finish",
-        (
-            jax.ShapeDtypeStruct((width, TAPS), F32),
-            jax.ShapeDtypeStruct((1, width), F32),
-            jax.ShapeDtypeStruct((width, LANES), F32),
-        ),
+    grad_filter, grad_skip = call(
+        filter_kernel,
+        "filter",
+        (jax.ShapeDtypeStruct((width, TAPS), F32), jax.ShapeDtypeStruct((1, width), F32)),
         [],
-        8 * size,
-        32 * size,
-    )(collect(filter_term, X_GROUPS), terms)
+        1 << 36,
+        1 << 28,
+    )(collect(filter_term + from_x, X_PAIRS))
+    terms, grad_filter, grad_skip = lax.optimization_barrier((terms, grad_filter, grad_skip))
     grad_skip = grad_skip.reshape(width)
+    grad_weight = jnp.sum(terms.astype(F32), axis=0) * norm_factor
     return (grad_query, grad_key, grad_value, grad_filter, grad_skip, grad_weight)
 
 

time: 92.1 us -> 90.9 us (0.987)
  the two profiles are of different devices: /device:TPU:34 before, /device:TPU:1 now
where the time goes in v5:
time: 90.9 us; the launch traced here: 90.3 us
  starting transfers between devices  34.4 us (38%)
  blocking collectives  33.9 us (37%)
  Pallas kernels  12.4 us (14%)
  waiting for transfers between devices  7.03 us (8%)
  local copies, waits for them, and re-layouts  1.1 us (1%)
    all_gather x1, blocking collectives, body(): lax.all_gather(grad_out, 'chan', axis=0, axis_index_groups=ZH_GROUPS)  25.5 us
    all_to_all x3, starting transfers between devices, exchange(): lax.all_to_all(value, axis, 0, 0, tiled=True, axis_index_groups=groups)  18.1 us
    all_gather x2, blocking collectives, collect(): return lax.all_gather(value, 'seq', axis=0, axis_index_groups=groups)  8.41 us
    ppermute x2, starting transfers between devices, passed_along(): return lax.ppermute(value, axis, pairs)  8.29 us
    ppermute x3, starting transfers between devices, swapped(): return lax.ppermute(value, 'seq', pairs)  7.93 us
    pallas_call x1, Pallas kernels, body(): call(lambda *refs: main_kernel(norm_factor, *refs), 'main', (block_bf16,...  4.81 us
    all_to_all x3, waiting for transfers between devices, exchange(): lax.all_to_all(value, axis, 0, 0, tiled=True, axis_index_groups=groups)  3.29 us
    pallas_call x1, Pallas kernels, body(): call(causal_kernel, 'causal', (pltpu.HBM((rows, width), F32), packed_out)...  2.5 us
  transfers between devices with their start and end apart: 8, of which 5 were waited for; matrix products, arithmetic and copies ran while one was open for 0% of the time, Pallas kernels for 13%

profile of v5, /device:TPU:1, one launch (start us, length us, event | category | flops | bytes accessed | tf_op | source)
XLA Modules:
  0.0 90.3 jit_solution(3489452553500169144)
XLA Ops:
  0.6 25.5 %all-gather = bf16[512,256]{1,0:T(8,128)(2,1)S(1)} all-gather(bf16[128,256]{1,0:T(8,128)(2,1)} %param.7), channel_id=2, replica_groups={{0,4,8,12},{1,5,9,13},{2,6,10,14},{3,7,11,15},{16,20,24,28},{17,21,25,2..., dimensions={0}, use_global_device_ids=true | all-gather | bytes 327680 | tf_op jit(solution)/shard_map/all_gather | solution.py:294
  26.1 0.0 copy-start.2
  26.1 0.0 copy-start.3
  26.1 0.0 copy-start
  26.1 0.0 copy-start.1
  26.1 1.1 %broadcast_in_dim.2 = bf16[4,4,128,256]{3,2,1,0:T(8,128)(2,1)} broadcast(bf16[4,128,256]{2,1,0:T(8,128)(2,1)S(1)} %bitcast.8), dimensions={1,2,3} | broadcast | bytes 1310720 | tf_op jit(solution)/shard_map/broadcast_in_dim | solution.py:51
  27.2 4.2 %all-to-all-start = ((bf16[4,4,128,256]{3,2,1,0:T(8,128)(2,1)}), bf16[4,4,128,256]{3,2,1,0:T(8,128)(2,1)S(1)}, u32[]{:S(2)}, u32[]{:S(2)}) async-start(bf16[4,4,128,256]{3,2,1,0:T(8,128)(2,1)} %broadcast_in_dim.2), calls=%async_computation | async-start | bytes 2097152 | tf_op jit(solution)/shard_map/all_to_all | solution.py:47
  31.4 0.0 copy-done.2
  31.4 0.0 copy-done.3
  31.4 5.9 %collective-permute-start = (f32[128,256]{1,0:T(8,128)S(1)}, f32[128,256]{1,0:T(8,128)S(1)}, u32[]{:S(2)}, u32[]{:S(2)}) collective-permute-start(f32[128,256]{1,0:T(8,128)S(1)} %convert_multiply_fusion.mixed_ref.refs_5_), channel_id=1, source_target_pairs={{0,16},{16,32},{32,48},{48,64},{64,80},{80,96},{96,112},{112,128},... | collective-permute-start | bytes 393224 | tf_op jit(solution)/shard_map/ppermute | solution.py:71
  37.4 1.9 %collective-permute-done.prev_ref.refs_4_ = f32[128,256]{1,0:T(8,128)S(1)} collective-permute-done((f32[128,256]{1,0:T(8,128)S(1)}, f32[128,256]{1,0:T(8,128)S(1)}, u32[]{:S(2)}, u32[]{:S(2)}) %collective-permute-start) | collective-permute-done | bytes 131104 | tf_op jit(solution)/shard_map/ppermute | solution.py:71
  39.3 0.0 copy-done
  39.3 0.0 copy-done.1
  39.3 2.5 %causal.1 = (f32[128,256]{1,0:T(8,128)}, bf16[8,6,128,128]{3,2,1,0:T(8,128)(2,1)}) custom-call(f32[128,256]{1,0:T(8,128)S(1)} %collective-permute-done.prev_ref.refs_4_, f32[128,256]{1,0:T(8,128)S(1)} %convert_multiply_fusion.mixed_ref.refs_5_, f32[256,128]{1,0:T(8,128)S(1)} %copy-done, f32[1,256]{1,0:T(1,128)S(1)} %bitcast.6, bf16[128,256]{1,0:T(8,128)(2,1)} %refs_2_.1), custom_call_target="tpu_custom_call" | custom-call | flops 8388608 | bytes 655360 | tf_op jit(solution)/shard_map/causal/pallas_call | solution.py:299
  41.8 1.0 %all-to-all-done.refs_0_.gathered_ref = bf16[4,4,128,256]{3,2,1,0:T(8,128)(2,1)S(1)} async-done(((bf16[4,4,128,256]{3,2,1,0:T(8,128)(2,1)}), bf16[4,4,128,256]{3,2,1,0:T(8,128)(2,1)S(1)}, u32[]{:S(2)}, u32[]{:S(2)}) %all-to-all-start) | async-done | bytes 1048608 | tf_op jit(solution)/shard_map/all_to_all | solution.py:47
  42.8 1.1 %pack.1 = bf16[8,6,128,128]{3,2,1,0:T(8,128)(2,1)} custom-call(bf16[4,4,128,256]{3,2,1,0:T(8,128)(2,1)S(1)} %all-to-all-done.refs_0_.gathered_ref, bf16[8,6,128,128]{3,2,1,0:T(8,128)(2,1)} %get-tuple-element.27.begun_ref), custom_call_target="tpu_custom_call", output_to_operand_aliasing={{}: (1, {})} | custom-call | bytes 2097152 | tf_op jit(solution)/shard_map/pack/pallas_call | solution.py:316
  43.9 8.9 %all-to-all-start.1 = ((bf16[8,6,128,128]{3,2,1,0:T(8,128)(2,1)}), bf16[8,6,128,128]{3,2,1,0:T(8,128)(2,1)S(1)}, u32[]{:S(2)}, u32[]{:S(2)}) async-start(bf16[8,6,128,128]{3,2,1,0:T(8,128)(2,1)} %pack.1), calls=%async_computation.1 | async-start | bytes 3145728 | tf_op jit(solution)/shard_map/all_to_all | solution.py:47
  52.8 4.8 %main.1 = (bf16[128,256]{1,0:T(8,128)(2,1)}, f32[128,256]{1,0:T(8,128)S(1)}, f32[256,128]{1,0:T(8,128)S(1)}) custom-call(bf16[4,4,128,256]{3,2,1,0:T(8,128)(2,1)S(1)} %all-to-all-done.refs_0_.gathered_ref, bf16[256,4096]{1,0:T(8,128)(2,1)} %refs_1_.1, bf16[128,256]{1,0:T(8,128)(2,1)} %refs_2_.1, f32[128,256]{1,0:T(8,128)} %get-tuple-element.25.refs_3_, ...), custom_call_target="tpu_custom_call" | custom-call | flops 276824064 | bytes 4194304 | tf_op jit(solution)/shard_map/main/pallas_call | solution.py:329
  57.6 2.0 %all-gather.1 = f32[512,128]{1,0:T(8,128)S(1)} all-gather(f32[256,128]{1,0:T(8,128)S(1)} %get-tuple-element.34), channel_id=3, replica_groups={{0,16},{32,48},{64,80},{96,112},{128,144},{160,176},{192,208},{224,240}..., dimensions={0}, use_global_device_ids=true | all-gather | bytes 393216 | tf_op jit(solution)/shard_map/all_gather | solution.py:55
  59.7 2.7 %collective-permute-start.2 = (f32[256,128]{1,0:T(8,128)S(1)}, f32[256,128]{1,0:T(8,128)S(1)}, u32[]{:S(2)}, u32[]{:S(2)}) collective-permute-start(f32[256,128]{1,0:T(8,128)S(1)} %reduce_sum.18), channel_id=1, source_target_pairs={{0,32},{16,48},{32,0},{48,16},{64,96},{80,112},{96,64},{112,80},{1... | collective-permute-start | bytes 393224 | tf_op jit(solution)/shard_map/ppermute | solution.py:65
  62.3 2.4 %collective-permute-start.1 = (f32[128,256]{1,0:T(8,128)S(1)}, f32[128,256]{1,0:T(8,128)S(1)}, u32[]{:S(2)}, u32[]{:S(2)}) collective-permute-start(f32[128,256]{1,0:T(8,128)S(1)} %get-tuple-element.28.grad_sum_ref), channel_id=1, source_target_pairs={{16,0},{32,16},{48,32},{64,48},{80,64},{96,80},{112,96},{128,112},... | collective-permute-start | bytes 393224 | tf_op jit(solution)/shard_map/ppermute | solution.py:71
  64.7 1.8 %collective-permute-done.2 = f32[256,128]{1,0:T(8,128)S(1)} collective-permute-done((f32[256,128]{1,0:T(8,128)S(1)}, f32[256,128]{1,0:T(8,128)S(1)}, u32[]{:S(2)}, u32[]{:S(2)}) %collective-permute-start.2) | collective-permute-done | bytes 131104 | tf_op jit(solution)/shard_map/ppermute | solution.py:65
  66.5 3.1 %collective-permute-start.3 = (bf16[256,128]{1,0:T(8,128)(2,1)S(1)}, bf16[256,128]{1,0:T(8,128)(2,1)S(1)}, u32[]{:S(2)}, u32[]{:S(2)}) collective-permute-start(bf16[256,128]{1,0:T(8,128)(2,1)S(1)} %add_convert_fusion), channel_id=1, source_target_pairs={{0,64},{16,80},{32,96},{48,112},{64,0},{80,16},{96,32},{112,48},{1... | collective-permute-start | bytes 196616 | tf_op jit(solution)/shard_map/ppermute | solution.py:65
  69.6 0.0 collective-permute-done.1.incoming_ref
  69.6 2.3 %ahead.1 = (bf16[128,256]{1,0:T(8,128)(2,1)}, bf16[128,256]{1,0:T(8,128)(2,1)}) custom-call(f32[128,256]{1,0:T(8,128)S(1)} %get-tuple-element.28.grad_sum_ref, f32[128,256]{1,0:T(8,128)S(1)} %collective-permute-done.1.incoming_ref, f32[256,128]{1,0:T(8,128)S(1)} %copy-done, f32[1,256]{1,0:T(1,128)S(1)} %bitcast.7, bf16[128,256]{1,0:T(8,128)(2,1)} %key_ref.1, ...), custom_call_target="tpu_custom_call" | custom-call | flops 8388608 | bytes 655360 | tf_op jit(solution)/shard_map/ahead/pallas_call | solution.py:350
  71.9 1.7 %all-to-all-done.1.pieces_ref = bf16[8,6,128,128]{3,2,1,0:T(8,128)(2,1)S(1)} async-done(((bf16[8,6,128,128]{3,2,1,0:T(8,128)(2,1)}), bf16[8,6,128,128]{3,2,1,0:T(8,128)(2,1)S(1)}, u32[]{:S(2)}, u32[]{:S(2)}) %all-to-all-start.1) | async-done | bytes 1572896 | tf_op jit(solution)/shard_map/all_to_all | solution.py:47
  73.5 1.1 %weight.1 = bf16[4,256,128]{2,1,0:T(8,128)(2,1)} custom-call(bf16[8,6,128,128]{3,2,1,0:T(8,128)(2,1)S(1)} %all-to-all-done.1.pieces_ref), custom_call_target="tpu_custom_call" | custom-call | flops 268435456 | bytes 2097152 | tf_op jit(solution)/shard_map/weight/pallas_call | solution.py:366
  74.7 0.0 collective-permute-done.3
  74.7 2.2 %collective-permute-start.4 = (f32[256,128]{1,0:T(8,128)S(1)}, f32[256,128]{1,0:T(8,128)S(1)}, u32[]{:S(2)}, u32[]{:S(2)}) collective-permute-start(f32[256,128]{1,0:T(8,128)S(1)} %convert_add_fusion), channel_id=1, source_target_pairs={{0,128},{16,144},{32,160},{48,176},{64,192},{80,208},{96,224},{112... | collective-permute-start | bytes 393224 | tf_op jit(solution)/shard_map/ppermute | solution.py:65
  76.9 5.0 %all-to-all-start.2 = ((bf16[4,256,128]{2,1,0:T(8,128)(2,1)}), bf16[4,256,128]{2,1,0:T(8,128)(2,1)S(1)}, u32[]{:S(2)}, u32[]{:S(2)}) async-start(bf16[4,256,128]{2,1,0:T(8,128)(2,1)} %weight.1), calls=%async_computation.2 | async-start | bytes 524288 | tf_op jit(solution)/shard_map/all_to_all | solution.py:47
  81.9 0.0 collective-permute-done.4
  81.9 6.4 %all-gather.2 = f32[512,128]{1,0:T(8,128)S(1)} all-gather(f32[256,128]{1,0:T(8,128)S(1)} %add.11), channel_id=4, replica_groups={{0,256},{16,272},{32,288},{48,304},{64,320},{80,336},{96,352},{112,368}..., dimensions={0}, use_global_device_ids=true | all-gather | bytes 393216 | tf_op jit(solution)/shard_map/all_gather | solution.py:55
  88.4 0.7 filter.1
  89.0 0.6 all-to-all-done.2
  89.7 0.7 broadcast_multiply_fusion
  (6 shorter events, 0.1 us)
Async XLA Ops:
  26.1 5.3 %copy-start.2 = (bf16[128,256]{1,0:T(8,128)(2,1)S(1)}, bf16[128,256]{1,0:T(8,128)(2,1)}, u32[]{:S(2)}) copy-start(bf16[128,256]{1,0:T(8,128)(2,1)} %value_ref.1) | copy-start | bytes 196612
  26.1 5.3 %copy-start.3 = (bf16[128,256]{1,0:T(8,128)(2,1)S(1)}, bf16[128,256]{1,0:T(8,128)(2,1)}, u32[]{:S(2)}) copy-start(bf16[128,256]{1,0:T(8,128)(2,1)} %key_ref.1) | copy-start | bytes 196612
  26.1 13.2 %copy-start = (f32[256,128]{1,0:T(8,128)S(1)}, f32[256,128]{1,0:T(8,128)}, u32[]{:S(2)}) copy-start(f32[256,128]{1,0:T(8,128)} %taps_ref.3) | copy-start | bytes 393220
  26.1 13.2 %copy-start.1 = (f32[256]{0:T(256)S(1)}, f32[256]{0:T(256)}, u32[]{:S(2)}) copy-start(f32[256]{0:T(256)} %param.12) | copy-start | bytes 3076
  27.2 15.6 %all-to-all-start = ((bf16[4,4,128,256]{3,2,1,0:T(8,128)(2,1)}), bf16[4,4,128,256]{3,2,1,0:T(8,128)(2,1)S(1)}, u32[]{:S(2)}, u32[]{:S(2)}) async-start(bf16[4,4,128,256]{3,2,1,0:T(8,128)(2,1)} %broadcast_in_dim.2), calls=%async_computation | async-start | bytes 2097152 | tf_op jit(solution)/shard_map/all_to_all | solution.py:47
  31.4 7.9 %collective-permute-start = (f32[128,256]{1,0:T(8,128)S(1)}, f32[128,256]{1,0:T(8,128)S(1)}, u32[]{:S(2)}, u32[]{:S(2)}) collective-permute-start(f32[128,256]{1,0:T(8,128)S(1)} %convert_multiply_fusion.mixed_ref.refs_5_), channel_id=1, source_target_pairs={{0,16},{16,32},{32,48},{48,64},{64,80},{80,96},{96,112},{112,128},... | collective-permute-start | bytes 393224 | tf_op jit(solution)/shard_map/ppermute | solution.py:71
  43.9 29.7 %all-to-all-start.1 = ((bf16[8,6,128,128]{3,2,1,0:T(8,128)(2,1)}), bf16[8,6,128,128]{3,2,1,0:T(8,128)(2,1)S(1)}, u32[]{:S(2)}, u32[]{:S(2)}) async-start(bf16[8,6,128,128]{3,2,1,0:T(8,128)(2,1)} %pack.1), calls=%async_computation.1 | async-start | bytes 3145728 | tf_op jit(solution)/shard_map/all_to_all | solution.py:47
  59.7 6.8 %collective-permute-start.2 = (f32[256,128]{1,0:T(8,128)S(1)}, f32[256,128]{1,0:T(8,128)S(1)}, u32[]{:S(2)}, u32[]{:S(2)}) collective-permute-start(f32[256,128]{1,0:T(8,128)S(1)} %reduce_sum.18), channel_id=1, source_target_pairs={{0,32},{16,48},{32,0},{48,16},{64,96},{80,112},{96,64},{112,80},{1... | collective-permute-start | bytes 393224 | tf_op jit(solution)/shard_map/ppermute | solution.py:65
  62.3 7.3 %collective-permute-start.1 = (f32[128,256]{1,0:T(8,128)S(1)}, f32[128,256]{1,0:T(8,128)S(1)}, u32[]{:S(2)}, u32[]{:S(2)}) collective-permute-start(f32[128,256]{1,0:T(8,128)S(1)} %get-tuple-element.28.grad_sum_ref), channel_id=1, source_target_pairs={{16,0},{32,16},{48,32},{64,48},{80,64},{96,80},{112,96},{128,112},... | collective-permute-start | bytes 393224 | tf_op jit(solution)/shard_map/ppermute | solution.py:71
  66.5 8.2 %collective-permute-start.3 = (bf16[256,128]{1,0:T(8,128)(2,1)S(1)}, bf16[256,128]{1,0:T(8,128)(2,1)S(1)}, u32[]{:S(2)}, u32[]{:S(2)}) collective-permute-start(bf16[256,128]{1,0:T(8,128)(2,1)S(1)} %add_convert_fusion), channel_id=1, source_target_pairs={{0,64},{16,80},{32,96},{48,112},{64,0},{80,16},{96,32},{112,48},{1... | collective-permute-start | bytes 196616 | tf_op jit(solution)/shard_map/ppermute | solution.py:65
  74.7 7.2 %collective-permute-start.4 = (f32[256,128]{1,0:T(8,128)S(1)}, f32[256,128]{1,0:T(8,128)S(1)}, u32[]{:S(2)}, u32[]{:S(2)}) collective-permute-start(f32[256,128]{1,0:T(8,128)S(1)} %convert_add_fusion), channel_id=1, source_target_pairs={{0,128},{16,144},{32,160},{48,176},{64,192},{80,208},{96,224},{112... | collective-permute-start | bytes 393224 | tf_op jit(solution)/shard_map/ppermute | solution.py:65
  76.9 12.7 %all-to-all-start.2 = ((bf16[4,256,128]{2,1,0:T(8,128)(2,1)}), bf16[4,256,128]{2,1,0:T(8,128)(2,1)S(1)}, u32[]{:S(2)}, u32[]{:S(2)}) async-start(bf16[4,256,128]{2,1,0:T(8,128)(2,1)} %weight.1), calls=%async_computation.2 | async-start | bytes 524288 | tf_op jit(solution)/shard_map/all_to_all | solution.py:47

commit v6 on v5

--- a/solution.py
+++ b/solution.py
@@ -110,6 +110,7 @@
     sem,
 ):
     copies = fetch((query_ref,), (query,), sem)
+    stores = []
     rows, width = mixed_ref.shape
     pad[:rows] = prev_ref[...]
     pad[rows:] = mixed_ref[...]
@@ -122,12 +123,13 @@
             starts = [(SUB * q + r, rows - SUB - SUB * q) for q in range(TAPS // SUB)]
             total = total + weighted(shifted, tap_rows, starts, rows)
         summed[:, cols] = total
+        stores += fetch((summed.at[:, cols],), (summed_ref.at[:, cols],), sem, 1 + lane // LANES)
         if lane == 0:
             finish(copies)
         mixers[lane // LANES] = (query[:, cols].astype(F32) * total).T.astype(BF16)
     targets, halves = packed_ref.shape[0], mixers.shape[0]
     places = [packed_ref.at[target, pl.ds(YS, halves)] for target in range(targets)]
-    finish(fetch([summed] + [mixers] * targets, [summed_ref] + places, sem, 1))
+    finish(stores + fetch([mixers] * targets, places, sem, 1 + halves))
 
 
 def pack_kernel(gathered_ref, begun_ref, packed_ref, sem):
@@ -306,7 +308,7 @@
             held_bf16,
             held_f32,
             held_mixers,
-            pltpu.SemaphoreType.DMA((2 + targets,)),
+            pltpu.SemaphoreType.DMA((1 + halves + targets,)),
         ],
         2 * size * TAPS,
         20 * size,
@@ -366,7 +368,7 @@
     partial = call(
         weight_kernel,
         "weight",
-        jax.ShapeDtypeStruct((ZL, width, LANES), BF16),
+        pltpu.VMEM((ZL, width, LANES), BF16),
         [],
         2 * XS * CORES * rows * width * ZL * LANES,
         2 * 1024 * 1024,

time: 90.9 us -> 90.9 us (level)
  no operation moved by 1% of the time
where the time goes in v6:
time: 90.9 us; the launch traced here: 90.3 us
  starting transfers between devices  34.4 us (38%)
  blocking collectives  33.9 us (37%)
  Pallas kernels  12.4 us (14%)
  waiting for transfers between devices  7.02 us (8%)
  local copies, waits for them, and re-layouts  1.1 us (1%)
    all_gather x1, blocking collectives, body(): lax.all_gather(grad_out, 'chan', axis=0, axis_index_groups=ZH_GROUPS)  25.5 us
    all_to_all x3, starting transfers between devices, exchange(): lax.all_to_all(value, axis, 0, 0, tiled=True, axis_index_groups=groups)  18.1 us
    all_gather x2, blocking collectives, collect(): return lax.all_gather(value, 'seq', axis=0, axis_index_groups=groups)  8.41 us
    ppermute x2, starting transfers between devices, passed_along(): return lax.ppermute(value, axis, pairs)  8.29 us
    ppermute x3, starting transfers between devices, swapped(): return lax.ppermute(value, 'seq', pairs)  7.93 us
    pallas_call x1, Pallas kernels, body(): call(lambda *refs: main_kernel(norm_factor, *refs), 'main', (block_bf16,...  4.81 us
    all_to_all x3, waiting for transfers between devices, exchange(): lax.all_to_all(value, axis, 0, 0, tiled=True, axis_index_groups=groups)  3.28 us
    pallas_call x1, Pallas kernels, body(): call(causal_kernel, 'causal', (pltpu.HBM((rows, width), F32), packed_out)...  2.51 us
  transfers between devices with their start and end apart: 8, of which 5 were waited for; matrix products, arithmetic and copies ran while one was open for 0% of the time, Pallas kernels for 13%

profile of v6, /device:TPU:1, one launch (start us, length us, event | category | flops | bytes accessed | tf_op | source)
XLA Modules:
  0.0 90.3 jit_solution(9673803654192448250)
XLA Ops:
  0.6 25.5 %all-gather = bf16[512,256]{1,0:T(8,128)(2,1)S(1)} all-gather(bf16[128,256]{1,0:T(8,128)(2,1)} %param.7), channel_id=2, replica_groups={{0,4,8,12},{1,5,9,13},{2,6,10,14},{3,7,11,15},{16,20,24,28},{17,21,25,2..., dimensions={0}, use_global_device_ids=true | all-gather | bytes 327680 | tf_op jit(solution)/shard_map/all_gather | solution.py:296
  26.1 0.0 copy-start.2
  26.1 0.0 copy-start.3
  26.1 0.0 copy-start
  26.1 0.0 copy-start.1
  26.1 1.1 %broadcast_in_dim.2 = bf16[4,4,128,256]{3,2,1,0:T(8,128)(2,1)} broadcast(bf16[4,128,256]{2,1,0:T(8,128)(2,1)S(1)} %bitcast.8), dimensions={1,2,3} | broadcast | bytes 1310720 | tf_op jit(solution)/shard_map/broadcast_in_dim | solution.py:51
  27.2 4.2 %all-to-all-start = ((bf16[4,4,128,256]{3,2,1,0:T(8,128)(2,1)}), bf16[4,4,128,256]{3,2,1,0:T(8,128)(2,1)S(1)}, u32[]{:S(2)}, u32[]{:S(2)}) async-start(bf16[4,4,128,256]{3,2,1,0:T(8,128)(2,1)} %broadcast_in_dim.2), calls=%async_computation | async-start | bytes 2097152 | tf_op jit(solution)/shard_map/all_to_all | solution.py:47
  31.4 0.0 copy-done.2
  31.4 0.0 copy-done.3
  31.4 5.9 %collective-permute-start = (f32[128,256]{1,0:T(8,128)S(1)}, f32[128,256]{1,0:T(8,128)S(1)}, u32[]{:S(2)}, u32[]{:S(2)}) collective-permute-start(f32[128,256]{1,0:T(8,128)S(1)} %convert_multiply_fusion.mixed_ref.refs_5_), channel_id=1, source_target_pairs={{0,16},{16,32},{32,48},{48,64},{64,80},{80,96},{96,112},{112,128},... | collective-permute-start | bytes 393224 | tf_op jit(solution)/shard_map/ppermute | solution.py:71
  37.4 1.9 %collective-permute-done.prev_ref.refs_4_ = f32[128,256]{1,0:T(8,128)S(1)} collective-permute-done((f32[128,256]{1,0:T(8,128)S(1)}, f32[128,256]{1,0:T(8,128)S(1)}, u32[]{:S(2)}, u32[]{:S(2)}) %collective-permute-start) | collective-permute-done | bytes 131104 | tf_op jit(solution)/shard_map/ppermute | solution.py:71
  39.3 0.0 copy-done
  39.3 0.0 copy-done.1
  39.3 2.5 %causal.1 = (f32[128,256]{1,0:T(8,128)}, bf16[8,6,128,128]{3,2,1,0:T(8,128)(2,1)}) custom-call(f32[128,256]{1,0:T(8,128)S(1)} %collective-permute-done.prev_ref.refs_4_, f32[128,256]{1,0:T(8,128)S(1)} %convert_multiply_fusion.mixed_ref.refs_5_, f32[256,128]{1,0:T(8,128)S(1)} %copy-done, f32[1,256]{1,0:T(1,128)S(1)} %bitcast.6, bf16[128,256]{1,0:T(8,128)(2,1)} %refs_2_.1), custom_call_target="tpu_custom_call" | custom-call | flops 8388608 | bytes 655360 | tf_op jit(solution)/shard_map/causal/pallas_call | solution.py:301
  41.8 1.0 %all-to-all-done.refs_0_.gathered_ref = bf16[4,4,128,256]{3,2,1,0:T(8,128)(2,1)S(1)} async-done(((bf16[4,4,128,256]{3,2,1,0:T(8,128)(2,1)}), bf16[4,4,128,256]{3,2,1,0:T(8,128)(2,1)S(1)}, u32[]{:S(2)}, u32[]{:S(2)}) %all-to-all-start) | async-done | bytes 1048608 | tf_op jit(solution)/shard_map/all_to_all | solution.py:47
  42.8 1.1 %pack.1 = bf16[8,6,128,128]{3,2,1,0:T(8,128)(2,1)} custom-call(bf16[4,4,128,256]{3,2,1,0:T(8,128)(2,1)S(1)} %all-to-all-done.refs_0_.gathered_ref, bf16[8,6,128,128]{3,2,1,0:T(8,128)(2,1)} %get-tuple-element.27.begun_ref), custom_call_target="tpu_custom_call", output_to_operand_aliasing={{}: (1, {})} | custom-call | bytes 2097152 | tf_op jit(solution)/shard_map/pack/pallas_call | solution.py:318
  43.9 8.9 %all-to-all-start.1 = ((bf16[8,6,128,128]{3,2,1,0:T(8,128)(2,1)}), bf16[8,6,128,128]{3,2,1,0:T(8,128)(2,1)S(1)}, u32[]{:S(2)}, u32[]{:S(2)}) async-start(bf16[8,6,128,128]{3,2,1,0:T(8,128)(2,1)} %pack.1), calls=%async_computation.1 | async-start | bytes 3145728 | tf_op jit(solution)/shard_map/all_to_all | solution.py:47
  52.8 4.8 %main.1 = (bf16[128,256]{1,0:T(8,128)(2,1)}, f32[128,256]{1,0:T(8,128)S(1)}, f32[256,128]{1,0:T(8,128)S(1)}) custom-call(bf16[4,4,128,256]{3,2,1,0:T(8,128)(2,1)S(1)} %all-to-all-done.refs_0_.gathered_ref, bf16[256,4096]{1,0:T(8,128)(2,1)} %refs_1_.1, bf16[128,256]{1,0:T(8,128)(2,1)} %refs_2_.1, f32[128,256]{1,0:T(8,128)} %get-tuple-element.25.refs_3_, ...), custom_call_target="tpu_custom_call" | custom-call | flops 276824064 | bytes 4194304 | tf_op jit(solution)/shard_map/main/pallas_call | solution.py:331
  57.6 2.0 %all-gather.1 = f32[512,128]{1,0:T(8,128)S(1)} all-gather(f32[256,128]{1,0:T(8,128)S(1)} %get-tuple-element.34), channel_id=3, replica_groups={{0,16},{32,48},{64,80},{96,112},{128,144},{160,176},{192,208},{224,240}..., dimensions={0}, use_global_device_ids=true | all-gather | bytes 393216 | tf_op jit(solution)/shard_map/all_gather | solution.py:55
  59.7 2.7 %collective-permute-start.2 = (f32[256,128]{1,0:T(8,128)S(1)}, f32[256,128]{1,0:T(8,128)S(1)}, u32[]{:S(2)}, u32[]{:S(2)}) collective-permute-start(f32[256,128]{1,0:T(8,128)S(1)} %reduce_sum.18), channel_id=1, source_target_pairs={{0,32},{16,48},{32,0},{48,16},{64,96},{80,112},{96,64},{112,80},{1... | collective-permute-start | bytes 393224 | tf_op jit(solution)/shard_map/ppermute | solution.py:65
  62.3 2.4 %collective-permute-start.1 = (f32[128,256]{1,0:T(8,128)S(1)}, f32[128,256]{1,0:T(8,128)S(1)}, u32[]{:S(2)}, u32[]{:S(2)}) collective-permute-start(f32[128,256]{1,0:T(8,128)S(1)} %get-tuple-element.28.grad_sum_ref), channel_id=1, source_target_pairs={{16,0},{32,16},{48,32},{64,48},{80,64},{96,80},{112,96},{128,112},... | collective-permute-start | bytes 393224 | tf_op jit(solution)/shard_map/ppermute | solution.py:71
  64.7 1.8 %collective-permute-done.2 = f32[256,128]{1,0:T(8,128)S(1)} collective-permute-done((f32[256,128]{1,0:T(8,128)S(1)}, f32[256,128]{1,0:T(8,128)S(1)}, u32[]{:S(2)}, u32[]{:S(2)}) %collective-permute-start.2) | collective-permute-done | bytes 131104 | tf_op jit(solution)/shard_map/ppermute | solution.py:65
  66.5 3.1 %collective-permute-start.3 = (bf16[256,128]{1,0:T(8,128)(2,1)S(1)}, bf16[256,128]{1,0:T(8,128)(2,1)S(1)}, u32[]{:S(2)}, u32[]{:S(2)}) collective-permute-start(bf16[256,128]{1,0:T(8,128)(2,1)S(1)} %add_convert_fusion), channel_id=1, source_target_pairs={{0,64},{16,80},{32,96},{48,112},{64,0},{80,16},{96,32},{112,48},{1... | collective-permute-start | bytes 196616 | tf_op jit(solution)/shard_map/ppermute | solution.py:65
  69.6 0.0 collective-permute-done.1.incoming_ref
  69.6 2.3 %ahead.1 = (bf16[128,256]{1,0:T(8,128)(2,1)}, bf16[128,256]{1,0:T(8,128)(2,1)}) custom-call(f32[128,256]{1,0:T(8,128)S(1)} %get-tuple-element.28.grad_sum_ref, f32[128,256]{1,0:T(8,128)S(1)} %collective-permute-done.1.incoming_ref, f32[256,128]{1,0:T(8,128)S(1)} %copy-done, f32[1,256]{1,0:T(1,128)S(1)} %bitcast.7, bf16[128,256]{1,0:T(8,128)(2,1)} %key_ref.1, ...), custom_call_target="tpu_custom_call" | custom-call | flops 8388608 | bytes 655360 | tf_op jit(solution)/shard_map/ahead/pallas_call | solution.py:352
  71.9 1.7 %all-to-all-done.1.pieces_ref = bf16[8,6,128,128]{3,2,1,0:T(8,128)(2,1)S(1)} async-done(((bf16[8,6,128,128]{3,2,1,0:T(8,128)(2,1)}), bf16[8,6,128,128]{3,2,1,0:T(8,128)(2,1)S(1)}, u32[]{:S(2)}, u32[]{:S(2)}) %all-to-all-start.1) | async-done | bytes 1572896 | tf_op jit(solution)/shard_map/all_to_all | solution.py:47
  73.5 1.1 %weight.1 = bf16[4,256,128]{2,1,0:T(8,128)(2,1)} custom-call(bf16[8,6,128,128]{3,2,1,0:T(8,128)(2,1)S(1)} %all-to-all-done.1.pieces_ref), custom_call_target="tpu_custom_call" | custom-call | flops 268435456 | bytes 2097152 | tf_op jit(solution)/shard_map/weight/pallas_call | solution.py:368
  74.7 0.0 collective-permute-done.3
  74.7 2.2 %collective-permute-start.4 = (f32[256,128]{1,0:T(8,128)S(1)}, f32[256,128]{1,0:T(8,128)S(1)}, u32[]{:S(2)}, u32[]{:S(2)}) collective-permute-start(f32[256,128]{1,0:T(8,128)S(1)} %convert_add_fusion), channel_id=1, source_target_pairs={{0,128},{16,144},{32,160},{48,176},{64,192},{80,208},{96,224},{112... | collective-permute-start | bytes 393224 | tf_op jit(solution)/shard_map/ppermute | solution.py:65
  76.9 5.0 %all-to-all-start.2 = ((bf16[4,256,128]{2,1,0:T(8,128)(2,1)}), bf16[4,256,128]{2,1,0:T(8,128)(2,1)S(1)}, u32[]{:S(2)}, u32[]{:S(2)}) async-start(bf16[4,256,128]{2,1,0:T(8,128)(2,1)} %weight.1), calls=%async_computation.2 | async-start | bytes 524288 | tf_op jit(solution)/shard_map/all_to_all | solution.py:47
  81.9 0.0 collective-permute-done.4
  81.9 6.4 %all-gather.2 = f32[512,128]{1,0:T(8,128)S(1)} all-gather(f32[256,128]{1,0:T(8,128)S(1)} %add.11), channel_id=4, replica_groups={{0,256},{16,272},{32,288},{48,304},{64,320},{80,336},{96,352},{112,368}..., dimensions={0}, use_global_device_ids=true | all-gather | bytes 393216 | tf_op jit(solution)/shard_map/all_gather | solution.py:55
  88.4 0.7 filter.1
  89.0 0.6 all-to-all-done.2
  89.7 0.7 broadcast_multiply_fusion
  (6 shorter events, 0.1 us)
Async XLA Ops:
  26.1 5.3 %copy-start.2 = (bf16[128,256]{1,0:T(8,128)(2,1)S(1)}, bf16[128,256]{1,0:T(8,128)(2,1)}, u32[]{:S(2)}) copy-start(bf16[128,256]{1,0:T(8,128)(2,1)} %value_ref.1) | copy-start | bytes 196612
  26.1 5.3 %copy-start.3 = (bf16[128,256]{1,0:T(8,128)(2,1)S(1)}, bf16[128,256]{1,0:T(8,128)(2,1)}, u32[]{:S(2)}) copy-start(bf16[128,256]{1,0:T(8,128)(2,1)} %key_ref.1) | copy-start | bytes 196612
  26.1 13.2 %copy-start = (f32[256,128]{1,0:T(8,128)S(1)}, f32[256,128]{1,0:T(8,128)}, u32[]{:S(2)}) copy-start(f32[256,128]{1,0:T(8,128)} %taps_ref.3) | copy-start | bytes 393220
  26.1 13.2 %copy-start.1 = (f32[256]{0:T(256)S(1)}, f32[256]{0:T(256)}, u32[]{:S(2)}) copy-start(f32[256]{0:T(256)} %param.12) | copy-start | bytes 3076
  27.2 15.6 %all-to-all-start = ((bf16[4,4,128,256]{3,2,1,0:T(8,128)(2,1)}), bf16[4,4,128,256]{3,2,1,0:T(8,128)(2,1)S(1)}, u32[]{:S(2)}, u32[]{:S(2)}) async-start(bf16[4,4,128,256]{3,2,1,0:T(8,128)(2,1)} %broadcast_in_dim.2), calls=%async_computation | async-start | bytes 2097152 | tf_op jit(solution)/shard_map/all_to_all | solution.py:47
  31.4 7.9 %collective-permute-start = (f32[128,256]{1,0:T(8,128)S(1)}, f32[128,256]{1,0:T(8,128)S(1)}, u32[]{:S(2)}, u32[]{:S(2)}) collective-permute-start(f32[128,256]{1,0:T(8,128)S(1)} %convert_multiply_fusion.mixed_ref.refs_5_), channel_id=1, source_target_pairs={{0,16},{16,32},{32,48},{48,64},{64,80},{80,96},{96,112},{112,128},... | collective-permute-start | bytes 393224 | tf_op jit(solution)/shard_map/ppermute | solution.py:71
  43.9 29.7 %all-to-all-start.1 = ((bf16[8,6,128,128]{3,2,1,0:T(8,128)(2,1)}), bf16[8,6,128,128]{3,2,1,0:T(8,128)(2,1)S(1)}, u32[]{:S(2)}, u32[]{:S(2)}) async-start(bf16[8,6,128,128]{3,2,1,0:T(8,128)(2,1)} %pack.1), calls=%async_computation.1 | async-start | bytes 3145728 | tf_op jit(solution)/shard_map/all_to_all | solution.py:47
  59.7 6.8 %collective-permute-start.2 = (f32[256,128]{1,0:T(8,128)S(1)}, f32[256,128]{1,0:T(8,128)S(1)}, u32[]{:S(2)}, u32[]{:S(2)}) collective-permute-start(f32[256,128]{1,0:T(8,128)S(1)} %reduce_sum.18), channel_id=1, source_target_pairs={{0,32},{16,48},{32,0},{48,16},{64,96},{80,112},{96,64},{112,80},{1... | collective-permute-start | bytes 393224 | tf_op jit(solution)/shard_map/ppermute | solution.py:65
  62.3 7.3 %collective-permute-start.1 = (f32[128,256]{1,0:T(8,128)S(1)}, f32[128,256]{1,0:T(8,128)S(1)}, u32[]{:S(2)}, u32[]{:S(2)}) collective-permute-start(f32[128,256]{1,0:T(8,128)S(1)} %get-tuple-element.28.grad_sum_ref), channel_id=1, source_target_pairs={{16,0},{32,16},{48,32},{64,48},{80,64},{96,80},{112,96},{128,112},... | collective-permute-start | bytes 393224 | tf_op jit(solution)/shard_map/ppermute | solution.py:71
  66.5 8.2 %collective-permute-start.3 = (bf16[256,128]{1,0:T(8,128)(2,1)S(1)}, bf16[256,128]{1,0:T(8,128)(2,1)S(1)}, u32[]{:S(2)}, u32[]{:S(2)}) collective-permute-start(bf16[256,128]{1,0:T(8,128)(2,1)S(1)} %add_convert_fusion), channel_id=1, source_target_pairs={{0,64},{16,80},{32,96},{48,112},{64,0},{80,16},{96,32},{112,48},{1... | collective-permute-start | bytes 196616 | tf_op jit(solution)/shard_map/ppermute | solution.py:65
  74.7 7.2 %collective-permute-start.4 = (f32[256,128]{1,0:T(8,128)S(1)}, f32[256,128]{1,0:T(8,128)S(1)}, u32[]{:S(2)}, u32[]{:S(2)}) collective-permute-start(f32[256,128]{1,0:T(8,128)S(1)} %convert_add_fusion), channel_id=1, source_target_pairs={{0,128},{16,144},{32,160},{48,176},{64,192},{80,208},{96,224},{112... | collective-permute-start | bytes 393224 | tf_op jit(solution)/shard_map/ppermute | solution.py:65
  76.9 12.7 %all-to-all-start.2 = ((bf16[4,256,128]{2,1,0:T(8,128)(2,1)}), bf16[4,256,128]{2,1,0:T(8,128)(2,1)S(1)}, u32[]{:S(2)}, u32[]{:S(2)}) async-start(bf16[4,256,128]{2,1,0:T(8,128)(2,1)} %weight.1), calls=%async_computation.2 | async-start | bytes 524288 | tf_op jit(solution)/shard_map/all_to_all | solution.py:47

commit v7 on v6

--- a/solution.py
+++ b/solution.py
@@ -170,8 +170,8 @@
     pad[rows:] = mixed_ref[...]
 
     total = None
+    finish(loads)
     for zh in range(ZH):
-        loads[zh].wait()
         for y in range(YS):
             term = lax.dot_general(
                 gathered_ref[y, zh],

time: 90.9 us -> 90.8 us (level)
  transfers between devices with their start and end apart: 8 -> 8, of which waited for: 5 -> 5; matrix products, arithmetic and copies ran while one was open for 0% -> 0% of each run, Pallas kernels for 13% -> 12%
where the time goes in v7:
time: 90.8 us; the launch traced here: 90.2 us
  starting transfers between devices  34.3 us (38%)
  blocking collectives  33.6 us (37%)
  Pallas kernels  12.3 us (14%)
  waiting for transfers between devices  7.41 us (8%)
  local copies, waits for them, and re-layouts  1.1 us (1%)
    all_gather x1, blocking collectives, body(): lax.all_gather(grad_out, 'chan', axis=0, axis_index_groups=ZH_GROUPS)  25.5 us
    all_to_all x3, starting transfers between devices, exchange(): lax.all_to_all(value, axis, 0, 0, tiled=True, axis_index_groups=groups)  18 us
    ppermute x2, starting transfers between devices, passed_along(): return lax.ppermute(value, axis, pairs)  8.29 us
    all_gather x2, blocking collectives, collect(): return lax.all_gather(value, 'seq', axis=0, axis_index_groups=groups)  8.13 us
    ppermute x3, starting transfers between devices, swapped(): return lax.ppermute(value, 'seq', pairs)  7.94 us
    pallas_call x1, Pallas kernels, body(): call(lambda *refs: main_kernel(norm_factor, *refs), 'main', (block_bf16,...  4.69 us
    all_to_all x3, waiting for transfers between devices, exchange(): lax.all_to_all(value, axis, 0, 0, tiled=True, axis_index_groups=groups)  3.67 us
    pallas_call x1, Pallas kernels, body(): call(causal_kernel, 'causal', (pltpu.HBM((rows, width), F32), packed_out)...  2.51 us
  transfers between devices with their start and end apart: 8, of which 5 were waited for; matrix products, arithmetic and copies ran while one was open for 0% of the time, Pallas kernels for 12%

profile of v7, /device:TPU:1, one launch (start us, length us, event | category | flops | bytes accessed | tf_op | source)
XLA Modules:
  0.0 90.2 jit_solution(8174335877279435347)
XLA Ops:
  0.6 25.5 %all-gather = bf16[512,256]{1,0:T(8,128)(2,1)S(1)} all-gather(bf16[128,256]{1,0:T(8,128)(2,1)} %param.7), channel_id=2, replica_groups={{0,4,8,12},{1,5,9,13},{2,6,10,14},{3,7,11,15},{16,20,24,28},{17,21,25,2..., dimensions={0}, use_global_device_ids=true | all-gather | bytes 327680 | tf_op jit(solution)/shard_map/all_gather | solution.py:296
  26.1 0.0 copy-start.2
  26.1 0.0 copy-start.3
  26.1 0.0 copy-start
  26.1 0.0 copy-start.1
  26.1 1.1 %broadcast_in_dim.2 = bf16[4,4,128,256]{3,2,1,0:T(8,128)(2,1)} broadcast(bf16[4,128,256]{2,1,0:T(8,128)(2,1)S(1)} %bitcast.8), dimensions={1,2,3} | broadcast | bytes 1310720 | tf_op jit(solution)/shard_map/broadcast_in_dim | solution.py:51
  27.2 4.2 %all-to-all-start = ((bf16[4,4,128,256]{3,2,1,0:T(8,128)(2,1)}), bf16[4,4,128,256]{3,2,1,0:T(8,128)(2,1)S(1)}, u32[]{:S(2)}, u32[]{:S(2)}) async-start(bf16[4,4,128,256]{3,2,1,0:T(8,128)(2,1)} %broadcast_in_dim.2), calls=%async_computation | async-start | bytes 2097152 | tf_op jit(solution)/shard_map/all_to_all | solution.py:47
  31.4 0.0 copy-done.2
  31.4 0.0 copy-done.3
  31.4 5.9 %collective-permute-start = (f32[128,256]{1,0:T(8,128)S(1)}, f32[128,256]{1,0:T(8,128)S(1)}, u32[]{:S(2)}, u32[]{:S(2)}) collective-permute-start(f32[128,256]{1,0:T(8,128)S(1)} %convert_multiply_fusion.mixed_ref.refs_5_), channel_id=1, source_target_pairs={{0,16},{16,32},{32,48},{48,64},{64,80},{80,96},{96,112},{112,128},... | collective-permute-start | bytes 393224 | tf_op jit(solution)/shard_map/ppermute | solution.py:71
  37.4 1.9 %collective-permute-done.prev_ref.refs_4_ = f32[128,256]{1,0:T(8,128)S(1)} collective-permute-done((f32[128,256]{1,0:T(8,128)S(1)}, f32[128,256]{1,0:T(8,128)S(1)}, u32[]{:S(2)}, u32[]{:S(2)}) %collective-permute-start) | collective-permute-done | bytes 131104 | tf_op jit(solution)/shard_map/ppermute | solution.py:71
  39.3 0.0 copy-done
  39.3 0.0 copy-done.1
  39.3 2.5 %causal.1 = (f32[128,256]{1,0:T(8,128)}, bf16[8,6,128,128]{3,2,1,0:T(8,128)(2,1)}) custom-call(f32[128,256]{1,0:T(8,128)S(1)} %collective-permute-done.prev_ref.refs_4_, f32[128,256]{1,0:T(8,128)S(1)} %convert_multiply_fusion.mixed_ref.refs_5_, f32[256,128]{1,0:T(8,128)S(1)} %copy-done, f32[1,256]{1,0:T(1,128)S(1)} %bitcast.6, bf16[128,256]{1,0:T(8,128)(2,1)} %refs_2_.1), custom_call_target="tpu_custom_call" | custom-call | flops 8388608 | bytes 655360 | tf_op jit(solution)/shard_map/causal/pallas_call | solution.py:301
  41.8 1.0 %all-to-all-done.refs_0_.gathered_ref = bf16[4,4,128,256]{3,2,1,0:T(8,128)(2,1)S(1)} async-done(((bf16[4,4,128,256]{3,2,1,0:T(8,128)(2,1)}), bf16[4,4,128,256]{3,2,1,0:T(8,128)(2,1)S(1)}, u32[]{:S(2)}, u32[]{:S(2)}) %all-to-all-start) | async-done | bytes 1048608 | tf_op jit(solution)/shard_map/all_to_all | solution.py:47
  42.8 1.1 %pack.1 = bf16[8,6,128,128]{3,2,1,0:T(8,128)(2,1)} custom-call(bf16[4,4,128,256]{3,2,1,0:T(8,128)(2,1)S(1)} %all-to-all-done.refs_0_.gathered_ref, bf16[8,6,128,128]{3,2,1,0:T(8,128)(2,1)} %get-tuple-element.27.begun_ref), custom_call_target="tpu_custom_call", output_to_operand_aliasing={{}: (1, {})} | custom-call | bytes 2097152 | tf_op jit(solution)/shard_map/pack/pallas_call | solution.py:318
  43.9 8.9 %all-to-all-start.1 = ((bf16[8,6,128,128]{3,2,1,0:T(8,128)(2,1)}), bf16[8,6,128,128]{3,2,1,0:T(8,128)(2,1)S(1)}, u32[]{:S(2)}, u32[]{:S(2)}) async-start(bf16[8,6,128,128]{3,2,1,0:T(8,128)(2,1)} %pack.1), calls=%async_computation.1 | async-start | bytes 3145728 | tf_op jit(solution)/shard_map/all_to_all | solution.py:47
  52.8 4.7 %main.1 = (bf16[128,256]{1,0:T(8,128)(2,1)}, f32[128,256]{1,0:T(8,128)S(1)}, f32[256,128]{1,0:T(8,128)S(1)}) custom-call(bf16[4,4,128,256]{3,2,1,0:T(8,128)(2,1)S(1)} %all-to-all-done.refs_0_.gathered_ref, bf16[256,4096]{1,0:T(8,128)(2,1)} %refs_1_.1, bf16[128,256]{1,0:T(8,128)(2,1)} %refs_2_.1, f32[128,256]{1,0:T(8,128)} %get-tuple-element.25.refs_3_, ...), custom_call_target="tpu_custom_call" | custom-call | flops 276824064 | bytes 4194304 | tf_op jit(solution)/shard_map/main/pallas_call | solution.py:331
  57.5 2.0 %all-gather.1 = f32[512,128]{1,0:T(8,128)S(1)} all-gather(f32[256,128]{1,0:T(8,128)S(1)} %get-tuple-element.34), channel_id=3, replica_groups={{0,16},{32,48},{64,80},{96,112},{128,144},{160,176},{192,208},{224,240}..., dimensions={0}, use_global_device_ids=true | all-gather | bytes 393216 | tf_op jit(solution)/shard_map/all_gather | solution.py:55
  59.5 2.7 %collective-permute-start.2 = (f32[256,128]{1,0:T(8,128)S(1)}, f32[256,128]{1,0:T(8,128)S(1)}, u32[]{:S(2)}, u32[]{:S(2)}) collective-permute-start(f32[256,128]{1,0:T(8,128)S(1)} %reduce_sum.18), channel_id=1, source_target_pairs={{0,32},{16,48},{32,0},{48,16},{64,96},{80,112},{96,64},{112,80},{1... | collective-permute-start | bytes 393224 | tf_op jit(solution)/shard_map/ppermute | solution.py:65
  62.2 2.4 %collective-permute-start.1 = (f32[128,256]{1,0:T(8,128)S(1)}, f32[128,256]{1,0:T(8,128)S(1)}, u32[]{:S(2)}, u32[]{:S(2)}) collective-permute-start(f32[128,256]{1,0:T(8,128)S(1)} %get-tuple-element.28.grad_sum_ref), channel_id=1, source_target_pairs={{16,0},{32,16},{48,32},{64,48},{80,64},{96,80},{112,96},{128,112},... | collective-permute-start | bytes 393224 | tf_op jit(solution)/shard_map/ppermute | solution.py:71
  64.6 1.8 %collective-permute-done.2 = f32[256,128]{1,0:T(8,128)S(1)} collective-permute-done((f32[256,128]{1,0:T(8,128)S(1)}, f32[256,128]{1,0:T(8,128)S(1)}, u32[]{:S(2)}, u32[]{:S(2)}) %collective-permute-start.2) | collective-permute-done | bytes 131104 | tf_op jit(solution)/shard_map/ppermute | solution.py:65
  66.4 3.1 %collective-permute-start.3 = (bf16[256,128]{1,0:T(8,128)(2,1)S(1)}, bf16[256,128]{1,0:T(8,128)(2,1)S(1)}, u32[]{:S(2)}, u32[]{:S(2)}) collective-permute-start(bf16[256,128]{1,0:T(8,128)(2,1)S(1)} %add_convert_fusion), channel_id=1, source_target_pairs={{0,64},{16,80},{32,96},{48,112},{64,0},{80,16},{96,32},{112,48},{1... | collective-permute-start | bytes 196616 | tf_op jit(solution)/shard_map/ppermute | solution.py:65
  69.5 0.0 collective-permute-done.1.incoming_ref
  69.5 2.3 %ahead.1 = (bf16[128,256]{1,0:T(8,128)(2,1)}, bf16[128,256]{1,0:T(8,128)(2,1)}) custom-call(f32[128,256]{1,0:T(8,128)S(1)} %get-tuple-element.28.grad_sum_ref, f32[128,256]{1,0:T(8,128)S(1)} %collective-permute-done.1.incoming_ref, f32[256,128]{1,0:T(8,128)S(1)} %copy-done, f32[1,256]{1,0:T(1,128)S(1)} %bitcast.7, bf16[128,256]{1,0:T(8,128)(2,1)} %key_ref.1, ...), custom_call_target="tpu_custom_call" | custom-call | flops 8388608 | bytes 655360 | tf_op jit(solution)/shard_map/ahead/pallas_call | solution.py:352
  71.8 1.8 %all-to-all-done.1.pieces_ref = bf16[8,6,128,128]{3,2,1,0:T(8,128)(2,1)S(1)} async-done(((bf16[8,6,128,128]{3,2,1,0:T(8,128)(2,1)}), bf16[8,6,128,128]{3,2,1,0:T(8,128)(2,1)S(1)}, u32[]{:S(2)}, u32[]{:S(2)}) %all-to-all-start.1) | async-done | bytes 1572896 | tf_op jit(solution)/shard_map/all_to_all | solution.py:47
  73.5 1.1 %weight.1 = bf16[4,256,128]{2,1,0:T(8,128)(2,1)} custom-call(bf16[8,6,128,128]{3,2,1,0:T(8,128)(2,1)S(1)} %all-to-all-done.1.pieces_ref), custom_call_target="tpu_custom_call" | custom-call | flops 268435456 | bytes 2097152 | tf_op jit(solution)/shard_map/weight/pallas_call | solution.py:368
  74.7 0.0 collective-permute-done.3
  74.7 2.2 %collective-permute-start.4 = (f32[256,128]{1,0:T(8,128)S(1)}, f32[256,128]{1,0:T(8,128)S(1)}, u32[]{:S(2)}, u32[]{:S(2)}) collective-permute-start(f32[256,128]{1,0:T(8,128)S(1)} %convert_add_fusion), channel_id=1, source_target_pairs={{0,128},{16,144},{32,160},{48,176},{64,192},{80,208},{96,224},{112... | collective-permute-start | bytes 393224 | tf_op jit(solution)/shard_map/ppermute | solution.py:65
  76.9 4.9 %all-to-all-start.2 = ((bf16[4,256,128]{2,1,0:T(8,128)(2,1)}), bf16[4,256,128]{2,1,0:T(8,128)(2,1)S(1)}, u32[]{:S(2)}, u32[]{:S(2)}) async-start(bf16[4,256,128]{2,1,0:T(8,128)(2,1)} %weight.1), calls=%async_computation.2 | async-start | bytes 524288 | tf_op jit(solution)/shard_map/all_to_all | solution.py:47
  81.8 0.0 collective-permute-done.4
  81.8 6.1 %all-gather.2 = f32[512,128]{1,0:T(8,128)S(1)} all-gather(f32[256,128]{1,0:T(8,128)S(1)} %add.11), channel_id=4, replica_groups={{0,256},{16,272},{32,288},{48,304},{64,320},{80,336},{96,352},{112,368}..., dimensions={0}, use_global_device_ids=true | all-gather | bytes 393216 | tf_op jit(solution)/shard_map/all_gather | solution.py:55
  88.0 0.7 filter.1
  88.6 0.9 all-to-all-done.2
  89.6 0.7 broadcast_multiply_fusion
  (6 shorter events, 0.1 us)
Async XLA Ops:
  26.1 5.3 %copy-start.2 = (bf16[128,256]{1,0:T(8,128)(2,1)S(1)}, bf16[128,256]{1,0:T(8,128)(2,1)}, u32[]{:S(2)}) copy-start(bf16[128,256]{1,0:T(8,128)(2,1)} %value_ref.1) | copy-start | bytes 196612
  26.1 5.3 %copy-start.3 = (bf16[128,256]{1,0:T(8,128)(2,1)S(1)}, bf16[128,256]{1,0:T(8,128)(2,1)}, u32[]{:S(2)}) copy-start(bf16[128,256]{1,0:T(8,128)(2,1)} %key_ref.1) | copy-start | bytes 196612
  26.1 13.2 %copy-start = (f32[256,128]{1,0:T(8,128)S(1)}, f32[256,128]{1,0:T(8,128)}, u32[]{:S(2)}) copy-start(f32[256,128]{1,0:T(8,128)} %taps_ref.3) | copy-start | bytes 393220
  26.1 13.2 %copy-start.1 = (f32[256]{0:T(256)S(1)}, f32[256]{0:T(256)}, u32[]{:S(2)}) copy-start(f32[256]{0:T(256)} %param.12) | copy-start | bytes 3076
  27.2 15.6 %all-to-all-start = ((bf16[4,4,128,256]{3,2,1,0:T(8,128)(2,1)}), bf16[4,4,128,256]{3,2,1,0:T(8,128)(2,1)S(1)}, u32[]{:S(2)}, u32[]{:S(2)}) async-start(bf16[4,4,128,256]{3,2,1,0:T(8,128)(2,1)} %broadcast_in_dim.2), calls=%async_computation | async-start | bytes 2097152 | tf_op jit(solution)/shard_map/all_to_all | solution.py:47
  31.4 7.9 %collective-permute-start = (f32[128,256]{1,0:T(8,128)S(1)}, f32[128,256]{1,0:T(8,128)S(1)}, u32[]{:S(2)}, u32[]{:S(2)}) collective-permute-start(f32[128,256]{1,0:T(8,128)S(1)} %convert_multiply_fusion.mixed_ref.refs_5_), channel_id=1, source_target_pairs={{0,16},{16,32},{32,48},{48,64},{64,80},{80,96},{96,112},{112,128},... | collective-permute-start | bytes 393224 | tf_op jit(solution)/shard_map/ppermute | solution.py:71
  43.9 29.7 %all-to-all-start.1 = ((bf16[8,6,128,128]{3,2,1,0:T(8,128)(2,1)}), bf16[8,6,128,128]{3,2,1,0:T(8,128)(2,1)S(1)}, u32[]{:S(2)}, u32[]{:S(2)}) async-start(bf16[8,6,128,128]{3,2,1,0:T(8,128)(2,1)} %pack.1), calls=%async_computation.1 | async-start | bytes 3145728 | tf_op jit(solution)/shard_map/all_to_all | solution.py:47
  59.5 6.8 %collective-permute-start.2 = (f32[256,128]{1,0:T(8,128)S(1)}, f32[256,128]{1,0:T(8,128)S(1)}, u32[]{:S(2)}, u32[]{:S(2)}) collective-permute-start(f32[256,128]{1,0:T(8,128)S(1)} %reduce_sum.18), channel_id=1, source_target_pairs={{0,32},{16,48},{32,0},{48,16},{64,96},{80,112},{96,64},{112,80},{1... | collective-permute-start | bytes 393224 | tf_op jit(solution)/shard_map/ppermute | solution.py:65
  62.2 7.3 %collective-permute-start.1 = (f32[128,256]{1,0:T(8,128)S(1)}, f32[128,256]{1,0:T(8,128)S(1)}, u32[]{:S(2)}, u32[]{:S(2)}) collective-permute-start(f32[128,256]{1,0:T(8,128)S(1)} %get-tuple-element.28.grad_sum_ref), channel_id=1, source_target_pairs={{16,0},{32,16},{48,32},{64,48},{80,64},{96,80},{112,96},{128,112},... | collective-permute-start | bytes 393224 | tf_op jit(solution)/shard_map/ppermute | solution.py:71
  66.4 8.3 %collective-permute-start.3 = (bf16[256,128]{1,0:T(8,128)(2,1)S(1)}, bf16[256,128]{1,0:T(8,128)(2,1)S(1)}, u32[]{:S(2)}, u32[]{:S(2)}) collective-permute-start(bf16[256,128]{1,0:T(8,128)(2,1)S(1)} %add_convert_fusion), channel_id=1, source_target_pairs={{0,64},{16,80},{32,96},{48,112},{64,0},{80,16},{96,32},{112,48},{1... | collective-permute-start | bytes 196616 | tf_op jit(solution)/shard_map/ppermute | solution.py:65
  74.7 7.1 %collective-permute-start.4 = (f32[256,128]{1,0:T(8,128)S(1)}, f32[256,128]{1,0:T(8,128)S(1)}, u32[]{:S(2)}, u32[]{:S(2)}) collective-permute-start(f32[256,128]{1,0:T(8,128)S(1)} %convert_add_fusion), channel_id=1, source_target_pairs={{0,128},{16,144},{32,160},{48,176},{64,192},{80,208},{96,224},{112... | collective-permute-start | bytes 393224 | tf_op jit(solution)/shard_map/ppermute | solution.py:65
  76.9 12.6 %all-to-all-start.2 = ((bf16[4,256,128]{2,1,0:T(8,128)(2,1)}), bf16[4,256,128]{2,1,0:T(8,128)(2,1)S(1)}, u32[]{:S(2)}, u32[]{:S(2)}) async-start(bf16[4,256,128]{2,1,0:T(8,128)(2,1)} %weight.1), calls=%async_computation.2 | async-start | bytes 524288 | tf_op jit(solution)/shard_map/all_to_all | solution.py:47
